TPU v7x, 512 devices: a whole 4x8x8 slice. The times are simulated.
512 devices in a mesh: dp: 16 (over z, x_hi), tensor: 32 (over x_lo, y, core).
Axes of the slice: x: 4 (x_hi: 2, x_lo: 2; x = x_hi * 2 + x_lo), y: 8, z: 8, core: 2. Of those that a mesh axis runs over, the one named last changes fastest.
Arguments:
- inputs: bfloat16 [4096, 2304], P(('dp', 'tensor')), may hold values from -6 to 6
- hidden_grad: bfloat16 [4096, 18432], P('dp', 'tensor'), may hold values from -6 to 6
- token_key: int32 [4096], P('dp'), may hold values from 0 to 16777215
- feature_key: int32 [18432], P('tensor'), may hold values from 0 to 16777215
- drop_seed: int32 [1], replicated, may hold values from 0 to 16777215
- gate_weight: bfloat16 [2304, 18432], P('dp', 'tensor'), may hold values from -0.125 to 0.125
- up_weight: bfloat16 [2304, 18432], P('dp', 'tensor'), may hold values from -0.125 to 0.125
- gate_first: float32 [2304, 18432], P('dp', 'tensor'), may hold values from -6 to 6
- gate_second: float32 [2304, 18432], P('dp', 'tensor'), may hold values from 1 to 100
- up_first: float32 [2304, 18432], P('dp', 'tensor'), may hold values from -6 to 6
- up_second: float32 [2304, 18432], P('dp', 'tensor'), may hold values from 1 to 100
Outputs:
- input_grad: bfloat16 [4096, 2304], P(('dp', 'tensor'))
- gate_updated: bfloat16 [2304, 18432], P('dp', 'tensor')
- up_updated: bfloat16 [2304, 18432], P('dp', 'tensor')
- gate_first_new: float32 [2304, 18432], P('dp', 'tensor')
- gate_second_new: float32 [2304, 18432], P('dp', 'tensor')
- up_first_new: float32 [2304, 18432], P('dp', 'tensor')
- up_second_new: float32 [2304, 18432], P('dp', 'tensor')
All inputs are finite; a program needn't handle non-finite values.
Results may differ from a plain program's by a relative error of at most 0.0049.
Values may be sent and summed in bfloat16 or wider, within the bound.
No kernel may reach another device: no remote copies, remote signals or barrier semaphores. Data moves between devices by JAX's collectives and lax.ppermute only.
A program may use at most 128 MiB of HBM per device.

v0:
```python
import math

import jax
import jax.numpy as jnp
from jax import lax
from jax.sharding import PartitionSpec as P

drop_level = 6554
keep_scale = 65536.0 / (65536.0 - 6554.0)
gelu_coeff = math.sqrt(2.0 / math.pi)
first_fix = 1.0 - 0.9**10
second_fix = 1.0 - 0.95**10


def keep_factor(token_key, feature_key, drop_seed):
    mixed = (
        token_key[:, None] * -1640531535
        + feature_key[None, :] * -1028477379
        + drop_seed[0] * 668265263
    )
    mixed = mixed ^ mixed >> 15 & 131071
    mixed = mixed * -2048144789
    mixed = mixed ^ mixed >> 13 & 524287
    mixed = mixed * -1028477387
    mixed = mixed ^ mixed >> 16 & 65535
    level = mixed & 65535
    return jnp.where(level >= drop_level, jnp.float32(keep_scale), jnp.float32(0.0))


def adamw(weight, first, second, grad):
    first_new = 0.9 * first + 0.1 * grad
    second_new = 0.95 * second + 0.05 * grad * grad
    wide = weight.astype(jnp.float32)
    step = first_new / first_fix / (jnp.sqrt(second_new / second_fix) + 1e-08) + 0.1 * wide
    return ((wide - 0.01 * step).astype(jnp.bfloat16), first_new, second_new)


def contract_rows(left, right):
    return lax.dot_general(
        left, right, (((0,), (0,)), ((), ())), preferred_element_type=jnp.float32
    )


def contract_cols(left, right):
    return lax.dot_general(
        left, right, (((1,), (1,)), ((), ())), preferred_element_type=jnp.float32
    )


def on_device(
    inputs,
    hidden_grad,
    token_key,
    feature_key,
    drop_seed,
    gate_weight,
    up_weight,
    gate_first,
    gate_second,
    up_first,
    up_second,
):
    groups = lax.axis_size("dp")
    own_rows = gate_weight.shape[0]
    own_units = gate_weight.shape[1]
    rows = lax.all_gather(inputs, "tensor", axis=0, tiled=True)
    gate_full, up_full = (
        lax.all_gather(gate_weight, "dp", axis=0, tiled=True),
        lax.all_gather(up_weight, "dp", axis=0, tiled=True),
    )
    gate = jnp.dot(rows, gate_full, preferred_element_type=jnp.float32)
    up = jnp.dot(rows, up_full, preferred_element_type=jnp.float32)
    keep = keep_factor(token_key, feature_key, drop_seed)
    tanh_part = jnp.tanh(gelu_coeff * (gate + 0.044715 * gate * gate * gate))
    act = 0.5 * gate * (1.0 + tanh_part)
    slope = 0.5 * (1.0 + tanh_part) + 0.5 * gate * (1.0 - tanh_part * tanh_part) * gelu_coeff * (
        1.0 + 3.0 * 0.044715 * gate * gate
    )
    dropped = hidden_grad.astype(jnp.float32) * keep
    dgate = (dropped * up * slope).astype(jnp.bfloat16)
    dup = (dropped * act).astype(jnp.bfloat16)
    partial_input = contract_cols(dgate, gate_full) + contract_cols(dup, up_full)
    input_grad = lax.psum_scatter(partial_input, "tensor", scatter_dimension=0, tiled=True).astype(
        jnp.bfloat16
    )
    part_gate = contract_rows(rows, dgate)
    part_up = contract_rows(rows, dup)
    recv_gate, recv_up = (
        lax.all_to_all(part_gate, "dp", split_axis=0, concat_axis=0, tiled=True),
        lax.all_to_all(part_up, "dp", split_axis=0, concat_axis=0, tiled=True),
    )
    grad_gate = jnp.sum(recv_gate.reshape(groups, own_rows, own_units), axis=0)
    grad_up = jnp.sum(recv_up.reshape(groups, own_rows, own_units), axis=0)
    gate_updated, gate_first_new, gate_second_new = adamw(
        gate_weight, gate_first, gate_second, grad_gate
    )
    up_updated, up_first_new, up_second_new = adamw(up_weight, up_first, up_second, grad_up)
    return (
        input_grad,
        gate_updated,
        up_updated,
        gate_first_new,
        gate_second_new,
        up_first_new,
        up_second_new,
    )


def solution(mesh):
    placed = (
        P(("dp", "tensor"), None),
        P("dp", "tensor"),
        P("dp"),
        P("tensor"),
        P(),
        P("dp", "tensor"),
        P("dp", "tensor"),
        P("dp", "tensor"),
        P("dp", "tensor"),
        P("dp", "tensor"),
        P("dp", "tensor"),
    )
    return jax.shard_map(
        on_device,
        mesh=mesh,
        in_specs=placed,
        out_specs=(
            P(("dp", "tensor"), None),
            P("dp", "tensor"),
            P("dp", "tensor"),
            P("dp", "tensor"),
            P("dp", "tensor"),
            P("dp", "tensor"),
            P("dp", "tensor"),
        ),
        check_vma=False,
    )
```

profile of v0, /device:TPU:262, one launch (start us, length us, event | category | flops | bytes accessed | tf_op | source)
XLA Modules:
  0.0 534.2 jit_solution(16252138896034400194)
XLA Ops:
  7.2 0.0 copy-start.2
  7.2 0.0 all-gather.4.cloned.1.call-start
  7.2 0.7 all-gather.4.cloned.1.call-update
  7.9 0.0 all-gather.8.cloned.1.call-start
  8.0 0.7 all-gather.8.cloned.1.call-update
  9.3 0.7 broadcast_multiply_fusion.1
  10.0 0.7 broadcast_multiply_fusion
  10.7 67.2 %all-gather.4.cloned.1.call-done = bf16[256,2304]{1,0:T(8,128)(2,1)} async-done(((bf16[8,2304]{1,0:T(8,128)(2,1)}), bf16[256,2304]{1,0:T(8,128)(2,1)}) %all-gather.4.cloned.1.call-update) | async-done | bytes 1179664 | tf_op jit(solution)/shard_map/all_gather | solution.py:66
  77.8 0.0 copy-start
  77.8 97.0 %all-gather.8.cloned.1.call-done = bf16[2304,576]{1,0:T(8,128)(2,1)} async-done(((bf16[144,576]{1,0:T(8,128)(2,1)}), bf16[2304,576]{1,0:T(8,128)(2,1)}) %all-gather.8.cloned.1.call-update) | async-done | bytes 2654224 | tf_op jit(solution)/shard_map/all_gather | solution.py:68
  174.8 3.4 fusion.17
  178.3 0.0 copy-done.2
  178.3 0.0 copy-done
  178.3 3.6 convolution_bitcast_fusion
  181.9 6.3 %copy.19 = f32[2304,576]{1,0:T(8,128)} copy(f32[2304,576]{0,1:T(8,128)} %convolution_bitcast_fusion) | data formatting | bytes 10616832 | tf_op jit(solution)/shard_map/dot_general | solution.py:39
  188.2 9.6 %all-to-all-start.1 = ((f32[16,144,576]{2,1,0:T(8,128)}), f32[16,144,576]{2,1,0:T(8,128)}, u32[]{:S(2)}, u32[]{:S(2)}) async-start(f32[16,144,576]{2,1,0:T(8,128)} %bitcast.18), calls=%async_computation.2 | async-start | bytes 11796480 | tf_op jit(solution)/shard_map/all_to_all | solution.py:90
  197.8 0.0 all-gather.6.cloned.1.call-start
  197.9 0.7 all-gather.6.cloned.1.call-update
  198.6 150.9 %all-gather.6.cloned.1.call-done = bf16[2304,576]{1,0:T(8,128)(2,1)} async-done(((bf16[144,576]{1,0:T(8,128)(2,1)}), bf16[2304,576]{1,0:T(8,128)(2,1)}) %all-gather.6.cloned.1.call-update) | async-done | bytes 2654224 | tf_op jit(solution)/shard_map/all_gather | solution.py:69
  349.5 3.6 fusion.1
  353.0 3.2 convolution_bitcast_fusion.1
  356.2 6.3 %copy.18 = f32[2304,576]{1,0:T(8,128)} copy(f32[2304,576]{0,1:T(8,128)} %convolution_bitcast_fusion.1) | data formatting | bytes 10616832 | tf_op jit(solution)/shard_map/dot_general | solution.py:39
  362.6 0.0 all-to-all-done.1
  362.6 10.6 %all-to-all-start = ((f32[16,144,576]{2,1,0:T(8,128)}), f32[16,144,576]{2,1,0:T(8,128)}, u32[]{:S(2)}, u32[]{:S(2)}) async-start(f32[16,144,576]{2,1,0:T(8,128)} %bitcast.17), calls=%async_computation.1 | async-start | bytes 11796480 | tf_op jit(solution)/shard_map/all_to_all | solution.py:89
  373.2 0.0 reduce-scatter.2.cloned.1.call-start
  373.2 0.0 copy-start.1
  373.2 3.1 fusion.18
  376.4 0.0 copy-done.1
  376.4 3.1 convolution_add_fusion
  379.5 0.0 reduce-scatter.2.cloned.1.call-update
  379.5 138.2 %reduce-scatter.2.cloned.1.call-done = f32[8,2304]{1,0:T(8,128)} async-done(((f32[256,2304]{1,0:T(8,128)}), f32[8,2304]{1,0:T(8,128)}) %reduce-scatter.2.cloned.1.call-update) | async-done | bytes 73744 | tf_op jit(solution)/shard_map/reduce_scatter | solution.py:83
  517.6 1.5 convert_element_type.27
  519.1 0.0 copy-start.3
  519.1 0.0 copy-start.5
  519.2 0.0 copy-start.6
  519.2 3.1 reduce_sum.19
  522.2 0.0 copy-done.3
  522.2 0.0 copy-done.5
  522.3 0.0 copy-done.6
  522.3 1.1 fusion.12
  523.4 0.0 copy-start.4
  523.4 0.0 copy-start.7
  523.4 0.0 all-to-all-done
  523.4 3.1 reduce_sum.18
  526.5 0.0 copy-done.4
  526.5 0.0 copy-done.7
  526.5 0.0 copy-done.8
  526.5 1.1 fusion.9
  (1 shorter events, 0.0 us)
Async XLA Ops:
  7.2 171.1 %copy-start.2 = (bf16[256,576]{0,1:T(8,128)(2,1)S(1)}, bf16[256,576]{0,1:T(8,128)(2,1)}, u32[]{:S(2)}) copy-start(bf16[256,576]{0,1:T(8,128)(2,1)} %param.12) | copy-start | bytes 884740
  7.2 70.7 %all-gather.4.cloned.1.call-start = ((), (), s32[]{:S(2)}) async-start(), calls=%async_computation.3 | async-start | bytes 1216512 | tf_op jit(solution)/shard_map/all_gather | solution.py:66
  7.9 166.9 %all-gather.8.cloned.1.call-start = ((), (), s32[]{:S(2)}) async-start(), calls=%async_computation.5 | async-start | bytes 3133440 | tf_op jit(solution)/shard_map/all_gather | solution.py:68
  77.8 100.4 %copy-start = (bf16[256,2304]{1,0:T(8,128)(2,1)S(1)}, bf16[256,2304]{1,0:T(8,128)(2,1)}, u32[]{:S(2)}) copy-start(bf16[256,2304]{1,0:T(8,128)(2,1)} %all-gather.4.cloned.1.call-done) | copy-start | bytes 3538948
  188.2 174.3 %all-to-all-start.1 = ((f32[16,144,576]{2,1,0:T(8,128)}), f32[16,144,576]{2,1,0:T(8,128)}, u32[]{:S(2)}, u32[]{:S(2)}) async-start(f32[16,144,576]{2,1,0:T(8,128)} %bitcast.18), calls=%async_computation.2 | async-start | bytes 11796480 | tf_op jit(solution)/shard_map/all_to_all | solution.py:90
  197.8 151.6 %all-gather.6.cloned.1.call-start = ((), (), s32[]{:S(2)}) async-start(), calls=%async_computation.4 | async-start | bytes 3133440 | tf_op jit(solution)/shard_map/all_gather | solution.py:69
  362.6 160.8 %all-to-all-start = ((f32[16,144,576]{2,1,0:T(8,128)}), f32[16,144,576]{2,1,0:T(8,128)}, u32[]{:S(2)}, u32[]{:S(2)}) async-start(f32[16,144,576]{2,1,0:T(8,128)} %bitcast.17), calls=%async_computation.1 | async-start | bytes 11796480 | tf_op jit(solution)/shard_map/all_to_all | solution.py:89
  373.2 144.5 %reduce-scatter.2.cloned.1.call-start = ((), (), s32[]{:S(2)}) async-start(), calls=%async_computation.6 | async-start | bytes 2433024 | tf_op jit(solution)/shard_map/reduce_scatter | solution.py:83
  373.2 3.2 copy-start.1
  519.1 3.1 copy-start.3
  519.1 3.1 copy-start.5
  519.2 3.1 copy-start.6
  523.4 3.1 copy-start.4
  523.4 3.1 copy-start.7
  523.4 3.1 copy-start.8
Sparse Core Ops, SparseCore 0:
  10.2 67.6 all-gather.3
  81.0 93.7 all-gather.7
  201.9 147.5 all-gather.5
  379.6 137.9 reduce-scatter.1
where the time goes:
time: 535 us; the launch traced here: 534 us
  waiting for transfers between devices  455 us (85%)
  starting transfers between devices  20.4 us (4%)
  matrix products  20 us (4%)
  between operations  14.5 us (3%)
  local copies, waits for them, and re-layouts  12.7 us (2%)
  other arithmetic  11.3 us (2%)
    all_gather x1, waiting for transfers between devices, on_device(): lax.all_gather(up_weight, 'dp', axis=0, tiled=True)  151 us
    reduce_scatter x1, waiting for transfers between devices, on_device(): lax.psum_scatter(partial_input, 'tensor', scatter_dimension=0, tiled=True)  138 us
    all_gather x1, waiting for transfers between devices, on_device(): lax.all_gather(gate_weight, 'dp', axis=0, tiled=True)  97 us
    all_gather x1, waiting for transfers between devices, on_device(): rows = lax.all_gather(inputs, 'tensor', axis=0, tiled=True)  67.2 us
    dot_general x2, local copies, waits for them, and re-layouts, contract_rows(): lax.dot_general(left, right, (((0,), (0,)), ((), ())), preferred_element_...  12.6 us
  transfers between devices with their start and end apart: 6, of which 4 were waited for; matrix products, arithmetic and copies ran while one was open for 5% of the time, Pallas kernels for 0%

commit v1 on v0

v1 whole, which is shorter than its diff:
```python
import math

import jax
import jax.numpy as jnp
from jax import lax
from jax.sharding import Mesh
from jax.sharding import PartitionSpec as P

drop_level = 6554
keep_scale = 65536.0 / (65536.0 - 6554.0)
gelu_coeff = math.sqrt(2.0 / math.pi)
first_fix = 1.0 - 0.9**10
second_fix = 1.0 - 0.95**10
bf16 = jnp.bfloat16
f32 = jnp.float32

plane = ("xh", "xl", "y")


def keep_mask(token_key, feature_key, drop_seed):
    mixed = (
        token_key[:, None] * -1640531535
        + feature_key[None, :] * -1028477379
        + drop_seed[0] * 668265263
    )
    mixed = mixed ^ mixed >> 15 & 131071
    mixed = mixed * -2048144789
    mixed = mixed ^ mixed >> 13 & 524287
    mixed = mixed * -1028477387
    mixed = mixed ^ mixed >> 16 & 65535
    level = mixed & 65535
    return level >= drop_level


def adamw(weight, first, second, grad):
    first_new = 0.9 * first + 0.1 * grad
    second_new = 0.95 * second + 0.05 * grad * grad
    wide = weight.astype(f32)
    step = first_new / first_fix / (jnp.sqrt(second_new / second_fix) + 1e-08) + 0.1 * wide
    return ((wide - 0.01 * step).astype(bf16), first_new, second_new)


def swap(x, axis):
    return lax.ppermute(x, axis, [(0, 1), (1, 0)])


def pick(index, first, second):
    return jnp.where(index == 0, first, second), jnp.where(index == 0, second, first)


def ring_sum(terms, axis):
    count = terms.shape[0]
    place = lax.axis_index(axis)
    right = [(i, (i + 1) % count) for i in range(count)]
    left = [(i, (i - 1) % count) for i in range(count)]

    def term(step):
        return lax.dynamic_index_in_dim(terms, lax.rem(place + step + count, count), 0, False)

    ahead, behind = count // 2, count - 1 - count // 2
    rightward, leftward = term(ahead), term(-behind) if behind else 0.0
    for step in range(ahead - 1, -1, -1):
        rightward = lax.ppermute(rightward.astype(bf16), axis, right).astype(f32)
        if step:
            rightward = rightward + term(step)
        if step <= behind - 1:
            leftward = lax.ppermute(leftward.astype(bf16), axis, left).astype(f32)
            if step:
                leftward = leftward + term(-step)
    return rightward + leftward + term(0)


def on_device(
    inputs,
    hidden_grad,
    token_key,
    feature_key,
    drop_seed,
    gate_weight,
    up_weight,
    gate_first,
    gate_second,
    up_first,
    up_second,
):
    xh = lax.axis_index("xh")
    core = lax.axis_index("core")
    own_rows, own_units = gate_weight.shape
    half = own_units // 2
    model = inputs.shape[1]
    own_inputs = inputs.shape[0]

    low = jnp.concatenate([gate_weight[:, :half], up_weight[:, :half]], axis=1)
    high = jnp.concatenate([gate_weight[:, half:], up_weight[:, half:]], axis=1)
    mine, other = pick(xh, low, high)
    other = swap(other, "xh")
    first_rows, second_rows = pick(xh, mine, other)
    weights = lax.all_gather(
        jnp.concatenate([first_rows, second_rows], axis=0), "z", axis=0, tiled=True
    )

    peers = lax.axis_size(plane)
    spread = jnp.broadcast_to(inputs[None], (peers,) + inputs.shape)
    rows = lax.all_to_all(spread, plane, split_axis=0, concat_axis=0).reshape(-1, model)
    rows = jnp.concatenate([rows, swap(rows, "core")], axis=0)

    keep = keep_mask(token_key, feature_key, drop_seed)
    masked = jnp.where(keep, hidden_grad, jnp.zeros_like(hidden_grad))
    mine_grad, other_grad = pick(xh, masked[:, :half], masked[:, half:])
    other_grad = swap(other_grad, "xh")
    lower, upper = pick(xh, mine_grad, other_grad)
    kept = jnp.concatenate([lower, upper], axis=0)
    kept = kept.reshape(-1, 2, own_inputs, half)
    kept = jnp.concatenate(pick(core, kept[:, 0], kept[:, 1]), axis=0).reshape(-1, half)

    both = jnp.dot(rows, weights, preferred_element_type=f32)
    gate, up = both[:, :half], both[:, half:]
    tanh_part = jnp.tanh(gelu_coeff * (gate + 0.044715 * gate * gate * gate))
    act = 0.5 * gate * (1.0 + tanh_part)
    slope = 0.5 * (1.0 + tanh_part) + 0.5 * gate * (1.0 - tanh_part * tanh_part) * gelu_coeff * (
        1.0 + 3.0 * 0.044715 * gate * gate
    )
    dropped = kept.astype(f32) * keep_scale
    dgate = (dropped * up * slope).astype(bf16)
    dup = (dropped * act).astype(bf16)
    dboth = jnp.concatenate([dgate, dup], axis=1)

    terms = lax.dot_general(rows, dboth, (((0,), (0,)), ((), ())), preferred_element_type=f32)
    terms, dboth = lax.optimization_barrier((terms, dboth))
    terms = terms.reshape(-1, 2, own_rows, own_units)
    own_terms, partner_terms = pick(xh, terms[:, 0], terms[:, 1])
    own_sum = lax.psum_scatter(own_terms, "z", scatter_dimension=0)
    partner_sum = ring_sum(partner_terms, "z")

    partial = lax.dot_general(
        dboth, weights, (((1,), (1,)), ((), ())), preferred_element_type=f32
    )
    here = partial.shape[0] // 2
    pair = partial[:here] + swap(partial[here:], "core")
    shares = lax.all_to_all(
        pair.astype(bf16).reshape(peers, own_inputs, model), plane, split_axis=0, concat_axis=0
    )
    input_grad = jnp.sum(shares.astype(f32), axis=0).astype(bf16)

    got_sum = swap(partner_sum.astype(bf16), "xh").astype(f32)
    low_sum, high_sum = pick(xh, own_sum, got_sum)
    grad_gate = jnp.concatenate([low_sum[:, :half], high_sum[:, :half]], axis=1)
    grad_up = jnp.concatenate([low_sum[:, half:], high_sum[:, half:]], axis=1)

    gate_updated, gate_first_new, gate_second_new = adamw(
        gate_weight, gate_first, gate_second, grad_gate
    )
    up_updated, up_first_new, up_second_new = adamw(up_weight, up_first, up_second, grad_up)
    return (
        input_grad,
        gate_updated,
        up_updated,
        gate_first_new,
        gate_second_new,
        up_first_new,
        up_second_new,
    )


def solution(mesh):
    dp_size, tensor_size = mesh.devices.shape
    fine = Mesh(
        mesh.devices.reshape(dp_size // 2, 2, 2, tensor_size // 4, 2), ("z", "xh", "xl", "y", "core")
    )
    dp, tensor = ("z", "xh"), ("xl", "y", "core")
    grid = P(dp, tensor)
    every = P(dp + tensor, None)
    return jax.shard_map(
        on_device,
        mesh=fine,
        in_specs=(every, grid, P(dp), P(tensor), P()) + (grid,) * 6,
        out_specs=(every,) + (grid,) * 6,
        check_vma=False,
    )
```

time: 535 us -> 198 us (0.37)
  the two profiles are of different devices: /device:TPU:262 before, /device:TPU:2 now
where the time goes in v1:
time: 198 us
  waiting for transfers between devices  73.6 us (37%)
  starting transfers between devices  63.2 us (32%)
  other arithmetic  20.8 us (11%)
  between operations  15.2 us (8%)
  matrix products  13 us (7%)
  local copies, waits for them, and re-layouts  11.7 us (6%)
    all_to_all x1, waiting for transfers between devices, on_device(): lax.all_to_all(spread, plane, split_axis=0, concat_axis=0)  26.9 us
    ppermute x4, waiting for transfers between devices, ring_sum(): rightward = lax.ppermute(rightward.astype(bf16), axis, right).astype(f32)  26.5 us
    ppermute x3, starting transfers between devices, ring_sum(): leftward = lax.ppermute(leftward.astype(bf16), axis, left).astype(f32)  19.1 us
    ppermute x5, waiting for transfers between devices, swap(): return lax.ppermute(x, axis, [(0, 1), (1, 0)])  17.6 us
    ppermute x5, starting transfers between devices, swap(): return lax.ppermute(x, axis, [(0, 1), (1, 0)])  16.2 us
    all_to_all x1, starting transfers between devices, on_device(): lax.all_to_all(spread, plane, split_axis=0, concat_axis=0)  10.3 us
    ppermute x4, starting transfers between devices, ring_sum(): rightward = lax.ppermute(rightward.astype(bf16), axis, right).astype(f32)  8.84 us
    all_to_all x1, starting transfers between devices, on_device(): lax.all_to_all(pair.astype(bf16).reshape(peers, own_inputs, model), plane...  8.78 us
  transfers between devices with their start and end apart: 16, of which 11 were waited for; matrix products, arithmetic and copies ran while one was open for 9% of the time, Pallas kernels for 0%

profile of v1, /device:TPU:2, one launch (start us, length us, event | category | flops | bytes accessed | tf_op | source)
XLA Modules:
  0.0 197.5 jit_solution(14171373722880250752)
XLA Ops:
  7.2 1.2 fusion.37
  8.6 4.0 %collective-permute-start.2 = (bf16[144,576]{1,0:T(8,128)(2,1)S(1)}, bf16[144,576]{1,0:T(8,128)(2,1)S(1)}, u32[]{:S(2)}, u32[]{:S(2)}) collective-permute-start(bf16[144,576]{1,0:T(8,128)(2,1)S(1)} %broadcast_select_fusion.6), channel_id=1, source_target_pairs={{0,32},{32,0},{1,33},{33,1},{2,34},{34,2},{3,35},{35,3},{4,36},{36... | collective-permute-start | bytes 497672 | tf_op jit(solution)/shard_map/ppermute | solution.py:44
  12.6 5.7 %collective-permute-done.2 = bf16[144,576]{1,0:T(8,128)(2,1)S(1)} collective-permute-done((bf16[144,576]{1,0:T(8,128)(2,1)S(1)}, bf16[144,576]{1,0:T(8,128)(2,1)S(1)}, u32[]{:S(2)}, u32[]{:S(2)}) %collective-permute-start.2) | collective-permute-done | bytes 165920 | tf_op jit(solution)/shard_map/ppermute | solution.py:44
  18.5 0.8 pad_maximum_fusion.5
  19.4 1.1 broadcast_in_dim.4
  20.5 10.3 %all-to-all-start = ((bf16[32,8,2304]{2,1,0:T(8,128)(2,1)}), bf16[32,8,2304]{2,1,0:T(8,128)(2,1)S(1)}, u32[]{:S(2)}, u32[]{:S(2)}) async-start(bf16[32,8,2304]{2,1,0:T(8,128)(2,1)} %broadcast_in_dim.4), calls=%async_computation | async-start | bytes 2359296 | tf_op jit(solution)/shard_map/all_to_all | solution.py:104
  30.8 0.2 copy.22
  31.7 0.4 fusion.5
  32.1 26.9 %all-to-all-done = bf16[32,8,2304]{2,1,0:T(8,128)(2,1)S(1)} async-done(((bf16[32,8,2304]{2,1,0:T(8,128)(2,1)}), bf16[32,8,2304]{2,1,0:T(8,128)(2,1)S(1)}, u32[]{:S(2)}, u32[]{:S(2)}) %all-to-all-start) | async-done | bytes 1179680 | tf_op jit(solution)/shard_map/all_to_all | solution.py:104
  58.9 1.9 collective-permute-start
  61.0 4.3 %collective-permute-start.1 = (bf16[256,288]{1,0:T(8,128)(2,1)S(1)}, bf16[256,288]{1,0:T(8,128)(2,1)S(1)}, u32[]{:S(2)}, u32[]{:S(2)}) collective-permute-start(bf16[256,288]{1,0:T(8,128)(2,1)S(1)} %broadcast_select_fusion.2), channel_id=1, source_target_pairs={{0,32},{32,0},{1,33},{33,1},{2,34},{34,2},{3,35},{35,3},{4,36},{36... | collective-permute-start | bytes 442376 | tf_op jit(solution)/shard_map/ppermute | solution.py:44
  65.3 6.4 %collective-permute-done.1 = bf16[256,288]{1,0:T(8,128)(2,1)S(1)} collective-permute-done((bf16[256,288]{1,0:T(8,128)(2,1)S(1)}, bf16[256,288]{1,0:T(8,128)(2,1)S(1)}, u32[]{:S(2)}, u32[]{:S(2)}) %collective-permute-start.1) | collective-permute-done | bytes 147488 | tf_op jit(solution)/shard_map/ppermute | solution.py:44
  72.0 0.2 copy.27
  72.3 3.8 %fusion.3 = f32[512,576]{0,1:T(8,128)S(1)} fusion(bf16[2304,576]{1,0:T(8,128)(2,1)} %all-gather.2.cloned.1.call-done, bf16[256,2304]{1,0:T(8,128)(2,1)} %collective-permute-done, bf16[256,2304]{1,0:T(8,128)(2,1)S(1)} %bitcast.73), kind=kOutput, calls=%fused_computation.7 | convolution fusion | flops 1363673088 | bytes 6193152 | tf_op jit(solution)/shard_map/dot_general | solution.py:116
  76.1 0.5 fusion.12
  76.6 5.2 %fusion.2 = f32[2304,576]{0,1:T(8,128)} fusion(bf16[256,2304]{1,0:T(8,128)(2,1)} %collective-permute-done, bf16[256,2304]{1,0:T(8,128)(2,1)S(1)} %bitcast.74, bf16[512,288]{0,1:T(8,128)(2,1)S(1)} %get-tuple-element.24, bf16[512,288]{0,1:T(8,128)(2,1)S(1)} %get-tuple-element.23), kind=kOutput, calls=%fused_computation.6 | convolution fusion | flops 1364852736 | bytes 8257536 | tf_op jit(solution)/shard_map/dot_general | solution.py:128
  81.8 6.4 %copy.29 = f32[2304,576]{1,0:T(8,128)} copy(f32[2304,576]{0,1:T(8,128)} %fusion.2) | data formatting | bytes 10616832 | tf_op jit(solution)/shard_map/optimization_barrier | solution.py:129
  88.2 4.0 %fusion.39 = f32[512,2304]{1,0:T(8,128)S(1)} fusion(bf16[512,576]{0,1:T(8,128)(2,1)S(1)} %pad_maximum_fusion.3, bf16[2304,576]{1,0:T(8,128)(2,1)} %all-gather.2.cloned.1.call-done), kind=kOutput, calls=%fused_computation.84 | convolution fusion | flops 1358954496 | bytes 7962624 | tf_op jit(solution)/shard_map/dot_general | solution.py:135
  92.4 2.0 %copy-done.1 = f32[512,2304]{1,0:T(8,128)} copy-done((f32[512,2304]{1,0:T(8,128)}, f32[512,2304]{1,0:T(8,128)S(1)}, u32[]{:S(2)}) %copy-start.1) | copy-done | bytes 4718616
  94.4 1.9 collective-permute-start.3
  96.4 2.0 %fusion = f32[8,144,576]{2,1,0:T(8,128)} fusion(f32[8,2,144,576]{3,2,1,0:T(8,128)S(1)} %bitcast.71, pred[]{:T(512)S(6)} %eq.5), kind=kLoop, calls=%fused_computation.1 | loop fusion | flops 663552 | bytes 7962625 | tf_op jit(solution)/shard_map/jit(_where)/select_n | solution.py:48
  98.4 2.6 %collective-permute-done.3 = f32[256,2304]{1,0:T(8,128)} collective-permute-done((f32[256,2304]{1,0:T(8,128)S(1)}, f32[256,2304]{1,0:T(8,128)}, u32[]{:S(2)}, u32[]{:S(2)}) %collective-permute-start.3) | collective-permute-done | bytes 2359328 | tf_op jit(solution)/shard_map/ppermute | solution.py:44
  101.0 3.6 %fusion.4 = bf16[32,8,2304]{2,1,0:T(8,128)(2,1)} fusion(f32[256,2304]{1,0:T(8,128)} %collective-permute-done.3, f32[512,2304]{1,0:T(8,128)} %copy-done.1), kind=kLoop, calls=%fused_computation.8 | loop fusion | flops 1179648 | bytes 5898240 | tf_op jit(solution)/shard_map/reshape | solution.py:141
  104.6 8.8 %all-to-all-start.1 = ((bf16[32,8,2304]{2,1,0:T(8,128)(2,1)}), bf16[32,8,2304]{2,1,0:T(8,128)(2,1)}, u32[]{:S(2)}, u32[]{:S(2)}) async-start(bf16[32,8,2304]{2,1,0:T(8,128)(2,1)} %fusion.4), calls=%async_computation.1 | async-start | bytes 2359296 | tf_op jit(solution)/shard_map/all_to_all | solution.py:140
  113.4 3.3 %bitcast_select_fusion.1 = f32[8,1,144,576]{3,2,1,0:T(8,128)S(1)} fusion(f32[8,2,144,576]{3,2,1,0:T(8,128)} %bitcast.70, pred[]{:T(512)S(6)} %eq.5), kind=kLoop, calls=%fused_computation.2 | loop fusion | flops 663552 | bytes 7962625 | tf_op jit(solution)/shard_map/jit(_where)/select_n | solution.py:48
  116.8 3.1 %collective-permute-start.4 = (bf16[144,576]{1,0:T(8,128)(2,1)S(1)}, bf16[144,576]{1,0:T(8,128)(2,1)}, u32[]{:S(2)}, u32[]{:S(2)}) collective-permute-start(bf16[144,576]{1,0:T(8,128)(2,1)S(1)} %get-tuple-element.21), channel_id=1, source_target_pairs={{0,64},{64,128},{128,192},{192,256},{256,320},{320,384},{384,448},... | collective-permute-start | bytes 497672 | tf_op jit(solution)/shard_map/ppermute | solution.py:63
  119.9 8.3 %collective-permute-start.8 = (bf16[144,576]{1,0:T(8,128)(2,1)S(1)}, bf16[144,576]{1,0:T(8,128)(2,1)S(1)}, u32[]{:S(2)}, u32[]{:S(2)}) collective-permute-start(bf16[144,576]{1,0:T(8,128)(2,1)S(1)} %get-tuple-element.22), channel_id=1, source_target_pairs={{0,448},{64,0},{128,64},{192,128},{256,192},{320,256},{384,320},{4... | collective-permute-start | bytes 497672 | tf_op jit(solution)/shard_map/ppermute | solution.py:67
  128.2 7.1 %collective-permute-done.4 = bf16[144,576]{1,0:T(8,128)(2,1)} collective-permute-done((bf16[144,576]{1,0:T(8,128)(2,1)S(1)}, bf16[144,576]{1,0:T(8,128)(2,1)}, u32[]{:S(2)}, u32[]{:S(2)}) %collective-permute-start.4) | collective-permute-done | bytes 165920 | tf_op jit(solution)/shard_map/ppermute | solution.py:63
  135.3 1.0 fusion.26
  136.3 1.9 collective-permute-start.5
  138.2 12.1 %collective-permute-done.5 = bf16[144,576]{1,0:T(8,128)(2,1)} collective-permute-done((bf16[144,576]{1,0:T(8,128)(2,1)S(1)}, bf16[144,576]{1,0:T(8,128)(2,1)}, u32[]{:S(2)}, u32[]{:S(2)}) %collective-permute-start.5) | collective-permute-done | bytes 165920 | tf_op jit(solution)/shard_map/ppermute | solution.py:63
  150.3 1.0 fusion.25
  151.3 1.9 collective-permute-start.6
  153.2 5.1 %collective-permute-start.9 = (bf16[144,576]{1,0:T(8,128)(2,1)S(1)}, bf16[144,576]{1,0:T(8,128)(2,1)}, u32[]{:S(2)}, u32[]{:S(2)}) collective-permute-start(bf16[144,576]{1,0:T(8,128)(2,1)S(1)} %get-tuple-element.20), channel_id=1, source_target_pairs={{0,448},{64,0},{128,64},{192,128},{256,192},{320,256},{384,320},{4... | collective-permute-start | bytes 497672 | tf_op jit(solution)/shard_map/ppermute | solution.py:67
  158.4 1.6 collective-permute-done.6
  159.9 1.5 collective-permute-done.9
  161.4 1.0 fusion.24
  162.4 5.7 %collective-permute-start.10 = (bf16[144,576]{1,0:T(8,128)(2,1)S(1)}, bf16[144,576]{1,0:T(8,128)(2,1)S(1)}, u32[]{:S(2)}, u32[]{:S(2)}) collective-permute-start(bf16[144,576]{1,0:T(8,128)(2,1)S(1)} %get-tuple-element.18), channel_id=1, source_target_pairs={{0,448},{64,0},{128,64},{192,128},{256,192},{320,256},{384,320},{4... | collective-permute-start | bytes 497672 | tf_op jit(solution)/shard_map/ppermute | solution.py:67
  168.1 1.9 collective-permute-start.7
  170.0 1.1 collective-permute-done.10
  171.1 5.7 %collective-permute-done.7 = bf16[144,576]{1,0:T(8,128)(2,1)} collective-permute-done((bf16[144,576]{1,0:T(8,128)(2,1)S(1)}, bf16[144,576]{1,0:T(8,128)(2,1)}, u32[]{:S(2)}, u32[]{:S(2)}) %collective-permute-start.7) | collective-permute-done | bytes 165920 | tf_op jit(solution)/shard_map/ppermute | solution.py:63
  176.8 1.0 fusion.21
  177.9 4.1 %collective-permute-start.11 = (bf16[144,576]{1,0:T(8,128)(2,1)S(1)}, bf16[144,576]{1,0:T(8,128)(2,1)S(1)}, u32[]{:S(2)}, u32[]{:S(2)}) collective-permute-start(bf16[144,576]{1,0:T(8,128)(2,1)S(1)} %fusion.21), channel_id=1, source_target_pairs={{0,32},{32,0},{1,33},{33,1},{2,34},{34,2},{3,35},{35,3},{4,36},{36... | collective-permute-start | bytes 497672 | tf_op jit(solution)/shard_map/ppermute | solution.py:44
  182.0 2.1 %reduce_sum.12 = bf16[8,2304]{1,0:T(8,128)(2,1)} reduce(bf16[32,8,2304]{2,1,0:T(8,128)(2,1)} %all-to-all-done.1, bf16[]{:T(256)} %constant.117.clone.1), dimensions={0}, to_apply=%region_0.1 | reduce | flops 571392 | bytes 1216514 | tf_op jit(solution)/shard_map/reduce_sum | solution.py:143
  184.0 2.9 %collective-permute-done.11 = bf16[144,576]{1,0:T(8,128)(2,1)S(1)} collective-permute-done((bf16[144,576]{1,0:T(8,128)(2,1)S(1)}, bf16[144,576]{1,0:T(8,128)(2,1)S(1)}, u32[]{:S(2)}, u32[]{:S(2)}) %collective-permute-start.11) | collective-permute-done | bytes 165920 | tf_op jit(solution)/shard_map/ppermute | solution.py:44
  186.9 1.0 convert_select_fusion.1
  188.2 1.2 fusion.18
  189.5 1.2 fusion.15
  (47 shorter events, 1.5 us)
Async XLA Ops:
  7.2 12.2 %copy-start.9 = (bf16[8,2304]{1,0:T(8,128)(2,1)S(1)}, bf16[8,2304]{1,0:T(8,128)(2,1)}, u32[]{:S(2)}) copy-start(bf16[8,2304]{1,0:T(8,128)(2,1)} %param.11) | copy-start | bytes 110596
  7.2 65.1 %all-gather.2.cloned.1.call-start = ((), (), s32[]{:S(2)}) async-start(), calls=%async_computation.3 | async-start | bytes 3317760 | tf_op jit(solution)/shard_map/all_gather | solution.py:98
  8.6 9.8 %collective-permute-start.2 = (bf16[144,576]{1,0:T(8,128)(2,1)S(1)}, bf16[144,576]{1,0:T(8,128)(2,1)S(1)}, u32[]{:S(2)}, u32[]{:S(2)}) collective-permute-start(bf16[144,576]{1,0:T(8,128)(2,1)S(1)} %broadcast_select_fusion.6), channel_id=1, source_target_pairs={{0,32},{32,0},{1,33},{33,1},{2,34},{34,2},{3,35},{35,3},{4,36},{36... | collective-permute-start | bytes 497672 | tf_op jit(solution)/shard_map/ppermute | solution.py:44
  18.5 12.3 %copy-start.8 = (bf16[256,576]{0,1:T(8,128)(2,1)S(1)}, bf16[256,576]{0,1:T(8,128)(2,1)}, u32[]{:S(2)}) copy-start(bf16[256,576]{0,1:T(8,128)(2,1)} %param.12) | copy-start | bytes 884740
  19.3 12.3 %copy-start.11 = (s32[256]{0:T(256)S(1)}, s32[256]{0:T(256)}, u32[]{:S(2)}) copy-start(s32[256]{0:T(256)} %param.13) | copy-start | bytes 3076
  19.3 12.4 %copy-start.10 = (s32[576]{0:T(1024)S(1)}, s32[576]{0:T(1024)}, u32[]{:S(2)}) copy-start(s32[576]{0:T(1024)} %param.14) | copy-start | bytes 6916
  20.5 38.5 %all-to-all-start = ((bf16[32,8,2304]{2,1,0:T(8,128)(2,1)}), bf16[32,8,2304]{2,1,0:T(8,128)(2,1)S(1)}, u32[]{:S(2)}, u32[]{:S(2)}) async-start(bf16[32,8,2304]{2,1,0:T(8,128)(2,1)} %broadcast_in_dim.4), calls=%async_computation | async-start | bytes 2359296 | tf_op jit(solution)/shard_map/all_to_all | solution.py:104
  30.7 156.2 %reduce-scatter.2.cloned.1.call-start = ((), (), s32[]{:S(2)}) async-start(), calls=%async_computation.4 | async-start | bytes 3317760 | tf_op jit(solution)/shard_map/reduce_scatter | solution.py:132
  58.9 13.3 %collective-permute-start = (bf16[256,2304]{1,0:T(8,128)(2,1)S(1)}, bf16[256,2304]{1,0:T(8,128)(2,1)}, u32[]{:S(2)}, u32[]{:S(2)}) collective-permute-start(bf16[256,2304]{1,0:T(8,128)(2,1)S(1)} %bitcast.72), channel_id=1, source_target_pairs={{0,1},{1,0},{2,3},{3,2},{4,5},{5,4},{6,7},{7,6},{8,9},{9,8},{10,11... | collective-permute-start | bytes 3538952 | tf_op jit(solution)/shard_map/ppermute | solution.py:44
  61.0 10.7 %collective-permute-start.1 = (bf16[256,288]{1,0:T(8,128)(2,1)S(1)}, bf16[256,288]{1,0:T(8,128)(2,1)S(1)}, u32[]{:S(2)}, u32[]{:S(2)}) collective-permute-start(bf16[256,288]{1,0:T(8,128)(2,1)S(1)} %broadcast_select_fusion.2), channel_id=1, source_target_pairs={{0,32},{32,0},{1,33},{33,1},{2,34},{34,2},{3,35},{35,3},{4,36},{36... | collective-permute-start | bytes 442376 | tf_op jit(solution)/shard_map/ppermute | solution.py:44
  88.2 8.2 %copy-start = (f32[2304,576]{1,0:T(8,128)S(1)}, f32[2304,576]{1,0:T(8,128)}, u32[]{:S(2)}) copy-start(f32[2304,576]{1,0:T(8,128)} %copy.29) | copy-start | bytes 15925252
  92.2 2.2 %copy-start.1 = (f32[512,2304]{1,0:T(8,128)}, f32[512,2304]{1,0:T(8,128)S(1)}, u32[]{:S(2)}) copy-start(f32[512,2304]{1,0:T(8,128)S(1)} %fusion.39) | copy-start | bytes 14155780
  94.4 6.5 %collective-permute-start.3 = (f32[256,2304]{1,0:T(8,128)S(1)}, f32[256,2304]{1,0:T(8,128)}, u32[]{:S(2)}, u32[]{:S(2)}) collective-permute-start(f32[256,2304]{1,0:T(8,128)S(1)} %slice.79), channel_id=1, source_target_pairs={{0,1},{1,0},{2,3},{3,2},{4,5},{5,4},{6,7},{7,6},{8,9},{9,8},{10,11... | collective-permute-start | bytes 7077896 | tf_op jit(solution)/shard_map/ppermute | solution.py:44
  104.6 77.4 %all-to-all-start.1 = ((bf16[32,8,2304]{2,1,0:T(8,128)(2,1)}), bf16[32,8,2304]{2,1,0:T(8,128)(2,1)}, u32[]{:S(2)}, u32[]{:S(2)}) async-start(bf16[32,8,2304]{2,1,0:T(8,128)(2,1)} %fusion.4), calls=%async_computation.1 | async-start | bytes 2359296 | tf_op jit(solution)/shard_map/all_to_all | solution.py:140
  116.8 18.5 %collective-permute-start.4 = (bf16[144,576]{1,0:T(8,128)(2,1)S(1)}, bf16[144,576]{1,0:T(8,128)(2,1)}, u32[]{:S(2)}, u32[]{:S(2)}) collective-permute-start(bf16[144,576]{1,0:T(8,128)(2,1)S(1)} %get-tuple-element.21), channel_id=1, source_target_pairs={{0,64},{64,128},{128,192},{192,256},{256,320},{320,384},{384,448},... | collective-permute-start | bytes 497672 | tf_op jit(solution)/shard_map/ppermute | solution.py:63
  119.9 18.3 %collective-permute-start.8 = (bf16[144,576]{1,0:T(8,128)(2,1)S(1)}, bf16[144,576]{1,0:T(8,128)(2,1)S(1)}, u32[]{:S(2)}, u32[]{:S(2)}) collective-permute-start(bf16[144,576]{1,0:T(8,128)(2,1)S(1)} %get-tuple-element.22), channel_id=1, source_target_pairs={{0,448},{64,0},{128,64},{192,128},{256,192},{320,256},{384,320},{4... | collective-permute-start | bytes 497672 | tf_op jit(solution)/shard_map/ppermute | solution.py:67
  136.3 14.0 %collective-permute-start.5 = (bf16[144,576]{1,0:T(8,128)(2,1)S(1)}, bf16[144,576]{1,0:T(8,128)(2,1)}, u32[]{:S(2)}, u32[]{:S(2)}) collective-permute-start(bf16[144,576]{1,0:T(8,128)(2,1)S(1)} %fusion.26), channel_id=1, source_target_pairs={{0,64},{64,128},{128,192},{192,256},{256,320},{320,384},{384,448},... | collective-permute-start | bytes 497672 | tf_op jit(solution)/shard_map/ppermute | solution.py:63
  151.3 8.6 %collective-permute-start.6 = (bf16[144,576]{1,0:T(8,128)(2,1)S(1)}, bf16[144,576]{1,0:T(8,128)(2,1)S(1)}, u32[]{:S(2)}, u32[]{:S(2)}) collective-permute-start(bf16[144,576]{1,0:T(8,128)(2,1)S(1)} %get-tuple-element.19), channel_id=1, source_target_pairs={{0,64},{64,128},{128,192},{192,256},{256,320},{320,384},{384,448},... | collective-permute-start | bytes 497672 | tf_op jit(solution)/shard_map/ppermute | solution.py:63
  153.2 8.2 %collective-permute-start.9 = (bf16[144,576]{1,0:T(8,128)(2,1)S(1)}, bf16[144,576]{1,0:T(8,128)(2,1)}, u32[]{:S(2)}, u32[]{:S(2)}) collective-permute-start(bf16[144,576]{1,0:T(8,128)(2,1)S(1)} %get-tuple-element.20), channel_id=1, source_target_pairs={{0,448},{64,0},{128,64},{192,128},{256,192},{320,256},{384,320},{4... | collective-permute-start | bytes 497672 | tf_op jit(solution)/shard_map/ppermute | solution.py:67
  162.4 8.7 %collective-permute-start.10 = (bf16[144,576]{1,0:T(8,128)(2,1)S(1)}, bf16[144,576]{1,0:T(8,128)(2,1)S(1)}, u32[]{:S(2)}, u32[]{:S(2)}) collective-permute-start(bf16[144,576]{1,0:T(8,128)(2,1)S(1)} %get-tuple-element.18), channel_id=1, source_target_pairs={{0,448},{64,0},{128,64},{192,128},{256,192},{320,256},{384,320},{4... | collective-permute-start | bytes 497672 | tf_op jit(solution)/shard_map/ppermute | solution.py:67
  168.1 8.7 %collective-permute-start.7 = (bf16[144,576]{1,0:T(8,128)(2,1)S(1)}, bf16[144,576]{1,0:T(8,128)(2,1)}, u32[]{:S(2)}, u32[]{:S(2)}) collective-permute-start(bf16[144,576]{1,0:T(8,128)(2,1)S(1)} %get-tuple-element.17), channel_id=1, source_target_pairs={{0,64},{64,128},{128,192},{192,256},{256,320},{320,384},{384,448},... | collective-permute-start | bytes 497672 | tf_op jit(solution)/shard_map/ppermute | solution.py:63
  177.8 10.4 %copy-start.2 = (bf16[144,576]{1,0:T(8,128)(2,1)S(1)}, bf16[144,576]{1,0:T(8,128)(2,1)}, u32[]{:S(2)}) copy-start(bf16[144,576]{1,0:T(8,128)(2,1)} %param.17) | copy-start | bytes 497668
  177.8 10.4 %copy-start.4 = (f32[144,576]{1,0:T(8,128)S(1)}, f32[144,576]{1,0:T(8,128)}, u32[]{:S(2)}) copy-start(f32[144,576]{1,0:T(8,128)} %param.20) | copy-start | bytes 995332
  177.8 10.4 %copy-start.5 = (f32[144,576]{1,0:T(8,128)S(1)}, f32[144,576]{1,0:T(8,128)}, u32[]{:S(2)}) copy-start(f32[144,576]{1,0:T(8,128)} %param.21) | copy-start | bytes 995332
  177.9 9.1 %collective-permute-start.11 = (bf16[144,576]{1,0:T(8,128)(2,1)S(1)}, bf16[144,576]{1,0:T(8,128)(2,1)S(1)}, u32[]{:S(2)}, u32[]{:S(2)}) collective-permute-start(bf16[144,576]{1,0:T(8,128)(2,1)S(1)} %fusion.21), channel_id=1, source_target_pairs={{0,32},{32,0},{1,33},{33,1},{2,34},{34,2},{3,35},{35,3},{4,36},{36... | collective-permute-start | bytes 497672 | tf_op jit(solution)/shard_map/ppermute | solution.py:44
  184.0 5.4 %copy-start.3 = (bf16[144,576]{1,0:T(8,128)(2,1)S(1)}, bf16[144,576]{1,0:T(8,128)(2,1)}, u32[]{:S(2)}) copy-start(bf16[144,576]{1,0:T(8,128)(2,1)} %param.16) | copy-start | bytes 497668
  184.0 5.4 %copy-start.6 = (f32[144,576]{1,0:T(8,128)S(1)}, f32[144,576]{1,0:T(8,128)}, u32[]{:S(2)}) copy-start(f32[144,576]{1,0:T(8,128)} %param.18) | copy-start | bytes 995332
  184.0 5.4 %copy-start.7 = (f32[144,576]{1,0:T(8,128)S(1)}, f32[144,576]{1,0:T(8,128)}, u32[]{:S(2)}) copy-start(f32[144,576]{1,0:T(8,128)} %param.19) | copy-start | bytes 995332
Sparse Core Ops, SparseCore 0:
  19.5 51.6 all-gather.1
  98.5 56.9 reduce-scatter.1

commit v2 on v1

v2 whole, which is shorter than its diff:
```python
import functools
import math

import jax
import jax.numpy as jnp
from jax import lax
from jax.experimental import pallas as pl
from jax.experimental.pallas import tpu as pltpu
from jax.sharding import Mesh
from jax.sharding import PartitionSpec as P

drop_level = 6554
keep_scale = 65536.0 / (65536.0 - 6554.0)
gelu_coeff = math.sqrt(2.0 / math.pi)
first_fix = 1.0 - 0.9**10
second_fix = 1.0 - 0.95**10
bf16 = jnp.bfloat16
f32 = jnp.float32

plane = ("xh", "xl", "y")


def keep_mask(token_key, feature_key, drop_seed):
    mixed = (
        token_key[:, None] * -1640531535
        + feature_key[None, :] * -1028477379
        + drop_seed[0] * 668265263
    )
    mixed = mixed ^ mixed >> 15 & 131071
    mixed = mixed * -2048144789
    mixed = mixed ^ mixed >> 13 & 524287
    mixed = mixed * -1028477387
    mixed = mixed ^ mixed >> 16 & 65535
    level = mixed & 65535
    return level >= drop_level


def adamw(weight, first, second, grad):
    first_new = 0.9 * first + 0.1 * grad
    second_new = 0.95 * second + 0.05 * grad * grad
    wide = weight.astype(f32)
    step = first_new / first_fix / (jnp.sqrt(second_new / second_fix) + 1e-08) + 0.1 * wide
    return ((wide - 0.01 * step).astype(bf16), first_new, second_new)


def swap(x, axis):
    return lax.ppermute(x, axis, [(0, 1), (1, 0)])


def pick(index, first, second):
    return jnp.where(index == 0, first, second), jnp.where(index == 0, second, first)


def in_vmem(kernel, outs, name):
    def call(scalar, *arrays):
        return pl.pallas_call(
            kernel,
            out_shape=outs,
            in_specs=[pl.BlockSpec(memory_space=pltpu.SMEM)]
            + [pl.BlockSpec(memory_space=pltpu.VMEM)] * len(arrays),
            out_specs=[pl.BlockSpec(memory_space=pltpu.VMEM)] * len(outs),
            compiler_params=pltpu.CompilerParams(vmem_limit_bytes=24 * 1024 * 1024),
            name=name,
        )(scalar, *arrays)

    return call


def block_product(place_ref, step, depth, turned_ref, dboth_ref):
    size = turned_ref.shape[0] // depth
    spot = lax.rem(place_ref[0] + step % depth, depth)
    part = turned_ref[pl.ds(pl.multiple_of(spot * size, 16), size), :]
    return jnp.dot(part, dboth_ref[...], preferred_element_type=f32)


def forward_kernel(
    depth, place_ref, core_rows, other_rows, weights, kept, dboth, turned, forth, back
):
    half = kept.shape[1]
    tokens = core_rows.shape[0]
    both = []
    for j, rows in enumerate((core_rows, other_rows)):
        both.append(jnp.dot(rows[...], weights[...], preferred_element_type=f32))
        turned[:, pl.ds(j * tokens, tokens)] = rows[...].T
    for j in range(2):
        span = pl.ds(j * tokens, tokens)
        gate, up = both[j][:, :half], both[j][:, half:]
        tanh_part = jnp.tanh(gelu_coeff * (gate + 0.044715 * gate * gate * gate))
        act = 0.5 * gate * (1.0 + tanh_part)
        slope = 0.5 * (1.0 + tanh_part) + 0.5 * gate * (
            1.0 - tanh_part * tanh_part
        ) * gelu_coeff * (1.0 + 3.0 * 0.044715 * gate * gate)
        dropped = kept[span, :].astype(f32) * keep_scale
        dboth[span, :half] = (dropped * up * slope).astype(bf16)
        dboth[span, half:] = (dropped * act).astype(bf16)
    far = depth // 2
    forth[...] = block_product(place_ref, far, depth, turned, dboth).astype(bf16)
    back[...] = block_product(place_ref, far + 1, depth, turned, dboth).astype(bf16)


def hop_kernel(depth, step, place_ref, arrived, turned, dboth, total):
    term = block_product(place_ref, step, depth, turned, dboth)
    total[...] = (arrived[...].astype(f32) + term).astype(total.dtype)


def inputs_kernel(place_ref, dboth, weights, core_part, other_part):
    half = core_part.shape[0]
    over_units = (((1,), (1,)), ((), ()))
    other_part[...] = lax.dot_general(
        dboth[half:, :], weights[...], over_units, preferred_element_type=f32
    ).astype(bf16)
    core_part[...] = lax.dot_general(
        dboth[:half, :], weights[...], over_units, preferred_element_type=f32
    )


def on_device(
    inputs,
    hidden_grad,
    token_key,
    feature_key,
    drop_seed,
    gate_weight,
    up_weight,
    gate_first,
    gate_second,
    up_first,
    up_second,
):
    xh = lax.axis_index("xh")
    core = lax.axis_index("core")
    depth = lax.axis_size("z")
    own_rows, own_units = gate_weight.shape
    half = own_units // 2
    pair_rows = 2 * own_rows
    own_inputs, model = inputs.shape
    peers = lax.axis_size(plane)

    def along(x, step):
        return lax.ppermute(x, "z", [(i, (i + step) % depth) for i in range(depth)])

    def across(x, step):
        pairs = [
            (2 * i + j, 2 * ((i + step) % depth) + 1 - j) for i in range(depth) for j in range(2)
        ]
        return lax.ppermute(x, ("z", "xh"), pairs)

    low = jnp.concatenate([gate_weight[:, :half], up_weight[:, :half]], axis=1)
    high = jnp.concatenate([gate_weight[:, half:], up_weight[:, half:]], axis=1)
    mine, other = pick(xh, low, high)
    first_rows, second_rows = pick(xh, mine, swap(other, "xh"))
    weights = lax.all_gather(
        jnp.concatenate([first_rows, second_rows], axis=0), "z", axis=0, tiled=True
    )

    spread = jnp.broadcast_to(inputs[None], (peers,) + inputs.shape)
    core_rows = lax.all_to_all(spread, plane, split_axis=0, concat_axis=0).reshape(-1, model)

    keep = keep_mask(token_key, feature_key, drop_seed)
    masked = jnp.where(keep, hidden_grad, jnp.zeros_like(hidden_grad))
    mine_grad, other_grad = pick(xh, masked[:, :half], masked[:, half:])
    other_grad = swap(other_grad, "xh")
    lower, upper = pick(xh, mine_grad, other_grad)
    kept = jnp.concatenate([lower, upper], axis=0)
    kept = kept.reshape(-1, 2, own_inputs, half)
    kept = jnp.concatenate(pick(core, kept[:, 0], kept[:, 1]), axis=0).reshape(-1, half)

    core_rows, kept = lax.optimization_barrier((core_rows, kept))
    far = depth // 2
    tokens = kept.shape[0]
    place = lax.axis_index("z").reshape(1)
    block = (pair_rows, own_units)
    dboth, turned, forth, back = in_vmem(
        functools.partial(forward_kernel, depth),
        [
            jax.ShapeDtypeStruct(shape, bf16)
            for shape in ((tokens, own_units), (model, tokens), block, block)
        ],
        "forward",
    )(place, core_rows, swap(core_rows, "core"), weights, kept)

    def add_term(arrived, step, dtype=bf16):
        return in_vmem(
            functools.partial(hop_kernel, depth, step),
            [jax.ShapeDtypeStruct(block, dtype)],
            "add_term",
        )(place, arrived, turned, dboth)[0]

    core_part, other_part = in_vmem(
        inputs_kernel,
        [jax.ShapeDtypeStruct((tokens // 2, model), dtype) for dtype in (f32, bf16)],
        "inputs",
    )(place, dboth, weights)
    pair = (core_part + swap(other_part, "core").astype(f32)).astype(bf16)

    forth, back = along(forth, 1), along(back, -1)
    forth, back, pair = lax.optimization_barrier((forth, back, pair))
    shares = lax.all_to_all(
        pair.reshape(peers, own_inputs, model), plane, split_axis=0, concat_axis=0
    )
    input_grad = jnp.sum(shares.astype(f32), axis=0).astype(bf16)

    for step in range(far - 1, 1, -1):
        forth = along(add_term(forth, step), 1)
        back = along(add_term(back, 1 - step), -1)
    forth, back = add_term(forth, 1), add_term(back, 0, f32)
    own_forth, partner_forth = pick(xh, forth[:own_rows], forth[own_rows:])
    own_back, partner_back = pick(xh, back[:own_rows], back[own_rows:])
    partner_forth = across(partner_forth, 1)
    own_forth = along(own_forth, 1)
    partner_back = swap(partner_back.astype(bf16), "xh")
    input_grad, own_forth, partner_forth, partner_back = lax.optimization_barrier(
        (input_grad, own_forth, partner_forth, partner_back)
    )
    own_sum = own_forth.astype(f32) + own_back
    got_sum = partner_forth.astype(f32) + partner_back.astype(f32)

    low_sum, high_sum = pick(xh, own_sum, got_sum)
    grad_gate = jnp.concatenate([low_sum[:, :half], high_sum[:, :half]], axis=1)
    grad_up = jnp.concatenate([low_sum[:, half:], high_sum[:, half:]], axis=1)

    gate_updated, gate_first_new, gate_second_new = adamw(
        gate_weight, gate_first, gate_second, grad_gate
    )
    up_updated, up_first_new, up_second_new = adamw(up_weight, up_first, up_second, grad_up)
    return (
        input_grad,
        gate_updated,
        up_updated,
        gate_first_new,
        gate_second_new,
        up_first_new,
        up_second_new,
    )


def solution(mesh):
    dp_size, tensor_size = mesh.devices.shape
    fine = Mesh(
        mesh.devices.reshape(dp_size // 2, 2, 2, tensor_size // 4, 2), ("z", "xh", "xl", "y", "core")
    )
    dp, tensor = ("z", "xh"), ("xl", "y", "core")
    grid = P(dp, tensor)
    every = P(dp + tensor, None)
    return jax.shard_map(
        on_device,
        mesh=fine,
        in_specs=(every, grid, P(dp), P(tensor), P()) + (grid,) * 6,
        out_specs=(every,) + (grid,) * 6,
        check_vma=False,
    )
```

time: 198 us -> 165 us (0.83)
  the two profiles are of different devices: /device:TPU:2 before, /device:TPU:8 now
where the time goes in v2:
time: 165 us; the launch traced here: 164 us
  starting transfers between devices  66.4 us (40%)
  waiting for transfers between devices  55.5 us (34%)
  between operations  15.1 us (9%)
  local copies, waits for them, and re-layouts  11.9 us (7%)
  other arithmetic  7.83 us (5%)
  Pallas kernels  7.15 us (4%)
    ppermute x7, starting transfers between devices, along(): return lax.ppermute(x, 'z', [(i, (i + step) % depth) for i in range(depth)])  25.6 us
    ppermute x5, starting transfers between devices, swap(): return lax.ppermute(x, axis, [(0, 1), (1, 0)])  18.5 us
    ppermute x7, waiting for transfers between devices, along(): return lax.ppermute(x, 'z', [(i, (i + step) % depth) for i in range(depth)])  17.6 us
    all_to_all x1, waiting for transfers between devices, on_device(): lax.all_to_all(spread, plane, split_axis=0, concat_axis=0)  15.9 us
    ppermute x5, waiting for transfers between devices, swap(): return lax.ppermute(x, axis, [(0, 1), (1, 0)])  14.4 us
    all_to_all x1, starting transfers between devices, on_device(): lax.all_to_all(spread, plane, split_axis=0, concat_axis=0)  10.3 us
    unnamed x41, local copies, waits for them, and re-layouts  9.32 us
    all_to_all x1, starting transfers between devices, on_device(): lax.all_to_all(pair.reshape(peers, own_inputs, model), plane, split_axis=...  8.43 us
  transfers between devices with their start and end apart: 16, of which 12 were waited for; matrix products, arithmetic and copies ran while one was open for 3% of the time, Pallas kernels for 1%

profile of v2, /device:TPU:8, one launch (start us, length us, event | category | flops | bytes accessed | tf_op | source)
XLA Modules:
  0.0 163.9 jit_solution(3332518107859132571)
XLA Ops:
  7.2 1.2 fusion.17
  8.6 4.9 %collective-permute-start.2 = (bf16[144,576]{1,0:T(8,128)(2,1)S(1)}, bf16[144,576]{1,0:T(8,128)(2,1)S(1)}, u32[]{:S(2)}, u32[]{:S(2)}) collective-permute-start(bf16[144,576]{1,0:T(8,128)(2,1)S(1)} %broadcast_select_fusion.8), channel_id=1, source_target_pairs={{0,32},{32,0},{1,33},{33,1},{2,34},{34,2},{3,35},{35,3},{4,36},{36... | collective-permute-start | bytes 497672 | tf_op jit(solution)/shard_map/ppermute | solution.py:47
  13.5 4.8 %collective-permute-done.2 = bf16[144,576]{1,0:T(8,128)(2,1)S(1)} collective-permute-done((bf16[144,576]{1,0:T(8,128)(2,1)S(1)}, bf16[144,576]{1,0:T(8,128)(2,1)S(1)}, u32[]{:S(2)}, u32[]{:S(2)}) %collective-permute-start.2) | collective-permute-done | bytes 165920 | tf_op jit(solution)/shard_map/ppermute | solution.py:47
  18.5 0.8 pad_maximum_fusion.1
  19.3 1.1 broadcast_in_dim.4
  20.5 10.3 %all-to-all-start = ((bf16[32,8,2304]{2,1,0:T(8,128)(2,1)}), bf16[32,8,2304]{2,1,0:T(8,128)(2,1)S(1)}, u32[]{:S(2)}, u32[]{:S(2)}) async-start(bf16[32,8,2304]{2,1,0:T(8,128)(2,1)} %broadcast_in_dim.4), calls=%async_computation | async-start | bytes 2359296 | tf_op jit(solution)/shard_map/all_to_all | solution.py:157
  32.2 4.9 %collective-permute-start = (bf16[256,288]{1,0:T(8,128)(2,1)S(1)}, bf16[256,288]{1,0:T(8,128)(2,1)S(1)}, u32[]{:S(2)}, u32[]{:S(2)}) collective-permute-start(bf16[256,288]{1,0:T(8,128)(2,1)S(1)} %broadcast_select_fusion.2), channel_id=1, source_target_pairs={{0,32},{32,0},{1,33},{33,1},{2,34},{34,2},{3,35},{35,3},{4,36},{36... | collective-permute-start | bytes 442376 | tf_op jit(solution)/shard_map/ppermute | solution.py:47
  37.1 7.8 %collective-permute-done = bf16[256,288]{1,0:T(8,128)(2,1)S(1)} collective-permute-done((bf16[256,288]{1,0:T(8,128)(2,1)S(1)}, bf16[256,288]{1,0:T(8,128)(2,1)S(1)}, u32[]{:S(2)}, u32[]{:S(2)}) %collective-permute-start) | collective-permute-done | bytes 147488 | tf_op jit(solution)/shard_map/ppermute | solution.py:47
  45.2 15.9 %all-to-all-done = bf16[32,8,2304]{2,1,0:T(8,128)(2,1)S(1)} async-done(((bf16[32,8,2304]{2,1,0:T(8,128)(2,1)}), bf16[32,8,2304]{2,1,0:T(8,128)(2,1)S(1)}, u32[]{:S(2)}, u32[]{:S(2)}) %all-to-all-start) | async-done | bytes 1179680 | tf_op jit(solution)/shard_map/all_to_all | solution.py:157
  61.1 1.9 %collective-permute-start.1 = (bf16[256,2304]{1,0:T(8,128)(2,1)S(1)}, bf16[256,2304]{1,0:T(8,128)(2,1)S(1)}, u32[]{:S(2)}, u32[]{:S(2)}) collective-permute-start(bf16[256,2304]{1,0:T(8,128)(2,1)S(1)} %bitcast.23), channel_id=1, source_target_pairs={{0,1},{1,0},{2,3},{3,2},{4,5},{5,4},{6,7},{7,6},{8,9},{9,8},{10,11... | collective-permute-start | bytes 3538952 | tf_op jit(solution)/shard_map/ppermute | solution.py:47
  63.0 1.0 copy-done.2
  64.0 1.8 %collective-permute-done.1.other_rows = bf16[256,2304]{1,0:T(8,128)(2,1)S(1)} collective-permute-done((bf16[256,2304]{1,0:T(8,128)(2,1)S(1)}, bf16[256,2304]{1,0:T(8,128)(2,1)S(1)}, u32[]{:S(2)}, u32[]{:S(2)}) %collective-permute-start.1) | collective-permute-done | bytes 1179680 | tf_op jit(solution)/shard_map/ppermute | solution.py:47
  65.8 1.1 copy-done.6
  66.9 4.2 %all-gather.2.cloned.1.call-done.weights = bf16[2304,576]{1,0:T(8,128)(2,1)} async-done(((bf16[288,576]{1,0:T(8,128)(2,1)}), bf16[2304,576]{1,0:T(8,128)(2,1)}) %all-gather.2.cloned.1.call-update) | async-done | bytes 2654224 | tf_op jit(solution)/shard_map/all_gather | solution.py:152
  71.1 1.8 %copy-done = bf16[2304,576]{1,0:T(8,128)(2,1)S(1)} copy-done((bf16[2304,576]{1,0:T(8,128)(2,1)S(1)}, bf16[2304,576]{1,0:T(8,128)(2,1)}, u32[]{:S(2)}) %copy-start) | copy-done | bytes 2654232
  72.9 1.3 copy-done.3
  74.2 1.3 copy-done.7
  75.5 2.7 %forward.1 = (bf16[512,576]{1,0:T(8,128)(2,1)S(1)}, bf16[2304,512]{1,0:T(8,128)(2,1)S(1)}, bf16[288,576]{1,0:T(8,128)(2,1)S(1)}, bf16[288,576]{1,0:T(8,128)(2,1)S(1)}) custom-call(s32[1]{0:T(128)} %bitcast.place_ref, bf16[256,2304]{1,0:T(8,128)(2,1)S(1)} %bitcast.24, bf16[256,2304]{1,0:T(8,128)(2,1)S(1)} %copy-done.7, bf16[2304,576]{1,0:T(8,128)(2,1)S(1)} %copy-done, ...), custom_call_target="tpu_custom_call" | custom-call | tf_op jit(solution)/shard_map/forward/pallas_call | solution.py:56
  78.2 2.0 %inputs.1 = (f32[256,2304]{1,0:T(8,128)S(1)}, bf16[256,2304]{1,0:T(8,128)(2,1)S(1)}) custom-call(s32[1]{0:T(128)} %bitcast.place_ref, bf16[512,576]{1,0:T(8,128)(2,1)S(1)} %get-tuple-element.26.dboth, bf16[2304,576]{1,0:T(8,128)(2,1)S(1)} %copy-done.1), custom_call_target="tpu_custom_call" | custom-call | tf_op jit(solution)/shard_map/inputs/pallas_call | solution.py:56
  80.3 1.9 %collective-permute-start.5 = (bf16[256,2304]{1,0:T(8,128)(2,1)S(1)}, bf16[256,2304]{1,0:T(8,128)(2,1)S(1)}, u32[]{:S(2)}, u32[]{:S(2)}) collective-permute-start(bf16[256,2304]{1,0:T(8,128)(2,1)S(1)} %get-tuple-element.28), channel_id=1, source_target_pairs={{0,1},{1,0},{2,3},{3,2},{4,5},{5,4},{6,7},{7,6},{8,9},{9,8},{10,11... | collective-permute-start | bytes 3538952 | tf_op jit(solution)/shard_map/ppermute | solution.py:47
  82.2 3.1 %collective-permute-start.3 = (bf16[288,576]{1,0:T(8,128)(2,1)S(1)}, bf16[288,576]{1,0:T(8,128)(2,1)S(1)}, u32[]{:S(2)}, u32[]{:S(2)}) collective-permute-start(bf16[288,576]{1,0:T(8,128)(2,1)S(1)} %get-tuple-element.24), channel_id=1, source_target_pairs={{0,64},{64,128},{128,192},{192,256},{256,320},{320,384},{384,448},... | collective-permute-start | bytes 995336 | tf_op jit(solution)/shard_map/ppermute | solution.py:140
  85.3 5.7 %collective-permute-start.4 = (bf16[288,576]{1,0:T(8,128)(2,1)S(1)}, bf16[288,576]{1,0:T(8,128)(2,1)S(1)}, u32[]{:S(2)}, u32[]{:S(2)}) collective-permute-start(bf16[288,576]{1,0:T(8,128)(2,1)S(1)} %get-tuple-element.25), channel_id=1, source_target_pairs={{0,448},{64,0},{128,64},{192,128},{256,192},{320,256},{384,320},{4... | collective-permute-start | bytes 995336 | tf_op jit(solution)/shard_map/ppermute | solution.py:140
  91.0 1.2 add_convert_fusion
  92.3 5.9 %collective-permute-done.3.arrived = bf16[288,576]{1,0:T(8,128)(2,1)S(1)} collective-permute-done((bf16[288,576]{1,0:T(8,128)(2,1)S(1)}, bf16[288,576]{1,0:T(8,128)(2,1)S(1)}, u32[]{:S(2)}, u32[]{:S(2)}) %collective-permute-start.3) | collective-permute-done | bytes 331808 | tf_op jit(solution)/shard_map/ppermute | solution.py:140
  98.2 1.2 collective-permute-done.4.arrived
  99.4 0.7 copy-done.8
  100.1 8.4 %all-to-all-start.1 = ((bf16[32,8,2304]{2,1,0:T(8,128)(2,1)}), bf16[32,8,2304]{2,1,0:T(8,128)(2,1)}, u32[]{:S(2)}, u32[]{:S(2)}) async-start(bf16[32,8,2304]{2,1,0:T(8,128)(2,1)} %bitcast.25), calls=%async_computation.1 | async-start | bytes 2359296 | tf_op jit(solution)/shard_map/all_to_all | solution.py:198
  108.5 1.0 copy-done.9
  109.5 0.4 add_term.9
  109.9 5.2 %collective-permute-start.10 = (bf16[288,576]{1,0:T(8,128)(2,1)S(1)}, bf16[288,576]{1,0:T(8,128)(2,1)S(1)}, u32[]{:S(2)}, u32[]{:S(2)}) collective-permute-start(bf16[288,576]{1,0:T(8,128)(2,1)S(1)} %add_term.9), channel_id=1, source_target_pairs={{0,448},{64,0},{128,64},{192,128},{256,192},{320,256},{384,320},{4... | collective-permute-start | bytes 995336 | tf_op jit(solution)/shard_map/ppermute | solution.py:140
  115.1 0.4 add_term.6
  115.5 1.9 %collective-permute-start.6 = (bf16[288,576]{1,0:T(8,128)(2,1)S(1)}, bf16[288,576]{1,0:T(8,128)(2,1)S(1)}, u32[]{:S(2)}, u32[]{:S(2)}) collective-permute-start(bf16[288,576]{1,0:T(8,128)(2,1)S(1)} %add_term.6), channel_id=1, source_target_pairs={{0,64},{64,128},{128,192},{192,256},{256,320},{320,384},{384,448},... | collective-permute-start | bytes 995336 | tf_op jit(solution)/shard_map/ppermute | solution.py:140
  117.4 4.5 %collective-permute-done.10.arrived = bf16[288,576]{1,0:T(8,128)(2,1)S(1)} collective-permute-done((bf16[288,576]{1,0:T(8,128)(2,1)S(1)}, bf16[288,576]{1,0:T(8,128)(2,1)S(1)}, u32[]{:S(2)}, u32[]{:S(2)}) %collective-permute-start.10) | collective-permute-done | bytes 331808 | tf_op jit(solution)/shard_map/ppermute | solution.py:140
  121.9 0.4 add_term.10
  122.3 5.6 %collective-permute-start.11 = (bf16[288,576]{1,0:T(8,128)(2,1)S(1)}, bf16[288,576]{1,0:T(8,128)(2,1)S(1)}, u32[]{:S(2)}, u32[]{:S(2)}) collective-permute-start(bf16[288,576]{1,0:T(8,128)(2,1)S(1)} %add_term.10), channel_id=1, source_target_pairs={{0,448},{64,0},{128,64},{192,128},{256,192},{320,256},{384,320},{4... | collective-permute-start | bytes 995336 | tf_op jit(solution)/shard_map/ppermute | solution.py:140
  127.9 0.4 add_term.7
  128.3 1.9 %collective-permute-start.7 = (bf16[288,576]{1,0:T(8,128)(2,1)S(1)}, bf16[288,576]{1,0:T(8,128)(2,1)S(1)}, u32[]{:S(2)}, u32[]{:S(2)}) collective-permute-start(bf16[288,576]{1,0:T(8,128)(2,1)S(1)} %add_term.7), channel_id=1, source_target_pairs={{0,64},{64,128},{128,192},{192,256},{256,320},{320,384},{384,448},... | collective-permute-start | bytes 995336 | tf_op jit(solution)/shard_map/ppermute | solution.py:140
  130.3 3.7 %collective-permute-done.11.arrived = bf16[288,576]{1,0:T(8,128)(2,1)S(1)} collective-permute-done((bf16[288,576]{1,0:T(8,128)(2,1)S(1)}, bf16[288,576]{1,0:T(8,128)(2,1)S(1)}, u32[]{:S(2)}, u32[]{:S(2)}) %collective-permute-start.11) | collective-permute-done | bytes 331808 | tf_op jit(solution)/shard_map/ppermute | solution.py:140
  134.4 4.9 %collective-permute-start.12 = (bf16[144,576]{1,0:T(8,128)(2,1)S(1)}, bf16[144,576]{1,0:T(8,128)(2,1)S(1)}, u32[]{:S(2)}, u32[]{:S(2)}) collective-permute-start(bf16[144,576]{1,0:T(8,128)(2,1)S(1)} %select_convert_fusion), channel_id=1, source_target_pairs={{0,32},{32,0},{1,33},{33,1},{2,34},{34,2},{3,35},{35,3},{4,36},{36... | collective-permute-start | bytes 497672 | tf_op jit(solution)/shard_map/ppermute | solution.py:47
  139.7 0.4 add_term.8
  140.2 3.5 %collective-permute-start.9 = (bf16[144,576]{1,0:T(8,128)(2,1)S(1)}, bf16[144,576]{1,0:T(8,128)(2,1)S(1)}, u32[]{:S(2)}, u32[]{:S(2)}) collective-permute-start(bf16[144,576]{1,0:T(8,128)(2,1)S(1)} %get-tuple-element.53), channel_id=1, source_target_pairs={{0,96},{32,64},{64,160},{96,128},{128,224},{160,192},{192,288},{22... | collective-permute-start | bytes 497672 | tf_op jit(solution)/shard_map/ppermute | solution.py:146
  143.7 2.2 %collective-permute-start.8 = (bf16[144,576]{1,0:T(8,128)(2,1)S(1)}, bf16[144,576]{1,0:T(8,128)(2,1)S(1)}, u32[]{:S(2)}, u32[]{:S(2)}) collective-permute-start(bf16[144,576]{1,0:T(8,128)(2,1)S(1)} %get-tuple-element.54), channel_id=1, source_target_pairs={{0,64},{64,128},{128,192},{192,256},{256,320},{320,384},{384,448},... | collective-permute-start | bytes 497672 | tf_op jit(solution)/shard_map/ppermute | solution.py:140
  145.9 2.1 %reduce_sum.12 = bf16[8,2304]{1,0:T(8,128)(2,1)} reduce(bf16[32,8,2304]{2,1,0:T(8,128)(2,1)} %all-to-all-done.1, bf16[]{:T(256)} %constant.56.clone.1), dimensions={0}, to_apply=%region_0.1 | reduce | flops 571392 | bytes 1216514 | tf_op jit(solution)/shard_map/reduce_sum | solution.py:201
  147.9 3.4 %collective-permute-done.9 = bf16[144,576]{1,0:T(8,128)(2,1)S(1)} collective-permute-done((bf16[144,576]{1,0:T(8,128)(2,1)S(1)}, bf16[144,576]{1,0:T(8,128)(2,1)S(1)}, u32[]{:S(2)}, u32[]{:S(2)}) %collective-permute-start.9) | collective-permute-done | bytes 165920 | tf_op jit(solution)/shard_map/ppermute | solution.py:146
  151.3 2.0 %collective-permute-done.8 = bf16[144,576]{1,0:T(8,128)(2,1)S(1)} collective-permute-done((bf16[144,576]{1,0:T(8,128)(2,1)S(1)}, bf16[144,576]{1,0:T(8,128)(2,1)S(1)}, u32[]{:S(2)}, u32[]{:S(2)}) %collective-permute-start.8) | collective-permute-done | bytes 165920 | tf_op jit(solution)/shard_map/ppermute | solution.py:140
  153.8 0.6 copy-done.10
  154.6 1.2 fusion.6
  155.8 1.2 fusion.3
  (57 shorter events, 3.0 us)
Async XLA Ops:
  7.2 63.9 %all-gather.2.cloned.1.call-start = ((), (), s32[]{:S(2)}) async-start(), calls=%async_computation.2 | async-start | bytes 3317760 | tf_op jit(solution)/shard_map/all_gather | solution.py:152
  8.6 10.8 %copy-start.17 = (bf16[8,2304]{1,0:T(8,128)(2,1)S(1)}, bf16[8,2304]{1,0:T(8,128)(2,1)}, u32[]{:S(2)}) copy-start(bf16[8,2304]{1,0:T(8,128)(2,1)} %param.11) | copy-start | bytes 110596
  8.6 9.8 %collective-permute-start.2 = (bf16[144,576]{1,0:T(8,128)(2,1)S(1)}, bf16[144,576]{1,0:T(8,128)(2,1)S(1)}, u32[]{:S(2)}, u32[]{:S(2)}) collective-permute-start(bf16[144,576]{1,0:T(8,128)(2,1)S(1)} %broadcast_select_fusion.8), channel_id=1, source_target_pairs={{0,32},{32,0},{1,33},{33,1},{2,34},{34,2},{3,35},{35,3},{4,36},{36... | collective-permute-start | bytes 497672 | tf_op jit(solution)/shard_map/ppermute | solution.py:47
  20.5 11.0 %copy-start.16 = (bf16[256,576]{0,1:T(8,128)(2,1)S(1)}, bf16[256,576]{0,1:T(8,128)(2,1)}, u32[]{:S(2)}) copy-start(bf16[256,576]{0,1:T(8,128)(2,1)} %param.12) | copy-start | bytes 884740
  20.5 11.2 %copy-start.19 = (s32[256]{0:T(256)S(1)}, s32[256]{0:T(256)}, u32[]{:S(2)}) copy-start(s32[256]{0:T(256)} %param.13) | copy-start | bytes 3076
  20.5 11.2 %copy-start.18 = (s32[576]{0:T(1024)S(1)}, s32[576]{0:T(1024)}, u32[]{:S(2)}) copy-start(s32[576]{0:T(1024)} %param.14) | copy-start | bytes 6916
  20.5 40.6 %all-to-all-start = ((bf16[32,8,2304]{2,1,0:T(8,128)(2,1)}), bf16[32,8,2304]{2,1,0:T(8,128)(2,1)S(1)}, u32[]{:S(2)}, u32[]{:S(2)}) async-start(bf16[32,8,2304]{2,1,0:T(8,128)(2,1)} %broadcast_in_dim.4), calls=%async_computation | async-start | bytes 2359296 | tf_op jit(solution)/shard_map/all_to_all | solution.py:157
  32.2 12.7 %collective-permute-start = (bf16[256,288]{1,0:T(8,128)(2,1)S(1)}, bf16[256,288]{1,0:T(8,128)(2,1)S(1)}, u32[]{:S(2)}, u32[]{:S(2)}) collective-permute-start(bf16[256,288]{1,0:T(8,128)(2,1)S(1)} %broadcast_select_fusion.2), channel_id=1, source_target_pairs={{0,32},{32,0},{1,33},{33,1},{2,34},{34,2},{3,35},{35,3},{4,36},{36... | collective-permute-start | bytes 442376 | tf_op jit(solution)/shard_map/ppermute | solution.py:47
  61.1 4.7 %collective-permute-start.1 = (bf16[256,2304]{1,0:T(8,128)(2,1)S(1)}, bf16[256,2304]{1,0:T(8,128)(2,1)S(1)}, u32[]{:S(2)}, u32[]{:S(2)}) collective-permute-start(bf16[256,2304]{1,0:T(8,128)(2,1)S(1)} %bitcast.23), channel_id=1, source_target_pairs={{0,1},{1,0},{2,3},{3,2},{4,5},{5,4},{6,7},{7,6},{8,9},{9,8},{10,11... | collective-permute-start | bytes 3538952 | tf_op jit(solution)/shard_map/ppermute | solution.py:47
  63.0 1.0 copy-start.2
  65.8 1.1 copy-start.6
  71.1 1.8 %copy-start = (bf16[2304,576]{1,0:T(8,128)(2,1)S(1)}, bf16[2304,576]{1,0:T(8,128)(2,1)}, u32[]{:S(2)}) copy-start(bf16[2304,576]{1,0:T(8,128)(2,1)} %all-gather.2.cloned.1.call-done.weights) | copy-start | bytes 7962628
  72.9 1.3 copy-start.3
  74.2 1.3 copy-start.7
  75.5 2.8 %copy-start.1 = (bf16[2304,576]{1,0:T(8,128)(2,1)S(1)}, bf16[2304,576]{1,0:T(8,128)(2,1)}, u32[]{:S(2)}) copy-start(bf16[2304,576]{1,0:T(8,128)(2,1)} %all-gather.2.cloned.1.call-done.weights) | copy-start | bytes 7962628
  80.3 10.8 %collective-permute-start.5 = (bf16[256,2304]{1,0:T(8,128)(2,1)S(1)}, bf16[256,2304]{1,0:T(8,128)(2,1)S(1)}, u32[]{:S(2)}, u32[]{:S(2)}) collective-permute-start(bf16[256,2304]{1,0:T(8,128)(2,1)S(1)} %get-tuple-element.28), channel_id=1, source_target_pairs={{0,1},{1,0},{2,3},{3,2},{4,5},{5,4},{6,7},{7,6},{8,9},{9,8},{10,11... | collective-permute-start | bytes 3538952 | tf_op jit(solution)/shard_map/ppermute | solution.py:47
  82.2 16.0 %collective-permute-start.3 = (bf16[288,576]{1,0:T(8,128)(2,1)S(1)}, bf16[288,576]{1,0:T(8,128)(2,1)S(1)}, u32[]{:S(2)}, u32[]{:S(2)}) collective-permute-start(bf16[288,576]{1,0:T(8,128)(2,1)S(1)} %get-tuple-element.24), channel_id=1, source_target_pairs={{0,64},{64,128},{128,192},{192,256},{256,320},{320,384},{384,448},... | collective-permute-start | bytes 995336 | tf_op jit(solution)/shard_map/ppermute | solution.py:140
  85.3 14.1 %collective-permute-start.4 = (bf16[288,576]{1,0:T(8,128)(2,1)S(1)}, bf16[288,576]{1,0:T(8,128)(2,1)S(1)}, u32[]{:S(2)}, u32[]{:S(2)}) collective-permute-start(bf16[288,576]{1,0:T(8,128)(2,1)S(1)} %get-tuple-element.25), channel_id=1, source_target_pairs={{0,448},{64,0},{128,64},{192,128},{256,192},{320,256},{384,320},{4... | collective-permute-start | bytes 995336 | tf_op jit(solution)/shard_map/ppermute | solution.py:140
  99.4 0.7 copy-start.8
  100.1 45.8 %all-to-all-start.1 = ((bf16[32,8,2304]{2,1,0:T(8,128)(2,1)}), bf16[32,8,2304]{2,1,0:T(8,128)(2,1)}, u32[]{:S(2)}, u32[]{:S(2)}) async-start(bf16[32,8,2304]{2,1,0:T(8,128)(2,1)} %bitcast.25), calls=%async_computation.1 | async-start | bytes 2359296 | tf_op jit(solution)/shard_map/all_to_all | solution.py:198
  108.5 1.0 copy-start.9
  109.9 12.0 %collective-permute-start.10 = (bf16[288,576]{1,0:T(8,128)(2,1)S(1)}, bf16[288,576]{1,0:T(8,128)(2,1)S(1)}, u32[]{:S(2)}, u32[]{:S(2)}) collective-permute-start(bf16[288,576]{1,0:T(8,128)(2,1)S(1)} %add_term.9), channel_id=1, source_target_pairs={{0,448},{64,0},{128,64},{192,128},{256,192},{320,256},{384,320},{4... | collective-permute-start | bytes 995336 | tf_op jit(solution)/shard_map/ppermute | solution.py:140
  115.5 12.4 %collective-permute-start.6 = (bf16[288,576]{1,0:T(8,128)(2,1)S(1)}, bf16[288,576]{1,0:T(8,128)(2,1)S(1)}, u32[]{:S(2)}, u32[]{:S(2)}) collective-permute-start(bf16[288,576]{1,0:T(8,128)(2,1)S(1)} %add_term.6), channel_id=1, source_target_pairs={{0,64},{64,128},{128,192},{192,256},{256,320},{320,384},{384,448},... | collective-permute-start | bytes 995336 | tf_op jit(solution)/shard_map/ppermute | solution.py:140
  122.3 11.6 %collective-permute-start.11 = (bf16[288,576]{1,0:T(8,128)(2,1)S(1)}, bf16[288,576]{1,0:T(8,128)(2,1)S(1)}, u32[]{:S(2)}, u32[]{:S(2)}) collective-permute-start(bf16[288,576]{1,0:T(8,128)(2,1)S(1)} %add_term.10), channel_id=1, source_target_pairs={{0,448},{64,0},{128,64},{192,128},{256,192},{320,256},{384,320},{4... | collective-permute-start | bytes 995336 | tf_op jit(solution)/shard_map/ppermute | solution.py:140
  128.3 11.3 %collective-permute-start.7 = (bf16[288,576]{1,0:T(8,128)(2,1)S(1)}, bf16[288,576]{1,0:T(8,128)(2,1)S(1)}, u32[]{:S(2)}, u32[]{:S(2)}) collective-permute-start(bf16[288,576]{1,0:T(8,128)(2,1)S(1)} %add_term.7), channel_id=1, source_target_pairs={{0,64},{64,128},{128,192},{192,256},{256,320},{320,384},{384,448},... | collective-permute-start | bytes 995336 | tf_op jit(solution)/shard_map/ppermute | solution.py:140
  134.3 5.7 %copy-start.4 = (f32[288,576]{1,0:T(8,128)}, f32[288,576]{1,0:T(8,128)S(1)}, u32[]{:S(2)}) copy-start(f32[288,576]{1,0:T(8,128)S(1)} %add_term.11) | copy-start | bytes 1990660
  134.4 13.5 %collective-permute-start.12 = (bf16[144,576]{1,0:T(8,128)(2,1)S(1)}, bf16[144,576]{1,0:T(8,128)(2,1)S(1)}, u32[]{:S(2)}, u32[]{:S(2)}) collective-permute-start(bf16[144,576]{1,0:T(8,128)(2,1)S(1)} %select_convert_fusion), channel_id=1, source_target_pairs={{0,32},{32,0},{1,33},{33,1},{2,34},{34,2},{3,35},{35,3},{4,36},{36... | collective-permute-start | bytes 497672 | tf_op jit(solution)/shard_map/ppermute | solution.py:47
  140.1 13.2 %copy-start.5 = (f32[288,576]{1,0:T(8,128)S(1)}, f32[288,576]{1,0:T(8,128)}, u32[]{:S(2)}) copy-start(f32[288,576]{1,0:T(8,128)} %copy-done.4) | copy-start | bytes 1990660
  140.2 11.2 %collective-permute-start.9 = (bf16[144,576]{1,0:T(8,128)(2,1)S(1)}, bf16[144,576]{1,0:T(8,128)(2,1)S(1)}, u32[]{:S(2)}, u32[]{:S(2)}) collective-permute-start(bf16[144,576]{1,0:T(8,128)(2,1)S(1)} %get-tuple-element.53), channel_id=1, source_target_pairs={{0,96},{32,64},{64,160},{96,128},{128,224},{160,192},{192,288},{22... | collective-permute-start | bytes 497672 | tf_op jit(solution)/shard_map/ppermute | solution.py:146
  143.7 9.6 %collective-permute-start.8 = (bf16[144,576]{1,0:T(8,128)(2,1)S(1)}, bf16[144,576]{1,0:T(8,128)(2,1)S(1)}, u32[]{:S(2)}, u32[]{:S(2)}) collective-permute-start(bf16[144,576]{1,0:T(8,128)(2,1)S(1)} %get-tuple-element.54), channel_id=1, source_target_pairs={{0,64},{64,128},{128,192},{192,256},{256,320},{320,384},{384,448},... | collective-permute-start | bytes 497672 | tf_op jit(solution)/shard_map/ppermute | solution.py:140
  153.4 0.9 copy-start.10
  153.4 1.1 copy-start.12
  153.5 1.2 copy-start.13
  153.7 2.1 %copy-start.11 = (bf16[144,576]{1,0:T(8,128)(2,1)S(1)}, bf16[144,576]{1,0:T(8,128)(2,1)}, u32[]{:S(2)}) copy-start(bf16[144,576]{1,0:T(8,128)(2,1)} %param.16) | copy-start | bytes 497668
  153.7 2.1 %copy-start.14 = (f32[144,576]{1,0:T(8,128)S(1)}, f32[144,576]{1,0:T(8,128)}, u32[]{:S(2)}) copy-start(f32[144,576]{1,0:T(8,128)} %param.18) | copy-start | bytes 995332
  153.7 2.1 %copy-start.15 = (f32[144,576]{1,0:T(8,128)S(1)}, f32[144,576]{1,0:T(8,128)}, u32[]{:S(2)}) copy-start(f32[144,576]{1,0:T(8,128)} %param.19) | copy-start | bytes 995332
Sparse Core Ops, SparseCore 0:
  19.5 51.5 all-gather.1

commit v3 on v2

--- a/solution.py
+++ b/solution.py
@@ -66,22 +66,32 @@
     return call
 
 
-def block_product(place_ref, step, depth, turned_ref, dboth_ref):
+def block_product(place_ref, step, depth, turned_ref, turned_other_ref, dboth_ref):
     size = turned_ref.shape[0] // depth
-    spot = lax.rem(place_ref[0] + step % depth, depth)
-    part = turned_ref[pl.ds(pl.multiple_of(spot * size, 16), size), :]
-    return jnp.dot(part, dboth_ref[...], preferred_element_type=f32)
+    place, core = place_ref[0] >> 1, place_ref[0] & 1
+    spot = lax.rem(place + (1 - 2 * core) * step + depth, depth)
+    span = pl.ds(pl.multiple_of(spot * size, 16), size)
+    tokens = turned_ref.shape[1]
+    return jnp.dot(turned_ref[span, :], dboth_ref[:tokens, :], preferred_element_type=f32) + jnp.dot(
+        turned_other_ref[span, :], dboth_ref[tokens:, :], preferred_element_type=f32
+    )
+
+
+def turn_kernel(place_ref, rows, turned):
+    turned[...] = rows[...].T
 
 
 def forward_kernel(
-    depth, place_ref, core_rows, other_rows, weights, kept, dboth, turned, forth, back
+    depth, place_ref, turned, turned_other, weights, kept, dboth, forth, back, middle
 ):
     half = kept.shape[1]
-    tokens = core_rows.shape[0]
-    both = []
-    for j, rows in enumerate((core_rows, other_rows)):
-        both.append(jnp.dot(rows[...], weights[...], preferred_element_type=f32))
-        turned[:, pl.ds(j * tokens, tokens)] = rows[...].T
+    tokens = turned.shape[1]
+    both = [
+        lax.dot_general(
+            part[...], weights[...], (((0,), (0,)), ((), ())), preferred_element_type=f32
+        )
+        for part in (turned, turned_other)
+    ]
     for j in range(2):
         span = pl.ds(j * tokens, tokens)
         gate, up = both[j][:, :half], both[j][:, half:]
@@ -94,12 +104,13 @@
         dboth[span, :half] = (dropped * up * slope).astype(bf16)
         dboth[span, half:] = (dropped * act).astype(bf16)
     far = depth // 2
-    forth[...] = block_product(place_ref, far, depth, turned, dboth).astype(bf16)
-    back[...] = block_product(place_ref, far + 1, depth, turned, dboth).astype(bf16)
-
-
-def hop_kernel(depth, step, place_ref, arrived, turned, dboth, total):
-    term = block_product(place_ref, step, depth, turned, dboth)
+    for out, step in ((forth, far), (back, 1 - far), (middle, 0)):
+        term = block_product(place_ref, step, depth, turned, turned_other, dboth)
+        out[...] = term.astype(out.dtype)
+
+
+def hop_kernel(depth, step, place_ref, arrived, turned, turned_other, dboth, total):
+    term = block_product(place_ref, step, depth, turned, turned_other, dboth)
     total[...] = (arrived[...].astype(f32) + term).astype(total.dtype)
 
 
@@ -136,14 +147,20 @@
     own_inputs, model = inputs.shape
     peers = lax.axis_size(plane)
 
+    def ring(x, step, turn):
+        pairs = [
+            ((i * 2 + j) * 2 + k, ((i + step * (1 - 2 * k)) % depth * 2 + (j ^ turn)) * 2 + k)
+            for i in range(depth)
+            for j in range(2)
+            for k in range(2)
+        ]
+        return lax.ppermute(x, ("z", "xh", "core"), pairs)
+
     def along(x, step):
-        return lax.ppermute(x, "z", [(i, (i + step) % depth) for i in range(depth)])
+        return ring(x, step, 0)
 
     def across(x, step):
-        pairs = [
-            (2 * i + j, 2 * ((i + step) % depth) + 1 - j) for i in range(depth) for j in range(2)
-        ]
-        return lax.ppermute(x, ("z", "xh"), pairs)
+        return ring(x, step, 1)
 
     low = jnp.concatenate([gate_weight[:, :half], up_weight[:, :half]], axis=1)
     high = jnp.concatenate([gate_weight[:, half:], up_weight[:, half:]], axis=1)
@@ -168,23 +185,24 @@
     core_rows, kept = lax.optimization_barrier((core_rows, kept))
     far = depth // 2
     tokens = kept.shape[0]
-    place = lax.axis_index("z").reshape(1)
+    place = (2 * lax.axis_index("z") + core).reshape(1)
     block = (pair_rows, own_units)
-    dboth, turned, forth, back = in_vmem(
+    turn = in_vmem(turn_kernel, [jax.ShapeDtypeStruct((model, tokens // 2), bf16)], "turn")
+    turned = turn(place, core_rows)[0]
+    turned_other = turn(place, swap(core_rows, "core"))[0]
+    dboth, forth, back, middle = in_vmem(
         functools.partial(forward_kernel, depth),
-        [
-            jax.ShapeDtypeStruct(shape, bf16)
-            for shape in ((tokens, own_units), (model, tokens), block, block)
-        ],
+        [jax.ShapeDtypeStruct(shape, bf16) for shape in ((tokens, own_units), block, block)]
+        + [jax.ShapeDtypeStruct(block, f32)],
         "forward",
-    )(place, core_rows, swap(core_rows, "core"), weights, kept)
-
-    def add_term(arrived, step, dtype=bf16):
+    )(place, turned, turned_other, weights, kept)
+
+    def add_term(arrived, step):
         return in_vmem(
             functools.partial(hop_kernel, depth, step),
-            [jax.ShapeDtypeStruct(block, dtype)],
+            [jax.ShapeDtypeStruct(block, bf16)],
             "add_term",
-        )(place, arrived, turned, dboth)[0]
+        )(place, arrived, turned, turned_other, dboth)[0]
 
     core_part, other_part = in_vmem(
         inputs_kernel,
@@ -194,26 +212,27 @@
     pair = (core_part + swap(other_part, "core").astype(f32)).astype(bf16)
 
     forth, back = along(forth, 1), along(back, -1)
-    forth, back, pair = lax.optimization_barrier((forth, back, pair))
+    own_sum, partner_sum = pick(xh, middle[:own_rows], middle[own_rows:])
+    got_sum = swap(partner_sum.astype(bf16), "xh")
+    forth, back, pair, got_sum = lax.optimization_barrier((forth, back, pair, got_sum))
     shares = lax.all_to_all(
         pair.reshape(peers, own_inputs, model), plane, split_axis=0, concat_axis=0
     )
     input_grad = jnp.sum(shares.astype(f32), axis=0).astype(bf16)
 
+    def last(message, step):
+        own, partner = pick(xh, message[:own_rows], message[own_rows:])
+        return along(own, step), across(partner, step)
+
     for step in range(far - 1, 1, -1):
         forth = along(add_term(forth, step), 1)
-        back = along(add_term(back, 1 - step), -1)
-    forth, back = add_term(forth, 1), add_term(back, 0, f32)
-    own_forth, partner_forth = pick(xh, forth[:own_rows], forth[own_rows:])
-    own_back, partner_back = pick(xh, back[:own_rows], back[own_rows:])
-    partner_forth = across(partner_forth, 1)
-    own_forth = along(own_forth, 1)
-    partner_back = swap(partner_back.astype(bf16), "xh")
-    input_grad, own_forth, partner_forth, partner_back = lax.optimization_barrier(
-        (input_grad, own_forth, partner_forth, partner_back)
-    )
-    own_sum = own_forth.astype(f32) + own_back
-    got_sum = partner_forth.astype(f32) + partner_back.astype(f32)
+        back = add_term(back, 1 - step)
+        back = along(back, -1) if step > 2 else last(back, -1)
+    forth = last(add_term(forth, 1), 1)
+    input_grad, *arrived = lax.optimization_barrier((input_grad, *forth, *back))
+    own_forth, partner_forth, own_back, partner_back = (x.astype(f32) for x in arrived)
+    own_sum = own_sum + own_forth + own_back
+    got_sum = got_sum.astype(f32) + partner_forth + partner_back
 
     low_sum, high_sum = pick(xh, own_sum, got_sum)
     grad_gate = jnp.concatenate([low_sum[:, :half], high_sum[:, :half]], axis=1)

time: 165 us -> 160 us (0.970)
  waiting for transfers between devices: 55.5 us -> 45.5 us
  starting transfers between devices: 66.4 us -> 73.5 us
  local copies, waits for them, and re-layouts: 11.9 us -> 7.24 us
  Pallas kernels: 7.15 us -> 9 us
    ppermute x8 -> x9, waiting for transfers between devices: 21 us -> 10.9 us  [ring(): return lax.ppermute(x, ('z', 'xh', 'core'), pairs)]
    ppermute x8 -> x9, starting transfers between devices: 29.1 us -> 38.2 us  [ring(): return lax.ppermute(x, ('z', 'xh', 'core'), pairs)]
    unnamed x41 -> x35, local copies, waits for them, and re-layouts: 9.32 us -> 4.7 us
    all_to_all x1, starting transfers between devices: 8.43 us -> 6.35 us  [on_device(): lax.all_to_all(pair.reshape(peers, own_inputs, model), plane, split_axis=...]
    pallas_call x8 -> x9, Pallas kernels: 7.15 us -> 9 us  [call(): pl.pallas_call(kernel, out_shape=outs, in_specs=[pl.BlockSpec(memory_spac...]
  transfers between devices with their start and end apart: 16 -> 17, of which waited for: 12 -> 10; matrix products, arithmetic and copies ran while one was open for 3% -> 3% of each run, Pallas kernels for 1% -> 2%
where the time goes in v3:
time: 160 us; the launch traced here: 159 us
  starting transfers between devices  73.5 us (46%)
  waiting for transfers between devices  45.5 us (28%)
  between operations  15.2 us (10%)
  Pallas kernels  9 us (6%)
  other arithmetic  8.92 us (6%)
  local copies, waits for them, and re-layouts  7.24 us (5%)
    ppermute x9, starting transfers between devices, ring(): return lax.ppermute(x, ('z', 'xh', 'core'), pairs)  38.2 us
    ppermute x5, starting transfers between devices, swap(): return lax.ppermute(x, axis, [(0, 1), (1, 0)])  18.5 us
    all_to_all x1, waiting for transfers between devices, on_device(): lax.all_to_all(spread, plane, split_axis=0, concat_axis=0)  15.9 us
    ppermute x5, waiting for transfers between devices, swap(): return lax.ppermute(x, axis, [(0, 1), (1, 0)])  15.2 us
    ppermute x9, waiting for transfers between devices, ring(): return lax.ppermute(x, ('z', 'xh', 'core'), pairs)  10.9 us
    all_to_all x1, starting transfers between devices, on_device(): lax.all_to_all(spread, plane, split_axis=0, concat_axis=0)  10.3 us
    pallas_call x9, Pallas kernels, call(): pl.pallas_call(kernel, out_shape=outs, in_specs=[pl.BlockSpec(memory_spac...  9 us
    all_to_all x1, starting transfers between devices, on_device(): lax.all_to_all(pair.reshape(peers, own_inputs, model), plane, split_axis=...  6.35 us
  transfers between devices with their start and end apart: 17, of which 10 were waited for; matrix products, arithmetic and copies ran while one was open for 3% of the time, Pallas kernels for 2%

profile of v3, /device:TPU:8, one launch (start us, length us, event | category | flops | bytes accessed | tf_op | source)
XLA Modules:
  0.0 159.3 jit_solution(1016840166718907895)
XLA Ops:
  7.2 1.2 fusion.17
  8.6 4.9 %collective-permute-start.2 = (bf16[144,576]{1,0:T(8,128)(2,1)S(1)}, bf16[144,576]{1,0:T(8,128)(2,1)S(1)}, u32[]{:S(2)}, u32[]{:S(2)}) collective-permute-start(bf16[144,576]{1,0:T(8,128)(2,1)S(1)} %broadcast_select_fusion.10), channel_id=1, source_target_pairs={{0,32},{32,0},{1,33},{33,1},{2,34},{34,2},{3,35},{35,3},{4,36},{36... | collective-permute-start | bytes 497672 | tf_op jit(solution)/shard_map/ppermute | solution.py:47
  13.5 4.8 %collective-permute-done.2 = bf16[144,576]{1,0:T(8,128)(2,1)S(1)} collective-permute-done((bf16[144,576]{1,0:T(8,128)(2,1)S(1)}, bf16[144,576]{1,0:T(8,128)(2,1)S(1)}, u32[]{:S(2)}, u32[]{:S(2)}) %collective-permute-start.2) | collective-permute-done | bytes 165920 | tf_op jit(solution)/shard_map/ppermute | solution.py:47
  18.5 0.8 pad_maximum_fusion.1
  19.3 1.1 broadcast_in_dim.4
  20.5 10.3 %all-to-all-start = ((bf16[32,8,2304]{2,1,0:T(8,128)(2,1)}), bf16[32,8,2304]{2,1,0:T(8,128)(2,1)S(1)}, u32[]{:S(2)}, u32[]{:S(2)}) async-start(bf16[32,8,2304]{2,1,0:T(8,128)(2,1)} %broadcast_in_dim.4), calls=%async_computation | async-start | bytes 2359296 | tf_op jit(solution)/shard_map/all_to_all | solution.py:174
  31.7 0.4 fusion
  32.2 4.9 %collective-permute-start = (bf16[256,288]{1,0:T(8,128)(2,1)S(1)}, bf16[256,288]{1,0:T(8,128)(2,1)S(1)}, u32[]{:S(2)}, u32[]{:S(2)}) collective-permute-start(bf16[256,288]{1,0:T(8,128)(2,1)S(1)} %broadcast_select_fusion.2), channel_id=1, source_target_pairs={{0,32},{32,0},{1,33},{33,1},{2,34},{34,2},{3,35},{35,3},{4,36},{36... | collective-permute-start | bytes 442376 | tf_op jit(solution)/shard_map/ppermute | solution.py:47
  37.1 7.8 %collective-permute-done = bf16[256,288]{1,0:T(8,128)(2,1)S(1)} collective-permute-done((bf16[256,288]{1,0:T(8,128)(2,1)S(1)}, bf16[256,288]{1,0:T(8,128)(2,1)S(1)}, u32[]{:S(2)}, u32[]{:S(2)}) %collective-permute-start) | collective-permute-done | bytes 147488 | tf_op jit(solution)/shard_map/ppermute | solution.py:47
  45.2 15.9 %all-to-all-done = bf16[32,8,2304]{2,1,0:T(8,128)(2,1)S(1)} async-done(((bf16[32,8,2304]{2,1,0:T(8,128)(2,1)}), bf16[32,8,2304]{2,1,0:T(8,128)(2,1)S(1)}, u32[]{:S(2)}, u32[]{:S(2)}) %all-to-all-start) | async-done | bytes 1179680 | tf_op jit(solution)/shard_map/all_to_all | solution.py:174
  61.1 1.9 %collective-permute-start.1 = (bf16[256,2304]{1,0:T(8,128)(2,1)S(1)}, bf16[256,2304]{1,0:T(8,128)(2,1)}, u32[]{:S(2)}, u32[]{:S(2)}) collective-permute-start(bf16[256,2304]{1,0:T(8,128)(2,1)S(1)} %bitcast.23), channel_id=1, source_target_pairs={{0,1},{1,0},{2,3},{3,2},{4,5},{5,4},{6,7},{7,6},{8,9},{9,8},{10,11... | collective-permute-start | bytes 3538952 | tf_op jit(solution)/shard_map/ppermute | solution.py:47
  63.0 0.4 turn.2.turned
  63.4 2.6 %collective-permute-done.1.rows = bf16[256,2304]{1,0:T(8,128)(2,1)} collective-permute-done((bf16[256,2304]{1,0:T(8,128)(2,1)S(1)}, bf16[256,2304]{1,0:T(8,128)(2,1)}, u32[]{:S(2)}, u32[]{:S(2)}) %collective-permute-start.1) | collective-permute-done | bytes 1179680 | tf_op jit(solution)/shard_map/ppermute | solution.py:47
  66.0 1.6 %turn.3.turned_other = bf16[2304,256]{1,0:T(8,128)(2,1)S(1)} custom-call(s32[1]{0:T(128)} %bitcast.place_ref, bf16[256,2304]{1,0:T(8,128)(2,1)} %collective-permute-done.1.rows), custom_call_target="tpu_custom_call" | custom-call | tf_op jit(solution)/shard_map/turn/pallas_call | solution.py:56
  67.6 3.5 %all-gather.2.cloned.1.call-done.weights = bf16[2304,576]{1,0:T(8,128)(2,1)} async-done(((bf16[288,576]{1,0:T(8,128)(2,1)}), bf16[2304,576]{1,0:T(8,128)(2,1)}) %all-gather.2.cloned.1.call-update) | async-done | bytes 2654224 | tf_op jit(solution)/shard_map/all_gather | solution.py:169
  71.1 1.8 %copy-done = bf16[2304,576]{1,0:T(8,128)(2,1)S(1)} copy-done((bf16[2304,576]{1,0:T(8,128)(2,1)S(1)}, bf16[2304,576]{1,0:T(8,128)(2,1)}, u32[]{:S(2)}) %copy-start) | copy-done | bytes 2654232
  72.9 3.0 %forward.1 = (bf16[512,576]{1,0:T(8,128)(2,1)S(1)}, bf16[288,576]{1,0:T(8,128)(2,1)S(1)}, bf16[288,576]{1,0:T(8,128)(2,1)S(1)}, f32[288,576]{1,0:T(8,128)S(1)}) custom-call(s32[1]{0:T(128)} %bitcast.place_ref, bf16[2304,256]{1,0:T(8,128)(2,1)S(1)} %turn.2.turned, bf16[2304,256]{1,0:T(8,128)(2,1)S(1)} %turn.3.turned_other, bf16[2304,576]{1,0:T(8,128)(2,1)S(1)} %copy-done, ...), custom_call_target="tpu_custom_call" | custom-call | tf_op jit(solution)/shard_map/forward/pallas_call | solution.py:56
  76.0 2.0 %inputs.1 = (f32[256,2304]{1,0:T(8,128)S(1)}, bf16[256,2304]{1,0:T(8,128)(2,1)S(1)}) custom-call(s32[1]{0:T(128)} %bitcast.place_ref, bf16[512,576]{1,0:T(8,128)(2,1)S(1)} %get-tuple-element.28.dboth, bf16[2304,576]{1,0:T(8,128)(2,1)S(1)} %copy-done), custom_call_target="tpu_custom_call" | custom-call | tf_op jit(solution)/shard_map/inputs/pallas_call | solution.py:56
  78.0 1.9 %collective-permute-start.5 = (bf16[256,2304]{1,0:T(8,128)(2,1)S(1)}, bf16[256,2304]{1,0:T(8,128)(2,1)S(1)}, u32[]{:S(2)}, u32[]{:S(2)}) collective-permute-start(bf16[256,2304]{1,0:T(8,128)(2,1)S(1)} %get-tuple-element.30), channel_id=1, source_target_pairs={{0,1},{1,0},{2,3},{3,2},{4,5},{5,4},{6,7},{7,6},{8,9},{9,8},{10,11... | collective-permute-start | bytes 3538952 | tf_op jit(solution)/shard_map/ppermute | solution.py:47
  80.0 4.9 %collective-permute-start.6 = (bf16[144,576]{1,0:T(8,128)(2,1)S(1)}, bf16[144,576]{1,0:T(8,128)(2,1)S(1)}, u32[]{:S(2)}, u32[]{:S(2)}) collective-permute-start(bf16[144,576]{1,0:T(8,128)(2,1)S(1)} %select_convert_fusion), channel_id=1, source_target_pairs={{0,32},{32,0},{1,33},{33,1},{2,34},{34,2},{3,35},{35,3},{4,36},{36... | collective-permute-start | bytes 497672 | tf_op jit(solution)/shard_map/ppermute | solution.py:47
  84.9 3.1 %collective-permute-start.3 = (bf16[288,576]{1,0:T(8,128)(2,1)S(1)}, bf16[288,576]{1,0:T(8,128)(2,1)S(1)}, u32[]{:S(2)}, u32[]{:S(2)}) collective-permute-start(bf16[288,576]{1,0:T(8,128)(2,1)S(1)} %get-tuple-element.26), channel_id=1, source_target_pairs={{0,64},{1,449},{32,96},{33,481},{64,128},{65,1},{96,160},{97,33},{... | collective-permute-start | bytes 995336 | tf_op jit(solution)/shard_map/ppermute | solution.py:157
  88.0 5.0 %collective-permute-start.4 = (bf16[288,576]{1,0:T(8,128)(2,1)S(1)}, bf16[288,576]{1,0:T(8,128)(2,1)S(1)}, u32[]{:S(2)}, u32[]{:S(2)}) collective-permute-start(bf16[288,576]{1,0:T(8,128)(2,1)S(1)} %get-tuple-element.27), channel_id=1, source_target_pairs={{0,448},{1,65},{32,480},{33,97},{64,0},{65,129},{96,32},{97,161},{... | collective-permute-start | bytes 995336 | tf_op jit(solution)/shard_map/ppermute | solution.py:157
  93.1 1.2 add_convert_fusion
  94.3 2.3 %collective-permute-done.3.arrived = bf16[288,576]{1,0:T(8,128)(2,1)S(1)} collective-permute-done((bf16[288,576]{1,0:T(8,128)(2,1)S(1)}, bf16[288,576]{1,0:T(8,128)(2,1)S(1)}, u32[]{:S(2)}, u32[]{:S(2)}) %collective-permute-start.3) | collective-permute-done | bytes 331808 | tf_op jit(solution)/shard_map/ppermute | solution.py:157
  96.6 0.7 copy-done.3
  97.3 1.9 %collective-permute-done.4.arrived = bf16[288,576]{1,0:T(8,128)(2,1)S(1)} collective-permute-done((bf16[288,576]{1,0:T(8,128)(2,1)S(1)}, bf16[288,576]{1,0:T(8,128)(2,1)S(1)}, u32[]{:S(2)}, u32[]{:S(2)}) %collective-permute-start.4) | collective-permute-done | bytes 331808 | tf_op jit(solution)/shard_map/ppermute | solution.py:157
  99.2 6.4 %all-to-all-start.1 = ((bf16[32,8,2304]{2,1,0:T(8,128)(2,1)}), bf16[32,8,2304]{2,1,0:T(8,128)(2,1)}, u32[]{:S(2)}, u32[]{:S(2)}) async-start(bf16[32,8,2304]{2,1,0:T(8,128)(2,1)} %bitcast.25), calls=%async_computation.1 | async-start | bytes 2359296 | tf_op jit(solution)/shard_map/all_to_all | solution.py:218
  105.6 1.0 copy-done.4
  106.6 0.4 add_term.5
  107.0 3.1 %collective-permute-start.7 = (bf16[288,576]{1,0:T(8,128)(2,1)S(1)}, bf16[288,576]{1,0:T(8,128)(2,1)S(1)}, u32[]{:S(2)}, u32[]{:S(2)}) collective-permute-start(bf16[288,576]{1,0:T(8,128)(2,1)S(1)} %add_term.5), channel_id=1, source_target_pairs={{0,64},{1,449},{32,96},{33,481},{64,128},{65,1},{96,160},{97,33},{... | collective-permute-start | bytes 995336 | tf_op jit(solution)/shard_map/ppermute | solution.py:157
  110.1 0.4 add_term.8
  110.5 4.2 %collective-permute-start.11 = (bf16[288,576]{1,0:T(8,128)(2,1)S(1)}, bf16[288,576]{1,0:T(8,128)(2,1)S(1)}, u32[]{:S(2)}, u32[]{:S(2)}) collective-permute-start(bf16[288,576]{1,0:T(8,128)(2,1)S(1)} %add_term.8), channel_id=1, source_target_pairs={{0,448},{1,65},{32,480},{33,97},{64,0},{65,129},{96,32},{97,161},{... | collective-permute-start | bytes 995336 | tf_op jit(solution)/shard_map/ppermute | solution.py:157
  114.7 3.6 %collective-permute-done.7.arrived = bf16[288,576]{1,0:T(8,128)(2,1)S(1)} collective-permute-done((bf16[288,576]{1,0:T(8,128)(2,1)S(1)}, bf16[288,576]{1,0:T(8,128)(2,1)S(1)}, u32[]{:S(2)}, u32[]{:S(2)}) %collective-permute-start.7) | collective-permute-done | bytes 331808 | tf_op jit(solution)/shard_map/ppermute | solution.py:157
  118.3 0.4 add_term.6
  118.7 1.9 %collective-permute-start.8 = (bf16[288,576]{1,0:T(8,128)(2,1)S(1)}, bf16[288,576]{1,0:T(8,128)(2,1)S(1)}, u32[]{:S(2)}, u32[]{:S(2)}) collective-permute-start(bf16[288,576]{1,0:T(8,128)(2,1)S(1)} %add_term.6), channel_id=1, source_target_pairs={{0,64},{1,449},{32,96},{33,481},{64,128},{65,1},{96,160},{97,33},{... | collective-permute-start | bytes 995336 | tf_op jit(solution)/shard_map/ppermute | solution.py:157
  120.6 0.4 add_term.9
  121.1 6.9 %collective-permute-start.12 = (bf16[144,576]{1,0:T(8,128)(2,1)S(1)}, bf16[144,576]{1,0:T(8,128)(2,1)}, u32[]{:S(2)}, u32[]{:S(2)}) collective-permute-start(bf16[144,576]{1,0:T(8,128)(2,1)S(1)} %get-tuple-element.58), channel_id=1, source_target_pairs={{0,448},{1,65},{32,480},{33,97},{64,0},{65,129},{96,32},{97,161},{... | collective-permute-start | bytes 497672 | tf_op jit(solution)/shard_map/ppermute | solution.py:157
  128.0 6.3 %collective-permute-start.13 = (bf16[144,576]{1,0:T(8,128)(2,1)S(1)}, bf16[144,576]{1,0:T(8,128)(2,1)}, u32[]{:S(2)}, u32[]{:S(2)}) collective-permute-start(bf16[144,576]{1,0:T(8,128)(2,1)S(1)} %get-tuple-element.57), channel_id=1, source_target_pairs={{0,480},{1,97},{32,448},{33,65},{64,32},{65,161},{96,0},{97,129},{... | collective-permute-start | bytes 497672 | tf_op jit(solution)/shard_map/ppermute | solution.py:157
  134.3 0.4 add_term.7
  134.8 3.1 %collective-permute-start.10 = (bf16[144,576]{1,0:T(8,128)(2,1)S(1)}, bf16[144,576]{1,0:T(8,128)(2,1)S(1)}, u32[]{:S(2)}, u32[]{:S(2)}) collective-permute-start(bf16[144,576]{1,0:T(8,128)(2,1)S(1)} %get-tuple-element.59), channel_id=1, source_target_pairs={{0,96},{1,481},{32,64},{33,449},{64,160},{65,33},{96,128},{97,1},{... | collective-permute-start | bytes 497672 | tf_op jit(solution)/shard_map/ppermute | solution.py:157
  137.9 4.5 %collective-permute-start.9 = (bf16[144,576]{1,0:T(8,128)(2,1)S(1)}, bf16[144,576]{1,0:T(8,128)(2,1)S(1)}, u32[]{:S(2)}, u32[]{:S(2)}) collective-permute-start(bf16[144,576]{1,0:T(8,128)(2,1)S(1)} %get-tuple-element.60), channel_id=1, source_target_pairs={{0,64},{1,449},{32,96},{33,481},{64,128},{65,1},{96,160},{97,33},{... | collective-permute-start | bytes 497672 | tf_op jit(solution)/shard_map/ppermute | solution.py:157
  142.5 2.1 %reduce_sum.12 = bf16[8,2304]{1,0:T(8,128)(2,1)} reduce(bf16[32,8,2304]{2,1,0:T(8,128)(2,1)} %all-to-all-done.1, bf16[]{:T(256)} %constant.58.clone.1), dimensions={0}, to_apply=%region_0.1 | reduce | flops 571392 | bytes 1216514 | tf_op jit(solution)/shard_map/reduce_sum | solution.py:221
  144.6 1.4 collective-permute-done.10
  146.0 1.6 %collective-permute-done.9 = bf16[144,576]{1,0:T(8,128)(2,1)S(1)} collective-permute-done((bf16[144,576]{1,0:T(8,128)(2,1)S(1)}, bf16[144,576]{1,0:T(8,128)(2,1)S(1)}, u32[]{:S(2)}, u32[]{:S(2)}) %collective-permute-start.9) | collective-permute-done | bytes 165920 | tf_op jit(solution)/shard_map/ppermute | solution.py:157
  147.6 1.2 fusion.10
  149.1 0.6 copy-done.5
  150.0 1.2 fusion.6
  151.2 1.2 fusion.3
  (55 shorter events, 1.8 us)
Async XLA Ops:
  7.2 63.9 %all-gather.2.cloned.1.call-start = ((), (), s32[]{:S(2)}) async-start(), calls=%async_computation.2 | async-start | bytes 3317760 | tf_op jit(solution)/shard_map/all_gather | solution.py:169
  8.6 10.8 %copy-start.14 = (bf16[8,2304]{1,0:T(8,128)(2,1)S(1)}, bf16[8,2304]{1,0:T(8,128)(2,1)}, u32[]{:S(2)}) copy-start(bf16[8,2304]{1,0:T(8,128)(2,1)} %param.11) | copy-start | bytes 110596
  8.6 9.8 %collective-permute-start.2 = (bf16[144,576]{1,0:T(8,128)(2,1)S(1)}, bf16[144,576]{1,0:T(8,128)(2,1)S(1)}, u32[]{:S(2)}, u32[]{:S(2)}) collective-permute-start(bf16[144,576]{1,0:T(8,128)(2,1)S(1)} %broadcast_select_fusion.10), channel_id=1, source_target_pairs={{0,32},{32,0},{1,33},{33,1},{2,34},{34,2},{3,35},{35,3},{4,36},{36... | collective-permute-start | bytes 497672 | tf_op jit(solution)/shard_map/ppermute | solution.py:47
  20.5 10.3 %copy-start.11 = (bf16[256,576]{0,1:T(8,128)(2,1)S(1)}, bf16[256,576]{0,1:T(8,128)(2,1)}, u32[]{:S(2)}) copy-start(bf16[256,576]{0,1:T(8,128)(2,1)} %param.12) | copy-start | bytes 884740
  20.5 11.2 %copy-start.16 = (s32[256]{0:T(256)S(1)}, s32[256]{0:T(256)}, u32[]{:S(2)}) copy-start(s32[256]{0:T(256)} %param.13) | copy-start | bytes 3076
  20.5 11.2 %copy-start.15 = (s32[576]{0:T(1024)S(1)}, s32[576]{0:T(1024)}, u32[]{:S(2)}) copy-start(s32[576]{0:T(1024)} %param.14) | copy-start | bytes 6916
  20.5 40.6 %all-to-all-start = ((bf16[32,8,2304]{2,1,0:T(8,128)(2,1)}), bf16[32,8,2304]{2,1,0:T(8,128)(2,1)S(1)}, u32[]{:S(2)}, u32[]{:S(2)}) async-start(bf16[32,8,2304]{2,1,0:T(8,128)(2,1)} %broadcast_in_dim.4), calls=%async_computation | async-start | bytes 2359296 | tf_op jit(solution)/shard_map/all_to_all | solution.py:174
  32.2 12.7 %collective-permute-start = (bf16[256,288]{1,0:T(8,128)(2,1)S(1)}, bf16[256,288]{1,0:T(8,128)(2,1)S(1)}, u32[]{:S(2)}, u32[]{:S(2)}) collective-permute-start(bf16[256,288]{1,0:T(8,128)(2,1)S(1)} %broadcast_select_fusion.2), channel_id=1, source_target_pairs={{0,32},{32,0},{1,33},{33,1},{2,34},{34,2},{3,35},{35,3},{4,36},{36... | collective-permute-start | bytes 442376 | tf_op jit(solution)/shard_map/ppermute | solution.py:47
  61.1 4.9 %collective-permute-start.1 = (bf16[256,2304]{1,0:T(8,128)(2,1)S(1)}, bf16[256,2304]{1,0:T(8,128)(2,1)}, u32[]{:S(2)}, u32[]{:S(2)}) collective-permute-start(bf16[256,2304]{1,0:T(8,128)(2,1)S(1)} %bitcast.23), channel_id=1, source_target_pairs={{0,1},{1,0},{2,3},{3,2},{4,5},{5,4},{6,7},{7,6},{8,9},{9,8},{10,11... | collective-permute-start | bytes 3538952 | tf_op jit(solution)/shard_map/ppermute | solution.py:47
  71.1 1.8 %copy-start = (bf16[2304,576]{1,0:T(8,128)(2,1)S(1)}, bf16[2304,576]{1,0:T(8,128)(2,1)}, u32[]{:S(2)}) copy-start(bf16[2304,576]{1,0:T(8,128)(2,1)} %all-gather.2.cloned.1.call-done.weights) | copy-start | bytes 7962628
  75.9 4.0 %copy-start.1 = (f32[288,576]{1,0:T(8,128)}, f32[288,576]{1,0:T(8,128)S(1)}, u32[]{:S(2)}) copy-start(f32[288,576]{1,0:T(8,128)S(1)} %get-tuple-element.31) | copy-start | bytes 1990660
  78.0 15.1 %collective-permute-start.5 = (bf16[256,2304]{1,0:T(8,128)(2,1)S(1)}, bf16[256,2304]{1,0:T(8,128)(2,1)S(1)}, u32[]{:S(2)}, u32[]{:S(2)}) collective-permute-start(bf16[256,2304]{1,0:T(8,128)(2,1)S(1)} %get-tuple-element.30), channel_id=1, source_target_pairs={{0,1},{1,0},{2,3},{3,2},{4,5},{5,4},{6,7},{7,6},{8,9},{9,8},{10,11... | collective-permute-start | bytes 3538952 | tf_op jit(solution)/shard_map/ppermute | solution.py:47
  80.0 14.3 %collective-permute-start.6 = (bf16[144,576]{1,0:T(8,128)(2,1)S(1)}, bf16[144,576]{1,0:T(8,128)(2,1)S(1)}, u32[]{:S(2)}, u32[]{:S(2)}) collective-permute-start(bf16[144,576]{1,0:T(8,128)(2,1)S(1)} %select_convert_fusion), channel_id=1, source_target_pairs={{0,32},{32,0},{1,33},{33,1},{2,34},{34,2},{3,35},{35,3},{4,36},{36... | collective-permute-start | bytes 497672 | tf_op jit(solution)/shard_map/ppermute | solution.py:47
  84.9 11.7 %collective-permute-start.3 = (bf16[288,576]{1,0:T(8,128)(2,1)S(1)}, bf16[288,576]{1,0:T(8,128)(2,1)S(1)}, u32[]{:S(2)}, u32[]{:S(2)}) collective-permute-start(bf16[288,576]{1,0:T(8,128)(2,1)S(1)} %get-tuple-element.26), channel_id=1, source_target_pairs={{0,64},{1,449},{32,96},{33,481},{64,128},{65,1},{96,160},{97,33},{... | collective-permute-start | bytes 995336 | tf_op jit(solution)/shard_map/ppermute | solution.py:157
  88.0 11.2 %collective-permute-start.4 = (bf16[288,576]{1,0:T(8,128)(2,1)S(1)}, bf16[288,576]{1,0:T(8,128)(2,1)S(1)}, u32[]{:S(2)}, u32[]{:S(2)}) collective-permute-start(bf16[288,576]{1,0:T(8,128)(2,1)S(1)} %get-tuple-element.27), channel_id=1, source_target_pairs={{0,448},{1,65},{32,480},{33,97},{64,0},{65,129},{96,32},{97,161},{... | collective-permute-start | bytes 995336 | tf_op jit(solution)/shard_map/ppermute | solution.py:157
  94.3 4.9 %copy-start.12 = (bf16[144,576]{1,0:T(8,128)(2,1)}, bf16[144,576]{1,0:T(8,128)(2,1)S(1)}, u32[]{:S(2)}) copy-start(bf16[144,576]{1,0:T(8,128)(2,1)S(1)} %collective-permute-done.6) | copy-start | bytes 497668
  96.6 0.7 copy-start.3
  99.2 43.3 %all-to-all-start.1 = ((bf16[32,8,2304]{2,1,0:T(8,128)(2,1)}), bf16[32,8,2304]{2,1,0:T(8,128)(2,1)}, u32[]{:S(2)}, u32[]{:S(2)}) async-start(bf16[32,8,2304]{2,1,0:T(8,128)(2,1)} %bitcast.25), calls=%async_computation.1 | async-start | bytes 2359296 | tf_op jit(solution)/shard_map/all_to_all | solution.py:218
  105.6 1.0 copy-start.4
  107.0 11.3 %collective-permute-start.7 = (bf16[288,576]{1,0:T(8,128)(2,1)S(1)}, bf16[288,576]{1,0:T(8,128)(2,1)S(1)}, u32[]{:S(2)}, u32[]{:S(2)}) collective-permute-start(bf16[288,576]{1,0:T(8,128)(2,1)S(1)} %add_term.5), channel_id=1, source_target_pairs={{0,64},{1,449},{32,96},{33,481},{64,128},{65,1},{96,160},{97,33},{... | collective-permute-start | bytes 995336 | tf_op jit(solution)/shard_map/ppermute | solution.py:157
  110.5 10.2 %collective-permute-start.11 = (bf16[288,576]{1,0:T(8,128)(2,1)S(1)}, bf16[288,576]{1,0:T(8,128)(2,1)S(1)}, u32[]{:S(2)}, u32[]{:S(2)}) collective-permute-start(bf16[288,576]{1,0:T(8,128)(2,1)S(1)} %add_term.8), channel_id=1, source_target_pairs={{0,448},{1,65},{32,480},{33,97},{64,0},{65,129},{96,32},{97,161},{... | collective-permute-start | bytes 995336 | tf_op jit(solution)/shard_map/ppermute | solution.py:157
  118.7 15.6 %collective-permute-start.8 = (bf16[288,576]{1,0:T(8,128)(2,1)S(1)}, bf16[288,576]{1,0:T(8,128)(2,1)S(1)}, u32[]{:S(2)}, u32[]{:S(2)}) collective-permute-start(bf16[288,576]{1,0:T(8,128)(2,1)S(1)} %add_term.6), channel_id=1, source_target_pairs={{0,64},{1,449},{32,96},{33,481},{64,128},{65,1},{96,160},{97,33},{... | collective-permute-start | bytes 995336 | tf_op jit(solution)/shard_map/ppermute | solution.py:157
  121.1 23.5 %collective-permute-start.12 = (bf16[144,576]{1,0:T(8,128)(2,1)S(1)}, bf16[144,576]{1,0:T(8,128)(2,1)}, u32[]{:S(2)}, u32[]{:S(2)}) collective-permute-start(bf16[144,576]{1,0:T(8,128)(2,1)S(1)} %get-tuple-element.58), channel_id=1, source_target_pairs={{0,448},{1,65},{32,480},{33,97},{64,0},{65,129},{96,32},{97,161},{... | collective-permute-start | bytes 497672 | tf_op jit(solution)/shard_map/ppermute | solution.py:157
  128.0 16.6 %collective-permute-start.13 = (bf16[144,576]{1,0:T(8,128)(2,1)S(1)}, bf16[144,576]{1,0:T(8,128)(2,1)}, u32[]{:S(2)}, u32[]{:S(2)}) collective-permute-start(bf16[144,576]{1,0:T(8,128)(2,1)S(1)} %get-tuple-element.57), channel_id=1, source_target_pairs={{0,480},{1,97},{32,448},{33,65},{64,32},{65,161},{96,0},{97,129},{... | collective-permute-start | bytes 497672 | tf_op jit(solution)/shard_map/ppermute | solution.py:157
  134.7 12.9 %copy-start.2 = (f32[288,576]{1,0:T(8,128)S(1)}, f32[288,576]{1,0:T(8,128)}, u32[]{:S(2)}) copy-start(f32[288,576]{1,0:T(8,128)} %copy-done.1) | copy-start | bytes 1990660
  134.7 12.9 %copy-start.13 = (bf16[144,576]{1,0:T(8,128)(2,1)S(1)}, bf16[144,576]{1,0:T(8,128)(2,1)}, u32[]{:S(2)}) copy-start(bf16[144,576]{1,0:T(8,128)(2,1)} %copy-done.12) | copy-start | bytes 497668
  134.8 11.2 %collective-permute-start.10 = (bf16[144,576]{1,0:T(8,128)(2,1)S(1)}, bf16[144,576]{1,0:T(8,128)(2,1)S(1)}, u32[]{:S(2)}, u32[]{:S(2)}) collective-permute-start(bf16[144,576]{1,0:T(8,128)(2,1)S(1)} %get-tuple-element.59), channel_id=1, source_target_pairs={{0,96},{1,481},{32,64},{33,449},{64,160},{65,33},{96,128},{97,1},{... | collective-permute-start | bytes 497672 | tf_op jit(solution)/shard_map/ppermute | solution.py:157
  137.9 9.7 %collective-permute-start.9 = (bf16[144,576]{1,0:T(8,128)(2,1)S(1)}, bf16[144,576]{1,0:T(8,128)(2,1)S(1)}, u32[]{:S(2)}, u32[]{:S(2)}) collective-permute-start(bf16[144,576]{1,0:T(8,128)(2,1)S(1)} %get-tuple-element.60), channel_id=1, source_target_pairs={{0,64},{1,449},{32,96},{33,481},{64,128},{65,1},{96,160},{97,33},{... | collective-permute-start | bytes 497672 | tf_op jit(solution)/shard_map/ppermute | solution.py:157
  148.8 0.9 copy-start.5
  148.8 1.1 copy-start.7
  148.8 1.2 copy-start.8
  149.1 2.1 %copy-start.6 = (bf16[144,576]{1,0:T(8,128)(2,1)S(1)}, bf16[144,576]{1,0:T(8,128)(2,1)}, u32[]{:S(2)}) copy-start(bf16[144,576]{1,0:T(8,128)(2,1)} %param.16) | copy-start | bytes 497668
  149.1 2.1 %copy-start.9 = (f32[144,576]{1,0:T(8,128)S(1)}, f32[144,576]{1,0:T(8,128)}, u32[]{:S(2)}) copy-start(f32[144,576]{1,0:T(8,128)} %param.18) | copy-start | bytes 995332
  149.1 2.1 %copy-start.10 = (f32[144,576]{1,0:T(8,128)S(1)}, f32[144,576]{1,0:T(8,128)}, u32[]{:S(2)}) copy-start(f32[144,576]{1,0:T(8,128)} %param.19) | copy-start | bytes 995332
Sparse Core Ops, SparseCore 0:
  19.5 51.5 all-gather.1

commit v4 on v3

--- a/solution.py
+++ b/solution.py
@@ -17,7 +17,7 @@
 bf16 = jnp.bfloat16
 f32 = jnp.float32
 
-plane = ("xh", "xl", "y")
+plane = ("y", "xh", "xl")
 
 
 def keep_mask(token_key, feature_key, drop_seed):
@@ -82,7 +82,7 @@
 
 
 def forward_kernel(
-    depth, place_ref, turned, turned_other, weights, kept, dboth, forth, back, middle
+    depth, place_ref, turned, turned_other, weights, kept, dboth, forth, back
 ):
     half = kept.shape[1]
     tokens = turned.shape[1]
@@ -104,9 +104,13 @@
         dboth[span, :half] = (dropped * up * slope).astype(bf16)
         dboth[span, half:] = (dropped * act).astype(bf16)
     far = depth // 2
-    for out, step in ((forth, far), (back, 1 - far), (middle, 0)):
+    for out, step in ((forth, far), (back, 1 - far)):
         term = block_product(place_ref, step, depth, turned, turned_other, dboth)
-        out[...] = term.astype(out.dtype)
+        out[...] = term.astype(bf16)
+
+
+def middle_kernel(depth, place_ref, turned, turned_other, dboth, total):
+    total[...] = block_product(place_ref, 0, depth, turned, turned_other, dboth)
 
 
 def hop_kernel(depth, step, place_ref, arrived, turned, turned_other, dboth, total):
@@ -178,9 +182,10 @@
     mine_grad, other_grad = pick(xh, masked[:, :half], masked[:, half:])
     other_grad = swap(other_grad, "xh")
     lower, upper = pick(xh, mine_grad, other_grad)
-    kept = jnp.concatenate([lower, upper], axis=0)
-    kept = kept.reshape(-1, 2, own_inputs, half)
-    kept = jnp.concatenate(pick(core, kept[:, 0], kept[:, 1]), axis=0).reshape(-1, half)
+    across_y = lax.axis_size("y")
+    kept = jnp.stack([lower, upper]).reshape(4, across_y, 2, own_inputs, half)
+    kept = kept.transpose(2, 1, 0, 3, 4)
+    kept = jnp.concatenate(pick(core, kept[0], kept[1]), axis=0).reshape(-1, half)
 
     core_rows, kept = lax.optimization_barrier((core_rows, kept))
     far = depth // 2
@@ -190,10 +195,9 @@
     turn = in_vmem(turn_kernel, [jax.ShapeDtypeStruct((model, tokens // 2), bf16)], "turn")
     turned = turn(place, core_rows)[0]
     turned_other = turn(place, swap(core_rows, "core"))[0]
-    dboth, forth, back, middle = in_vmem(
+    dboth, forth, back = in_vmem(
         functools.partial(forward_kernel, depth),
-        [jax.ShapeDtypeStruct(shape, bf16) for shape in ((tokens, own_units), block, block)]
-        + [jax.ShapeDtypeStruct(block, f32)],
+        [jax.ShapeDtypeStruct(shape, bf16) for shape in ((tokens, own_units), block, block)],
         "forward",
     )(place, turned, turned_other, weights, kept)
 
@@ -209,16 +213,16 @@
         [jax.ShapeDtypeStruct((tokens // 2, model), dtype) for dtype in (f32, bf16)],
         "inputs",
     )(place, dboth, weights)
-    pair = (core_part + swap(other_part, "core").astype(f32)).astype(bf16)
+    pair = core_part + swap(other_part, "core").astype(f32)
 
     forth, back = along(forth, 1), along(back, -1)
+    forth, back, pair, dboth = lax.optimization_barrier((forth, back, pair, dboth))
+    columns = lax.psum_scatter(pair.reshape(across_y, -1, model), "y", scatter_dimension=0)
+    middle = in_vmem(
+        functools.partial(middle_kernel, depth), [jax.ShapeDtypeStruct(block, f32)], "middle"
+    )(place, turned, turned_other, dboth)[0]
     own_sum, partner_sum = pick(xh, middle[:own_rows], middle[own_rows:])
     got_sum = swap(partner_sum.astype(bf16), "xh")
-    forth, back, pair, got_sum = lax.optimization_barrier((forth, back, pair, got_sum))
-    shares = lax.all_to_all(
-        pair.reshape(peers, own_inputs, model), plane, split_axis=0, concat_axis=0
-    )
-    input_grad = jnp.sum(shares.astype(f32), axis=0).astype(bf16)
 
     def last(message, step):
         own, partner = pick(xh, message[:own_rows], message[own_rows:])
@@ -228,8 +232,13 @@
         forth = along(add_term(forth, step), 1)
         back = add_term(back, 1 - step)
         back = along(back, -1) if step > 2 else last(back, -1)
+    forth, got_sum = lax.optimization_barrier((forth, got_sum))
     forth = last(add_term(forth, 1), 1)
-    input_grad, *arrived = lax.optimization_barrier((input_grad, *forth, *back))
+    columns, *arrived = lax.optimization_barrier((columns, *forth, *back))
+    shares = lax.all_to_all(
+        columns.reshape(4, own_inputs, model), ("xh", "xl"), split_axis=0, concat_axis=0
+    )
+    input_grad = jnp.sum(shares, axis=0).astype(bf16)
     own_forth, partner_forth, own_back, partner_back = (x.astype(f32) for x in arrived)
     own_sum = own_sum + own_forth + own_back
     got_sum = got_sum.astype(f32) + partner_forth + partner_back

time: 160 us -> 158 us (0.988)
  the two profiles are of different devices: /device:TPU:8 before, /device:TPU:2 now
where the time goes in v4:
time: 158 us; the launch traced here: 157 us
  starting transfers between devices  67.1 us (42%)
  waiting for transfers between devices  50.4 us (32%)
  between operations  15.2 us (10%)
  Pallas kernels  9.24 us (6%)
  other arithmetic  7.89 us (5%)
  local copies, waits for them, and re-layouts  7.28 us (5%)
    ppermute x9, starting transfers between devices, ring(): return lax.ppermute(x, ('z', 'xh', 'core'), pairs)  35.9 us
    ppermute x5, waiting for transfers between devices, swap(): return lax.ppermute(x, axis, [(0, 1), (1, 0)])  16.5 us
    all_to_all x1, waiting for transfers between devices, on_device(): lax.all_to_all(spread, plane, split_axis=0, concat_axis=0)  15.9 us
    ppermute x5, starting transfers between devices, swap(): return lax.ppermute(x, axis, [(0, 1), (1, 0)])  15.8 us
    ppermute x9, waiting for transfers between devices, ring(): return lax.ppermute(x, ('z', 'xh', 'core'), pairs)  13.5 us
    all_to_all x1, starting transfers between devices, on_device(): lax.all_to_all(spread, plane, split_axis=0, concat_axis=0)  10.4 us
    pallas_call x10, Pallas kernels, call(): pl.pallas_call(kernel, out_shape=outs, in_specs=[pl.BlockSpec(memory_spac...  9.24 us
    all_to_all x1, starting transfers between devices, on_device(): lax.all_to_all(columns.reshape(4, own_inputs, model), ('xh', 'xl'), split...  4.88 us
  transfers between devices with their start and end apart: 18, of which 11 were waited for; matrix products, arithmetic and copies ran while one was open for 5% of the time, Pallas kernels for 3%

profile of v4, /device:TPU:2, one launch (start us, length us, event | category | flops | bytes accessed | tf_op | source)
XLA Modules:
  0.0 157.1 jit_solution(68527847944367997)
XLA Ops:
  7.2 1.2 fusion.17
  8.6 4.0 %collective-permute-start.2 = (bf16[144,576]{1,0:T(8,128)(2,1)S(1)}, bf16[144,576]{1,0:T(8,128)(2,1)S(1)}, u32[]{:S(2)}, u32[]{:S(2)}) collective-permute-start(bf16[144,576]{1,0:T(8,128)(2,1)S(1)} %broadcast_select_fusion.8), channel_id=1, source_target_pairs={{0,32},{32,0},{1,33},{33,1},{2,34},{34,2},{3,35},{35,3},{4,36},{36... | collective-permute-start | bytes 497672 | tf_op jit(solution)/shard_map/ppermute | solution.py:47
  12.6 5.7 %collective-permute-done.2 = bf16[144,576]{1,0:T(8,128)(2,1)S(1)} collective-permute-done((bf16[144,576]{1,0:T(8,128)(2,1)S(1)}, bf16[144,576]{1,0:T(8,128)(2,1)S(1)}, u32[]{:S(2)}, u32[]{:S(2)}) %collective-permute-start.2) | collective-permute-done | bytes 165920 | tf_op jit(solution)/shard_map/ppermute | solution.py:47
  18.5 0.8 pad_maximum_fusion.2
  19.3 1.1 broadcast_in_dim.4
  20.5 10.4 %all-to-all-start = ((bf16[32,8,2304]{2,1,0:T(8,128)(2,1)}), bf16[32,8,2304]{2,1,0:T(8,128)(2,1)S(1)}, u32[]{:S(2)}, u32[]{:S(2)}) async-start(bf16[32,8,2304]{2,1,0:T(8,128)(2,1)} %broadcast_in_dim.4), calls=%async_computation | async-start | bytes 2359296 | tf_op jit(solution)/shard_map/all_to_all | solution.py:178
  32.3 4.0 %collective-permute-start = (bf16[256,288]{1,0:T(8,128)(2,1)S(1)}, bf16[256,288]{1,0:T(8,128)(2,1)S(1)}, u32[]{:S(2)}, u32[]{:S(2)}) collective-permute-start(bf16[256,288]{1,0:T(8,128)(2,1)S(1)} %broadcast_select_fusion), channel_id=1, source_target_pairs={{0,32},{32,0},{1,33},{33,1},{2,34},{34,2},{3,35},{35,3},{4,36},{36... | collective-permute-start | bytes 442376 | tf_op jit(solution)/shard_map/ppermute | solution.py:47
  36.3 8.2 %collective-permute-done = bf16[256,288]{1,0:T(8,128)(2,1)S(1)} collective-permute-done((bf16[256,288]{1,0:T(8,128)(2,1)S(1)}, bf16[256,288]{1,0:T(8,128)(2,1)S(1)}, u32[]{:S(2)}, u32[]{:S(2)}) %collective-permute-start) | collective-permute-done | bytes 147488 | tf_op jit(solution)/shard_map/ppermute | solution.py:47
  44.9 15.9 %all-to-all-done = bf16[32,8,2304]{2,1,0:T(8,128)(2,1)S(1)} async-done(((bf16[32,8,2304]{2,1,0:T(8,128)(2,1)}), bf16[32,8,2304]{2,1,0:T(8,128)(2,1)S(1)}, u32[]{:S(2)}, u32[]{:S(2)}) %all-to-all-start) | async-done | bytes 1179680 | tf_op jit(solution)/shard_map/all_to_all | solution.py:178
  60.9 1.9 %collective-permute-start.1 = (bf16[256,2304]{1,0:T(8,128)(2,1)S(1)}, bf16[256,2304]{1,0:T(8,128)(2,1)}, u32[]{:S(2)}, u32[]{:S(2)}) collective-permute-start(bf16[256,2304]{1,0:T(8,128)(2,1)S(1)} %bitcast.30), channel_id=1, source_target_pairs={{0,1},{1,0},{2,3},{3,2},{4,5},{5,4},{6,7},{7,6},{8,9},{9,8},{10,11... | collective-permute-start | bytes 3538952 | tf_op jit(solution)/shard_map/ppermute | solution.py:47
  63.1 2.6 %collective-permute-done.1.rows = bf16[256,2304]{1,0:T(8,128)(2,1)} collective-permute-done((bf16[256,2304]{1,0:T(8,128)(2,1)S(1)}, bf16[256,2304]{1,0:T(8,128)(2,1)}, u32[]{:S(2)}, u32[]{:S(2)}) %collective-permute-start.1) | collective-permute-done | bytes 1179680 | tf_op jit(solution)/shard_map/ppermute | solution.py:47
  65.7 1.6 %turn.3.turned_other = bf16[2304,256]{1,0:T(8,128)(2,1)S(1)} custom-call(s32[1]{0:T(128)} %bitcast.place_ref, bf16[256,2304]{1,0:T(8,128)(2,1)} %collective-permute-done.1.rows), custom_call_target="tpu_custom_call" | custom-call | tf_op jit(solution)/shard_map/turn/pallas_call | solution.py:56
  67.4 3.8 %all-gather.2.cloned.1.call-done.weights = bf16[2304,576]{1,0:T(8,128)(2,1)} async-done(((bf16[288,576]{1,0:T(8,128)(2,1)}), bf16[2304,576]{1,0:T(8,128)(2,1)}) %all-gather.2.cloned.1.call-update) | async-done | bytes 2654224 | tf_op jit(solution)/shard_map/all_gather | solution.py:173
  71.1 1.8 %copy-done = bf16[2304,576]{1,0:T(8,128)(2,1)S(1)} copy-done((bf16[2304,576]{1,0:T(8,128)(2,1)S(1)}, bf16[2304,576]{1,0:T(8,128)(2,1)}, u32[]{:S(2)}) %copy-start) | copy-done | bytes 2654232
  73.0 2.8 %forward.1 = (bf16[512,576]{1,0:T(8,128)(2,1)S(1)}, bf16[288,576]{1,0:T(8,128)(2,1)S(1)}, bf16[288,576]{1,0:T(8,128)(2,1)S(1)}) custom-call(s32[1]{0:T(128)} %bitcast.place_ref, bf16[2304,256]{1,0:T(8,128)(2,1)S(1)} %turn.2.turned, bf16[2304,256]{1,0:T(8,128)(2,1)S(1)} %turn.3.turned_other, bf16[2304,576]{1,0:T(8,128)(2,1)S(1)} %copy-done, ...), custom_call_target="tpu_custom_call" | custom-call | tf_op jit(solution)/shard_map/forward/pallas_call | solution.py:56
  75.8 2.0 %inputs.1 = (f32[256,2304]{1,0:T(8,128)S(1)}, bf16[256,2304]{1,0:T(8,128)(2,1)S(1)}) custom-call(s32[1]{0:T(128)} %bitcast.place_ref, bf16[512,576]{1,0:T(8,128)(2,1)S(1)} %get-tuple-element.34.dboth, bf16[2304,576]{1,0:T(8,128)(2,1)S(1)} %copy-done), custom_call_target="tpu_custom_call" | custom-call | tf_op jit(solution)/shard_map/inputs/pallas_call | solution.py:56
  77.8 1.9 %collective-permute-start.5 = (bf16[256,2304]{1,0:T(8,128)(2,1)S(1)}, bf16[256,2304]{1,0:T(8,128)(2,1)S(1)}, u32[]{:S(2)}, u32[]{:S(2)}) collective-permute-start(bf16[256,2304]{1,0:T(8,128)(2,1)S(1)} %get-tuple-element.31), channel_id=1, source_target_pairs={{0,1},{1,0},{2,3},{3,2},{4,5},{5,4},{6,7},{7,6},{8,9},{9,8},{10,11... | collective-permute-start | bytes 3538952 | tf_op jit(solution)/shard_map/ppermute | solution.py:47
  79.8 3.1 %collective-permute-start.3 = (bf16[288,576]{1,0:T(8,128)(2,1)S(1)}, bf16[288,576]{1,0:T(8,128)(2,1)S(1)}, u32[]{:S(2)}, u32[]{:S(2)}) collective-permute-start(bf16[288,576]{1,0:T(8,128)(2,1)S(1)} %get-tuple-element.27), channel_id=1, source_target_pairs={{0,64},{1,449},{32,96},{33,481},{64,128},{65,1},{96,160},{97,33},{... | collective-permute-start | bytes 995336 | tf_op jit(solution)/shard_map/ppermute | solution.py:161
  82.9 6.1 %collective-permute-start.4 = (bf16[288,576]{1,0:T(8,128)(2,1)S(1)}, bf16[288,576]{1,0:T(8,128)(2,1)S(1)}, u32[]{:S(2)}, u32[]{:S(2)}) collective-permute-start(bf16[288,576]{1,0:T(8,128)(2,1)S(1)} %get-tuple-element.28), channel_id=1, source_target_pairs={{0,448},{1,65},{32,480},{33,97},{64,0},{65,129},{96,32},{97,161},{... | collective-permute-start | bytes 995336 | tf_op jit(solution)/shard_map/ppermute | solution.py:161
  89.0 1.7 %convert_add_fusion = f32[256,2304]{1,0:T(8,128)} fusion(f32[256,2304]{1,0:T(8,128)S(1)} %get-tuple-element.30, bf16[256,2304]{1,0:T(8,128)(2,1)S(1)} %collective-permute-done.5), kind=kLoop, calls=%fused_computation | loop fusion | flops 1179648 | bytes 5898240 | tf_op jit(solution)/shard_map/add | solution.py:216
  90.7 1.9 %collective-permute-done.3.arrived = bf16[288,576]{1,0:T(8,128)(2,1)S(1)} collective-permute-done((bf16[288,576]{1,0:T(8,128)(2,1)S(1)}, bf16[288,576]{1,0:T(8,128)(2,1)S(1)}, u32[]{:S(2)}, u32[]{:S(2)}) %collective-permute-start.3) | collective-permute-done | bytes 331808 | tf_op jit(solution)/shard_map/ppermute | solution.py:161
  92.6 0.7 copy-done.3
  93.3 2.1 %collective-permute-done.4.arrived = bf16[288,576]{1,0:T(8,128)(2,1)S(1)} collective-permute-done((bf16[288,576]{1,0:T(8,128)(2,1)S(1)}, bf16[288,576]{1,0:T(8,128)(2,1)S(1)}, u32[]{:S(2)}, u32[]{:S(2)}) %collective-permute-start.4) | collective-permute-done | bytes 331808 | tf_op jit(solution)/shard_map/ppermute | solution.py:161
  95.5 1.0 copy-done.4
  96.5 0.4 add_term.5
  96.9 1.9 %collective-permute-start.6 = (bf16[288,576]{1,0:T(8,128)(2,1)S(1)}, bf16[288,576]{1,0:T(8,128)(2,1)S(1)}, u32[]{:S(2)}, u32[]{:S(2)}) collective-permute-start(bf16[288,576]{1,0:T(8,128)(2,1)S(1)} %add_term.5), channel_id=1, source_target_pairs={{0,64},{1,449},{32,96},{33,481},{64,128},{65,1},{96,160},{97,33},{... | collective-permute-start | bytes 995336 | tf_op jit(solution)/shard_map/ppermute | solution.py:161
  98.8 0.4 add_term.8
  99.2 5.6 %collective-permute-start.11 = (bf16[288,576]{1,0:T(8,128)(2,1)S(1)}, bf16[288,576]{1,0:T(8,128)(2,1)S(1)}, u32[]{:S(2)}, u32[]{:S(2)}) collective-permute-start(bf16[288,576]{1,0:T(8,128)(2,1)S(1)} %add_term.8), channel_id=1, source_target_pairs={{0,448},{1,65},{32,480},{33,97},{64,0},{65,129},{96,32},{97,161},{... | collective-permute-start | bytes 995336 | tf_op jit(solution)/shard_map/ppermute | solution.py:161
  104.8 0.4 middle.1
  105.2 2.8 %collective-permute-done.6.arrived = bf16[288,576]{1,0:T(8,128)(2,1)S(1)} collective-permute-done((bf16[288,576]{1,0:T(8,128)(2,1)S(1)}, bf16[288,576]{1,0:T(8,128)(2,1)S(1)}, u32[]{:S(2)}, u32[]{:S(2)}) %collective-permute-start.6) | collective-permute-done | bytes 331808 | tf_op jit(solution)/shard_map/ppermute | solution.py:161
  108.0 0.4 add_term.6
  108.4 1.9 %collective-permute-start.7 = (bf16[288,576]{1,0:T(8,128)(2,1)S(1)}, bf16[288,576]{1,0:T(8,128)(2,1)S(1)}, u32[]{:S(2)}, u32[]{:S(2)}) collective-permute-start(bf16[288,576]{1,0:T(8,128)(2,1)S(1)} %add_term.6), channel_id=1, source_target_pairs={{0,64},{1,449},{32,96},{33,481},{64,128},{65,1},{96,160},{97,33},{... | collective-permute-start | bytes 995336 | tf_op jit(solution)/shard_map/ppermute | solution.py:161
  110.4 4.0 %collective-permute-start.8 = (bf16[144,576]{1,0:T(8,128)(2,1)S(1)}, bf16[144,576]{1,0:T(8,128)(2,1)S(1)}, u32[]{:S(2)}, u32[]{:S(2)}) collective-permute-start(bf16[144,576]{1,0:T(8,128)(2,1)S(1)} %select_convert_fusion), channel_id=1, source_target_pairs={{0,32},{32,0},{1,33},{33,1},{2,34},{34,2},{3,35},{35,3},{4,36},{36... | collective-permute-start | bytes 497672 | tf_op jit(solution)/shard_map/ppermute | solution.py:47
  114.4 0.4 add_term.9
  114.9 7.8 %collective-permute-start.13 = (bf16[144,576]{1,0:T(8,128)(2,1)S(1)}, bf16[144,576]{1,0:T(8,128)(2,1)S(1)}, u32[]{:S(2)}, u32[]{:S(2)}) collective-permute-start(bf16[144,576]{1,0:T(8,128)(2,1)S(1)} %get-tuple-element.59), channel_id=1, source_target_pairs={{0,480},{1,97},{32,448},{33,65},{64,32},{65,161},{96,0},{97,129},{... | collective-permute-start | bytes 497672 | tf_op jit(solution)/shard_map/ppermute | solution.py:161
  122.7 3.9 %collective-permute-start.12 = (bf16[144,576]{1,0:T(8,128)(2,1)S(1)}, bf16[144,576]{1,0:T(8,128)(2,1)S(1)}, u32[]{:S(2)}, u32[]{:S(2)}) collective-permute-start(bf16[144,576]{1,0:T(8,128)(2,1)S(1)} %get-tuple-element.60), channel_id=1, source_target_pairs={{0,448},{1,65},{32,480},{33,97},{64,0},{65,129},{96,32},{97,161},{... | collective-permute-start | bytes 497672 | tf_op jit(solution)/shard_map/ppermute | solution.py:161
  126.7 0.4 add_term.7
  127.1 3.6 %collective-permute-start.10 = (bf16[144,576]{1,0:T(8,128)(2,1)S(1)}, bf16[144,576]{1,0:T(8,128)(2,1)S(1)}, u32[]{:S(2)}, u32[]{:S(2)}) collective-permute-start(bf16[144,576]{1,0:T(8,128)(2,1)S(1)} %get-tuple-element.61), channel_id=1, source_target_pairs={{0,96},{1,481},{32,64},{33,449},{64,160},{65,33},{96,128},{97,1},{... | collective-permute-start | bytes 497672 | tf_op jit(solution)/shard_map/ppermute | solution.py:161
  130.7 1.9 %collective-permute-start.9 = (bf16[144,576]{1,0:T(8,128)(2,1)S(1)}, bf16[144,576]{1,0:T(8,128)(2,1)S(1)}, u32[]{:S(2)}, u32[]{:S(2)}) collective-permute-start(bf16[144,576]{1,0:T(8,128)(2,1)S(1)} %get-tuple-element.62), channel_id=1, source_target_pairs={{0,64},{1,449},{32,96},{33,481},{64,128},{65,1},{96,160},{97,33},{... | collective-permute-start | bytes 497672 | tf_op jit(solution)/shard_map/ppermute | solution.py:161
  132.7 5.7 %collective-permute-done.10 = bf16[144,576]{1,0:T(8,128)(2,1)S(1)} collective-permute-done((bf16[144,576]{1,0:T(8,128)(2,1)S(1)}, bf16[144,576]{1,0:T(8,128)(2,1)S(1)}, u32[]{:S(2)}, u32[]{:S(2)}) %collective-permute-start.10) | collective-permute-done | bytes 165920 | tf_op jit(solution)/shard_map/ppermute | solution.py:161
  138.3 1.1 collective-permute-done.9
  139.4 4.9 %all-to-all-start.1 = ((f32[4,8,2304]{2,1,0:T(8,128)}), f32[4,8,2304]{2,1,0:T(8,128)S(1)}, u32[]{:S(2)}, u32[]{:S(2)}) async-start(f32[4,8,2304]{2,1,0:T(8,128)} %bitcast.36), calls=%async_computation.2 | async-start | bytes 589824 | tf_op jit(solution)/shard_map/all_to_all | solution.py:238
  144.3 1.1 fusion.10
  145.7 0.6 copy-done.5
  146.6 1.2 fusion.6
  147.8 1.2 fusion.3
  149.0 0.7 all-to-all-done.1
  149.7 0.6 reduce_sum.9
  (58 shorter events, 2.6 us)
Async XLA Ops:
  7.2 64.0 %all-gather.2.cloned.1.call-start = ((), (), s32[]{:S(2)}) async-start(), calls=%async_computation.3 | async-start | bytes 3317760 | tf_op jit(solution)/shard_map/all_gather | solution.py:173
  8.6 10.8 %copy-start.13 = (bf16[8,2304]{1,0:T(8,128)(2,1)S(1)}, bf16[8,2304]{1,0:T(8,128)(2,1)}, u32[]{:S(2)}) copy-start(bf16[8,2304]{1,0:T(8,128)(2,1)} %param.11) | copy-start | bytes 110596
  8.6 9.8 %collective-permute-start.2 = (bf16[144,576]{1,0:T(8,128)(2,1)S(1)}, bf16[144,576]{1,0:T(8,128)(2,1)S(1)}, u32[]{:S(2)}, u32[]{:S(2)}) collective-permute-start(bf16[144,576]{1,0:T(8,128)(2,1)S(1)} %broadcast_select_fusion.8), channel_id=1, source_target_pairs={{0,32},{32,0},{1,33},{33,1},{2,34},{34,2},{3,35},{35,3},{4,36},{36... | collective-permute-start | bytes 497672 | tf_op jit(solution)/shard_map/ppermute | solution.py:47
  20.5 11.1 %copy-start.11 = (bf16[256,576]{0,1:T(8,128)(2,1)S(1)}, bf16[256,576]{0,1:T(8,128)(2,1)}, u32[]{:S(2)}) copy-start(bf16[256,576]{0,1:T(8,128)(2,1)} %param.12) | copy-start | bytes 884740
  20.5 11.3 %copy-start.15 = (s32[256]{0:T(256)S(1)}, s32[256]{0:T(256)}, u32[]{:S(2)}) copy-start(s32[256]{0:T(256)} %param.13) | copy-start | bytes 3076
  20.5 11.3 %copy-start.14 = (s32[576]{0:T(1024)S(1)}, s32[576]{0:T(1024)}, u32[]{:S(2)}) copy-start(s32[576]{0:T(1024)} %param.14) | copy-start | bytes 6916
  20.5 40.4 %all-to-all-start = ((bf16[32,8,2304]{2,1,0:T(8,128)(2,1)}), bf16[32,8,2304]{2,1,0:T(8,128)(2,1)S(1)}, u32[]{:S(2)}, u32[]{:S(2)}) async-start(bf16[32,8,2304]{2,1,0:T(8,128)(2,1)} %broadcast_in_dim.4), calls=%async_computation | async-start | bytes 2359296 | tf_op jit(solution)/shard_map/all_to_all | solution.py:178
  30.9 108.5 %reduce-scatter.2.cloned.1.call-start = ((), (), s32[]{:S(2)}) async-start(), calls=%async_computation.4 | async-start | bytes 2654208 | tf_op jit(solution)/shard_map/reduce_scatter | solution.py:220
  32.3 12.2 %collective-permute-start = (bf16[256,288]{1,0:T(8,128)(2,1)S(1)}, bf16[256,288]{1,0:T(8,128)(2,1)S(1)}, u32[]{:S(2)}, u32[]{:S(2)}) collective-permute-start(bf16[256,288]{1,0:T(8,128)(2,1)S(1)} %broadcast_select_fusion), channel_id=1, source_target_pairs={{0,32},{32,0},{1,33},{33,1},{2,34},{34,2},{3,35},{35,3},{4,36},{36... | collective-permute-start | bytes 442376 | tf_op jit(solution)/shard_map/ppermute | solution.py:47
  60.9 4.9 %collective-permute-start.1 = (bf16[256,2304]{1,0:T(8,128)(2,1)S(1)}, bf16[256,2304]{1,0:T(8,128)(2,1)}, u32[]{:S(2)}, u32[]{:S(2)}) collective-permute-start(bf16[256,2304]{1,0:T(8,128)(2,1)S(1)} %bitcast.30), channel_id=1, source_target_pairs={{0,1},{1,0},{2,3},{3,2},{4,5},{5,4},{6,7},{7,6},{8,9},{9,8},{10,11... | collective-permute-start | bytes 3538952 | tf_op jit(solution)/shard_map/ppermute | solution.py:47
  71.1 1.8 %copy-start = (bf16[2304,576]{1,0:T(8,128)(2,1)S(1)}, bf16[2304,576]{1,0:T(8,128)(2,1)}, u32[]{:S(2)}) copy-start(bf16[2304,576]{1,0:T(8,128)(2,1)} %all-gather.2.cloned.1.call-done.weights) | copy-start | bytes 7962628
  77.8 11.2 %collective-permute-start.5 = (bf16[256,2304]{1,0:T(8,128)(2,1)S(1)}, bf16[256,2304]{1,0:T(8,128)(2,1)S(1)}, u32[]{:S(2)}, u32[]{:S(2)}) collective-permute-start(bf16[256,2304]{1,0:T(8,128)(2,1)S(1)} %get-tuple-element.31), channel_id=1, source_target_pairs={{0,1},{1,0},{2,3},{3,2},{4,5},{5,4},{6,7},{7,6},{8,9},{9,8},{10,11... | collective-permute-start | bytes 3538952 | tf_op jit(solution)/shard_map/ppermute | solution.py:47
  79.8 12.8 %collective-permute-start.3 = (bf16[288,576]{1,0:T(8,128)(2,1)S(1)}, bf16[288,576]{1,0:T(8,128)(2,1)S(1)}, u32[]{:S(2)}, u32[]{:S(2)}) collective-permute-start(bf16[288,576]{1,0:T(8,128)(2,1)S(1)} %get-tuple-element.27), channel_id=1, source_target_pairs={{0,64},{1,449},{32,96},{33,481},{64,128},{65,1},{96,160},{97,33},{... | collective-permute-start | bytes 995336 | tf_op jit(solution)/shard_map/ppermute | solution.py:161
  82.9 12.6 %collective-permute-start.4 = (bf16[288,576]{1,0:T(8,128)(2,1)S(1)}, bf16[288,576]{1,0:T(8,128)(2,1)S(1)}, u32[]{:S(2)}, u32[]{:S(2)}) collective-permute-start(bf16[288,576]{1,0:T(8,128)(2,1)S(1)} %get-tuple-element.28), channel_id=1, source_target_pairs={{0,448},{1,65},{32,480},{33,97},{64,0},{65,129},{96,32},{97,161},{... | collective-permute-start | bytes 995336 | tf_op jit(solution)/shard_map/ppermute | solution.py:161
  92.6 0.7 copy-start.3
  95.5 1.0 copy-start.4
  96.9 11.2 %collective-permute-start.6 = (bf16[288,576]{1,0:T(8,128)(2,1)S(1)}, bf16[288,576]{1,0:T(8,128)(2,1)S(1)}, u32[]{:S(2)}, u32[]{:S(2)}) collective-permute-start(bf16[288,576]{1,0:T(8,128)(2,1)S(1)} %add_term.5), channel_id=1, source_target_pairs={{0,64},{1,449},{32,96},{33,481},{64,128},{65,1},{96,160},{97,33},{... | collective-permute-start | bytes 995336 | tf_op jit(solution)/shard_map/ppermute | solution.py:161
  99.2 15.2 %collective-permute-start.11 = (bf16[288,576]{1,0:T(8,128)(2,1)S(1)}, bf16[288,576]{1,0:T(8,128)(2,1)S(1)}, u32[]{:S(2)}, u32[]{:S(2)}) collective-permute-start(bf16[288,576]{1,0:T(8,128)(2,1)S(1)} %add_term.8), channel_id=1, source_target_pairs={{0,448},{1,65},{32,480},{33,97},{64,0},{65,129},{96,32},{97,161},{... | collective-permute-start | bytes 995336 | tf_op jit(solution)/shard_map/ppermute | solution.py:161
  105.2 5.2 %copy-start.1 = (f32[288,576]{1,0:T(8,128)}, f32[288,576]{1,0:T(8,128)S(1)}, u32[]{:S(2)}) copy-start(f32[288,576]{1,0:T(8,128)S(1)} %middle.1) | copy-start | bytes 1990660
  108.4 18.2 %collective-permute-start.7 = (bf16[288,576]{1,0:T(8,128)(2,1)S(1)}, bf16[288,576]{1,0:T(8,128)(2,1)S(1)}, u32[]{:S(2)}, u32[]{:S(2)}) collective-permute-start(bf16[288,576]{1,0:T(8,128)(2,1)S(1)} %add_term.6), channel_id=1, source_target_pairs={{0,64},{1,449},{32,96},{33,481},{64,128},{65,1},{96,160},{97,33},{... | collective-permute-start | bytes 995336 | tf_op jit(solution)/shard_map/ppermute | solution.py:161
  110.4 16.2 %collective-permute-start.8 = (bf16[144,576]{1,0:T(8,128)(2,1)S(1)}, bf16[144,576]{1,0:T(8,128)(2,1)S(1)}, u32[]{:S(2)}, u32[]{:S(2)}) collective-permute-start(bf16[144,576]{1,0:T(8,128)(2,1)S(1)} %select_convert_fusion), channel_id=1, source_target_pairs={{0,32},{32,0},{1,33},{33,1},{2,34},{34,2},{3,35},{35,3},{4,36},{36... | collective-permute-start | bytes 497672 | tf_op jit(solution)/shard_map/ppermute | solution.py:47
  114.9 17.8 %collective-permute-start.13 = (bf16[144,576]{1,0:T(8,128)(2,1)S(1)}, bf16[144,576]{1,0:T(8,128)(2,1)S(1)}, u32[]{:S(2)}, u32[]{:S(2)}) collective-permute-start(bf16[144,576]{1,0:T(8,128)(2,1)S(1)} %get-tuple-element.59), channel_id=1, source_target_pairs={{0,480},{1,97},{32,448},{33,65},{64,32},{65,161},{96,0},{97,129},{... | collective-permute-start | bytes 497672 | tf_op jit(solution)/shard_map/ppermute | solution.py:161
  122.7 9.9 %collective-permute-start.12 = (bf16[144,576]{1,0:T(8,128)(2,1)S(1)}, bf16[144,576]{1,0:T(8,128)(2,1)S(1)}, u32[]{:S(2)}, u32[]{:S(2)}) collective-permute-start(bf16[144,576]{1,0:T(8,128)(2,1)S(1)} %get-tuple-element.60), channel_id=1, source_target_pairs={{0,448},{1,65},{32,480},{33,97},{64,0},{65,129},{96,32},{97,161},{... | collective-permute-start | bytes 497672 | tf_op jit(solution)/shard_map/ppermute | solution.py:161
  127.1 17.2 %copy-start.2 = (f32[288,576]{1,0:T(8,128)S(1)}, f32[288,576]{1,0:T(8,128)}, u32[]{:S(2)}) copy-start(f32[288,576]{1,0:T(8,128)} %copy-done.1) | copy-start | bytes 1990660
  127.1 11.2 %collective-permute-start.10 = (bf16[144,576]{1,0:T(8,128)(2,1)S(1)}, bf16[144,576]{1,0:T(8,128)(2,1)S(1)}, u32[]{:S(2)}, u32[]{:S(2)}) collective-permute-start(bf16[144,576]{1,0:T(8,128)(2,1)S(1)} %get-tuple-element.61), channel_id=1, source_target_pairs={{0,96},{1,481},{32,64},{33,449},{64,160},{65,33},{96,128},{97,1},{... | collective-permute-start | bytes 497672 | tf_op jit(solution)/shard_map/ppermute | solution.py:161
  130.7 8.7 %collective-permute-start.9 = (bf16[144,576]{1,0:T(8,128)(2,1)S(1)}, bf16[144,576]{1,0:T(8,128)(2,1)S(1)}, u32[]{:S(2)}, u32[]{:S(2)}) collective-permute-start(bf16[144,576]{1,0:T(8,128)(2,1)S(1)} %get-tuple-element.62), channel_id=1, source_target_pairs={{0,64},{1,449},{32,96},{33,481},{64,128},{65,1},{96,160},{97,33},{... | collective-permute-start | bytes 497672 | tf_op jit(solution)/shard_map/ppermute | solution.py:161
  132.7 5.7 %copy-start.12 = (bf16[144,576]{1,0:T(8,128)(2,1)}, bf16[144,576]{1,0:T(8,128)(2,1)S(1)}, u32[]{:S(2)}) copy-start(bf16[144,576]{1,0:T(8,128)(2,1)S(1)} %collective-permute-done.12) | copy-start | bytes 497668
  139.4 10.3 %all-to-all-start.1 = ((f32[4,8,2304]{2,1,0:T(8,128)}), f32[4,8,2304]{2,1,0:T(8,128)S(1)}, u32[]{:S(2)}, u32[]{:S(2)}) async-start(f32[4,8,2304]{2,1,0:T(8,128)} %bitcast.36), calls=%async_computation.2 | async-start | bytes 589824 | tf_op jit(solution)/shard_map/all_to_all | solution.py:238
  145.4 0.9 copy-start.5
  145.4 1.1 copy-start.7
  145.4 1.2 copy-start.8
  145.7 2.1 %copy-start.6 = (bf16[144,576]{1,0:T(8,128)(2,1)S(1)}, bf16[144,576]{1,0:T(8,128)(2,1)}, u32[]{:S(2)}) copy-start(bf16[144,576]{1,0:T(8,128)(2,1)} %param.16) | copy-start | bytes 497668
  145.7 2.1 %copy-start.9 = (f32[144,576]{1,0:T(8,128)S(1)}, f32[144,576]{1,0:T(8,128)}, u32[]{:S(2)}) copy-start(f32[144,576]{1,0:T(8,128)} %param.18) | copy-start | bytes 995332
  145.7 2.1 %copy-start.10 = (f32[144,576]{1,0:T(8,128)S(1)}, f32[144,576]{1,0:T(8,128)}, u32[]{:S(2)}) copy-start(f32[144,576]{1,0:T(8,128)} %param.19) | copy-start | bytes 995332
Sparse Core Ops, SparseCore 0:
  19.5 51.6 all-gather.1
  95.6 41.9 reduce-scatter.1

commit v5 on v4

--- a/solution.py
+++ b/solution.py
@@ -51,7 +51,7 @@
     return jnp.where(index == 0, first, second), jnp.where(index == 0, second, first)
 
 
-def in_vmem(kernel, outs, name):
+def in_vmem(kernel, outs, name, scratch=()):
     def call(scalar, *arrays):
         return pl.pallas_call(
             kernel,
@@ -59,6 +59,7 @@
             in_specs=[pl.BlockSpec(memory_space=pltpu.SMEM)]
             + [pl.BlockSpec(memory_space=pltpu.VMEM)] * len(arrays),
             out_specs=[pl.BlockSpec(memory_space=pltpu.VMEM)] * len(outs),
+            scratch_shapes=scratch,
             compiler_params=pltpu.CompilerParams(vmem_limit_bytes=24 * 1024 * 1024),
             name=name,
         )(scalar, *arrays)
@@ -68,7 +69,7 @@
 
 def block_product(place_ref, step, depth, turned_ref, turned_other_ref, dboth_ref):
     size = turned_ref.shape[0] // depth
-    place, core = place_ref[0] >> 1, place_ref[0] & 1
+    place, core = place_ref[0] >> 2, place_ref[0] >> 1 & 1
     spot = lax.rem(place + (1 - 2 * core) * step + depth, depth)
     span = pl.ds(pl.multiple_of(spot * size, 16), size)
     tokens = turned_ref.shape[1]
@@ -109,8 +110,11 @@
         out[...] = term.astype(bf16)
 
 
-def middle_kernel(depth, place_ref, turned, turned_other, dboth, total):
-    total[...] = block_product(place_ref, 0, depth, turned, turned_other, dboth)
+def halves_of(place_ref, rows):
+    xh = place_ref[0] & 1
+    return pl.ds(pl.multiple_of(xh * rows, 16), rows), pl.ds(
+        pl.multiple_of((1 - xh) * rows, 16), rows
+    )
 
 
 def hop_kernel(depth, step, place_ref, arrived, turned, turned_other, dboth, total):
@@ -118,15 +122,41 @@
     total[...] = (arrived[...].astype(f32) + term).astype(total.dtype)
 
 
-def inputs_kernel(place_ref, dboth, weights, core_part, other_part):
-    half = core_part.shape[0]
-    over_units = (((1,), (1,)), ((), ()))
-    other_part[...] = lax.dot_general(
-        dboth[half:, :], weights[...], over_units, preferred_element_type=f32
-    ).astype(bf16)
-    core_part[...] = lax.dot_general(
-        dboth[:half, :], weights[...], over_units, preferred_element_type=f32
-    )
+def hop_with_own_kernel(
+    depth, step, place_ref, arrived, turned, turned_other, dboth, total, own_sum, scratch
+):
+    size, rows = arrived.shape[0], own_sum.shape[0]
+    term = block_product(place_ref, step, depth, turned, turned_other, dboth)
+    total[:size, :] = (arrived[...].astype(f32) + term).astype(bf16)
+    scratch[...] = block_product(place_ref, 0, depth, turned, turned_other, dboth)
+    own, partner = halves_of(place_ref, rows)
+    own_sum[...] = scratch[own, :]
+    total[size:, :] = scratch[partner, :].astype(bf16)
+
+
+def last_hop_kernel(
+    depth, step, place_ref, arrived, turned, turned_other, dboth, *refs
+):
+    *extra, own_out, partner_out, scratch = refs
+    size, rows = scratch.shape[0], own_out.shape[0]
+    term = block_product(place_ref, step, depth, turned, turned_other, dboth)
+    scratch[...] = arrived[:size, :].astype(f32) + term
+    own, partner = halves_of(place_ref, rows)
+    own_out[...] = scratch[own, :].astype(bf16)
+    total = scratch[partner, :]
+    for ref in extra:
+        total = total + ref[size:, :].astype(f32)
+    partner_out[...] = total.astype(bf16)
+
+
+def inputs_kernel(half, place_ref, dboth, weights, out):
+    tokens = out.shape[0]
+    out[...] = lax.dot_general(
+        dboth[half * tokens : (half + 1) * tokens, :],
+        weights[...],
+        (((1,), (1,)), ((), ())),
+        preferred_element_type=f32,
+    ).astype(out.dtype)
 
 
 def on_device(
@@ -190,7 +220,7 @@
     core_rows, kept = lax.optimization_barrier((core_rows, kept))
     far = depth // 2
     tokens = kept.shape[0]
-    place = (2 * lax.axis_index("z") + core).reshape(1)
+    place = (4 * lax.axis_index("z") + 2 * core + xh).reshape(1)
     block = (pair_rows, own_units)
     turn = in_vmem(turn_kernel, [jax.ShapeDtypeStruct((model, tokens // 2), bf16)], "turn")
     turned = turn(place, core_rows)[0]
@@ -201,47 +231,56 @@
         "forward",
     )(place, turned, turned_other, weights, kept)
 
+    rows_block, wide = (own_rows, own_units), pltpu.VMEM(block, f32)
+
+    def hop(kernel, step, outs, scratch, arrived, *extra):
+        return in_vmem(
+            functools.partial(kernel, depth, step),
+            [jax.ShapeDtypeStruct(shape, dtype) for shape, dtype in outs],
+            "hop",
+            scratch,
+        )(place, arrived, turned, turned_other, dboth, *extra)
+
     def add_term(arrived, step):
+        return hop(hop_kernel, step, [(block, bf16)], (), arrived)[0]
+
+    def last(arrived, step, way, *extra):
+        outs = [(rows_block, bf16)] * 2
+        own, partner = hop(last_hop_kernel, step, outs, [wide], arrived, *extra)
+        return along(own, way), across(partner, way)
+
+    def back_product(part, dtype):
         return in_vmem(
-            functools.partial(hop_kernel, depth, step),
-            [jax.ShapeDtypeStruct(block, bf16)],
-            "add_term",
-        )(place, arrived, turned, turned_other, dboth)[0]
-
-    core_part, other_part = in_vmem(
-        inputs_kernel,
-        [jax.ShapeDtypeStruct((tokens // 2, model), dtype) for dtype in (f32, bf16)],
-        "inputs",
-    )(place, dboth, weights)
-    pair = core_part + swap(other_part, "core").astype(f32)
+            functools.partial(inputs_kernel, part),
+            [jax.ShapeDtypeStruct((tokens // 2, model), dtype)],
+            "inputs",
+        )(place, dboth, weights)[0]
+
+    other_part = swap(back_product(1, bf16), "core")
+    pair = back_product(0, f32) + other_part.astype(f32)
 
     forth, back = along(forth, 1), along(back, -1)
-    forth, back, pair, dboth = lax.optimization_barrier((forth, back, pair, dboth))
+    forth, back, dboth = lax.optimization_barrier((forth, back, dboth))
     columns = lax.psum_scatter(pair.reshape(across_y, -1, model), "y", scatter_dimension=0)
-    middle = in_vmem(
-        functools.partial(middle_kernel, depth), [jax.ShapeDtypeStruct(block, f32)], "middle"
-    )(place, turned, turned_other, dboth)[0]
-    own_sum, partner_sum = pick(xh, middle[:own_rows], middle[own_rows:])
-    got_sum = swap(partner_sum.astype(bf16), "xh")
-
-    def last(message, step):
-        own, partner = pick(xh, message[:own_rows], message[own_rows:])
-        return along(own, step), across(partner, step)
-
-    for step in range(far - 1, 1, -1):
+    forth = along(add_term(forth, far - 1), 1)
+    message = (pair_rows + own_rows, own_units)
+    back, own_sum = hop(
+        hop_with_own_kernel, 2 - far, [(message, bf16), (rows_block, f32)], [wide], back
+    )
+    back = along(back, -1)
+    returned = back
+    for step in range(far - 2, 1, -1):
         forth = along(add_term(forth, step), 1)
-        back = add_term(back, 1 - step)
-        back = along(back, -1) if step > 2 else last(back, -1)
-    forth, got_sum = lax.optimization_barrier((forth, got_sum))
-    forth = last(add_term(forth, 1), 1)
-    columns, *arrived = lax.optimization_barrier((columns, *forth, *back))
+        back = last(back, 1 - step, -1) if step == 2 else along(add_term(back, 1 - step), -1)
+    forth = last(forth, 1, 1, returned)
+    columns, *back = lax.optimization_barrier((columns, *back))
     shares = lax.all_to_all(
         columns.reshape(4, own_inputs, model), ("xh", "xl"), split_axis=0, concat_axis=0
     )
     input_grad = jnp.sum(shares, axis=0).astype(bf16)
-    own_forth, partner_forth, own_back, partner_back = (x.astype(f32) for x in arrived)
+    own_forth, partner_forth, own_back, partner_back = (x.astype(f32) for x in (*forth, *back))
     own_sum = own_sum + own_forth + own_back
-    got_sum = got_sum.astype(f32) + partner_forth + partner_back
+    got_sum = partner_forth + partner_back
 
     low_sum, high_sum = pick(xh, own_sum, got_sum)
     grad_gate = jnp.concatenate([low_sum[:, :half], high_sum[:, :half]], axis=1)

time: 158 us -> 155 us (0.981)
  starting transfers between devices: 67.1 us -> 61.3 us
  waiting for transfers between devices: 50.4 us -> 52.4 us
    ppermute x5 -> x4, starting transfers between devices: 15.8 us -> 11.8 us  [swap(): return lax.ppermute(x, axis, [(0, 1), (1, 0)])]
    ppermute x9, starting transfers between devices: 35.9 us -> 34 us  [ring(): return lax.ppermute(x, ('z', 'xh', 'core'), pairs)]
    ppermute x5 -> x4, waiting for transfers between devices: 16.5 us -> 18.2 us  [swap(): return lax.ppermute(x, axis, [(0, 1), (1, 0)])]
    unnamed x33 -> x31, local copies, waits for them, and re-layouts: 4.7 us -> 4.37 us
  transfers between devices with their start and end apart: 18 -> 17, of which waited for: 11 -> 11; matrix products, arithmetic and copies ran while one was open for 5% -> 4% of each run, Pallas kernels for 3% -> 4%
where the time goes in v5:
time: 155 us; the launch traced here: 154 us
  starting transfers between devices  61.3 us (40%)
  waiting for transfers between devices  52.4 us (34%)
  between operations  15.1 us (10%)
  Pallas kernels  10.3 us (7%)
  other arithmetic  7.75 us (5%)
  local copies, waits for them, and re-layouts  6.96 us (4%)
    ppermute x9, starting transfers between devices, ring(): return lax.ppermute(x, ('z', 'xh', 'core'), pairs)  34 us
    ppermute x4, waiting for transfers between devices, swap(): return lax.ppermute(x, axis, [(0, 1), (1, 0)])  18.2 us
    all_to_all x1, waiting for transfers between devices, on_device(): lax.all_to_all(spread, plane, split_axis=0, concat_axis=0)  15.9 us
    ppermute x9, waiting for transfers between devices, ring(): return lax.ppermute(x, ('z', 'xh', 'core'), pairs)  14.5 us
    ppermute x4, starting transfers between devices, swap(): return lax.ppermute(x, axis, [(0, 1), (1, 0)])  11.8 us
    all_to_all x1, starting transfers between devices, on_device(): lax.all_to_all(spread, plane, split_axis=0, concat_axis=0)  10.4 us
    pallas_call x10, Pallas kernels, call(): pl.pallas_call(kernel, out_shape=outs, in_specs=[pl.BlockSpec(memory_spac...  10.3 us
    all_to_all x1, starting transfers between devices, on_device(): lax.all_to_all(columns.reshape(4, own_inputs, model), ('xh', 'xl'), split...  5.01 us
  transfers between devices with their start and end apart: 17, of which 11 were waited for; matrix products, arithmetic and copies ran while one was open for 4% of the time, Pallas kernels for 4%

profile of v5, /device:TPU:2, one launch (start us, length us, event | category | flops | bytes accessed | tf_op | source)
XLA Modules:
  0.0 153.8 jit_solution(10385141601497177641)
XLA Ops:
  7.2 1.2 fusion.17
  8.6 4.0 %collective-permute-start.2 = (bf16[144,576]{1,0:T(8,128)(2,1)S(1)}, bf16[144,576]{1,0:T(8,128)(2,1)S(1)}, u32[]{:S(2)}, u32[]{:S(2)}) collective-permute-start(bf16[144,576]{1,0:T(8,128)(2,1)S(1)} %broadcast_select_fusion.4), channel_id=1, source_target_pairs={{0,32},{32,0},{1,33},{33,1},{2,34},{34,2},{3,35},{35,3},{4,36},{36... | collective-permute-start | bytes 497672 | tf_op jit(solution)/shard_map/ppermute | solution.py:47
  12.6 5.7 %collective-permute-done.2 = bf16[144,576]{1,0:T(8,128)(2,1)S(1)} collective-permute-done((bf16[144,576]{1,0:T(8,128)(2,1)S(1)}, bf16[144,576]{1,0:T(8,128)(2,1)S(1)}, u32[]{:S(2)}, u32[]{:S(2)}) %collective-permute-start.2) | collective-permute-done | bytes 165920 | tf_op jit(solution)/shard_map/ppermute | solution.py:47
  18.5 0.8 pad_maximum_fusion.2
  19.3 1.1 broadcast_in_dim.4
  20.5 10.4 %all-to-all-start = ((bf16[32,8,2304]{2,1,0:T(8,128)(2,1)}), bf16[32,8,2304]{2,1,0:T(8,128)(2,1)S(1)}, u32[]{:S(2)}, u32[]{:S(2)}) async-start(bf16[32,8,2304]{2,1,0:T(8,128)(2,1)} %broadcast_in_dim.4), calls=%async_computation | async-start | bytes 2359296 | tf_op jit(solution)/shard_map/all_to_all | solution.py:208
  31.8 0.4 fusion
  32.3 4.0 %collective-permute-start = (bf16[256,288]{1,0:T(8,128)(2,1)S(1)}, bf16[256,288]{1,0:T(8,128)(2,1)S(1)}, u32[]{:S(2)}, u32[]{:S(2)}) collective-permute-start(bf16[256,288]{1,0:T(8,128)(2,1)S(1)} %broadcast_select_fusion), channel_id=1, source_target_pairs={{0,32},{32,0},{1,33},{33,1},{2,34},{34,2},{3,35},{35,3},{4,36},{36... | collective-permute-start | bytes 442376 | tf_op jit(solution)/shard_map/ppermute | solution.py:47
  36.3 8.2 %collective-permute-done = bf16[256,288]{1,0:T(8,128)(2,1)S(1)} collective-permute-done((bf16[256,288]{1,0:T(8,128)(2,1)S(1)}, bf16[256,288]{1,0:T(8,128)(2,1)S(1)}, u32[]{:S(2)}, u32[]{:S(2)}) %collective-permute-start) | collective-permute-done | bytes 147488 | tf_op jit(solution)/shard_map/ppermute | solution.py:47
  45.0 15.9 %all-to-all-done = bf16[32,8,2304]{2,1,0:T(8,128)(2,1)S(1)} async-done(((bf16[32,8,2304]{2,1,0:T(8,128)(2,1)}), bf16[32,8,2304]{2,1,0:T(8,128)(2,1)S(1)}, u32[]{:S(2)}, u32[]{:S(2)}) %all-to-all-start) | async-done | bytes 1179680 | tf_op jit(solution)/shard_map/all_to_all | solution.py:208
  60.9 1.9 %collective-permute-start.1 = (bf16[256,2304]{1,0:T(8,128)(2,1)S(1)}, bf16[256,2304]{1,0:T(8,128)(2,1)}, u32[]{:S(2)}, u32[]{:S(2)}) collective-permute-start(bf16[256,2304]{1,0:T(8,128)(2,1)S(1)} %bitcast.30), channel_id=1, source_target_pairs={{0,1},{1,0},{2,3},{3,2},{4,5},{5,4},{6,7},{7,6},{8,9},{9,8},{10,11... | collective-permute-start | bytes 3538952 | tf_op jit(solution)/shard_map/ppermute | solution.py:47
  63.2 2.6 %collective-permute-done.1.rows = bf16[256,2304]{1,0:T(8,128)(2,1)} collective-permute-done((bf16[256,2304]{1,0:T(8,128)(2,1)S(1)}, bf16[256,2304]{1,0:T(8,128)(2,1)}, u32[]{:S(2)}, u32[]{:S(2)}) %collective-permute-start.1) | collective-permute-done | bytes 1179680 | tf_op jit(solution)/shard_map/ppermute | solution.py:47
  65.7 1.6 %turn.3.turned_other = bf16[2304,256]{1,0:T(8,128)(2,1)S(1)} custom-call(s32[1]{0:T(128)} %bitcast.place_ref, bf16[256,2304]{1,0:T(8,128)(2,1)} %collective-permute-done.1.rows), custom_call_target="tpu_custom_call" | custom-call | tf_op jit(solution)/shard_map/turn/pallas_call | solution.py:56
  67.4 3.8 %all-gather.2.cloned.1.call-done.weights = bf16[2304,576]{1,0:T(8,128)(2,1)} async-done(((bf16[288,576]{1,0:T(8,128)(2,1)}), bf16[2304,576]{1,0:T(8,128)(2,1)}) %all-gather.2.cloned.1.call-update) | async-done | bytes 2654224 | tf_op jit(solution)/shard_map/all_gather | solution.py:203
  71.2 1.8 %copy-done = bf16[2304,576]{1,0:T(8,128)(2,1)S(1)} copy-done((bf16[2304,576]{1,0:T(8,128)(2,1)S(1)}, bf16[2304,576]{1,0:T(8,128)(2,1)}, u32[]{:S(2)}) %copy-start) | copy-done | bytes 2654232
  73.0 2.8 %forward.1 = (bf16[512,576]{1,0:T(8,128)(2,1)S(1)}, bf16[288,576]{1,0:T(8,128)(2,1)S(1)}, bf16[288,576]{1,0:T(8,128)(2,1)S(1)}) custom-call(s32[1]{0:T(128)} %bitcast.place_ref, bf16[2304,256]{1,0:T(8,128)(2,1)S(1)} %turn.2.turned, bf16[2304,256]{1,0:T(8,128)(2,1)S(1)} %turn.3.turned_other, bf16[2304,576]{1,0:T(8,128)(2,1)S(1)} %copy-done, ...), custom_call_target="tpu_custom_call" | custom-call | tf_op jit(solution)/shard_map/forward/pallas_call | solution.py:56
  75.8 0.7 copy-done.3
  76.6 1.1 inputs.3
  77.7 1.9 %collective-permute-start.3 = (bf16[256,2304]{1,0:T(8,128)(2,1)S(1)}, bf16[256,2304]{1,0:T(8,128)(2,1)S(1)}, u32[]{:S(2)}, u32[]{:S(2)}) collective-permute-start(bf16[256,2304]{1,0:T(8,128)(2,1)S(1)} %inputs.3), channel_id=1, source_target_pairs={{0,1},{1,0},{2,3},{3,2},{4,5},{5,4},{6,7},{7,6},{8,9},{9,8},{10,11... | collective-permute-start | bytes 3538952 | tf_op jit(solution)/shard_map/ppermute | solution.py:47
  79.6 1.1 inputs.2
  80.8 1.7 %collective-permute-done.3 = bf16[256,2304]{1,0:T(8,128)(2,1)S(1)} collective-permute-done((bf16[256,2304]{1,0:T(8,128)(2,1)S(1)}, bf16[256,2304]{1,0:T(8,128)(2,1)S(1)}, u32[]{:S(2)}, u32[]{:S(2)}) %collective-permute-start.3) | collective-permute-done | bytes 1179680 | tf_op jit(solution)/shard_map/ppermute | solution.py:47
  82.5 1.6 %convert_add_fusion = f32[256,2304]{1,0:T(8,128)} fusion(f32[256,2304]{1,0:T(8,128)S(1)} %inputs.2, bf16[256,2304]{1,0:T(8,128)(2,1)S(1)} %collective-permute-done.3), kind=kLoop, calls=%fused_computation | loop fusion | flops 1179648 | bytes 5898240 | tf_op jit(solution)/shard_map/add | solution.py:260
  84.1 3.2 %collective-permute-start.4 = (bf16[288,576]{1,0:T(8,128)(2,1)}, bf16[288,576]{1,0:T(8,128)(2,1)S(1)}, u32[]{:S(2)}, u32[]{:S(2)}) collective-permute-start(bf16[288,576]{1,0:T(8,128)(2,1)} %copy-done.3), channel_id=1, source_target_pairs={{0,64},{1,449},{32,96},{33,481},{64,128},{65,1},{96,160},{97,33},{... | collective-permute-start | bytes 995336 | tf_op jit(solution)/shard_map/ppermute | solution.py:191
  87.4 6.0 %collective-permute-start.5 = (bf16[288,576]{1,0:T(8,128)(2,1)S(1)}, bf16[288,576]{1,0:T(8,128)(2,1)S(1)}, u32[]{:S(2)}, u32[]{:S(2)}) collective-permute-start(bf16[288,576]{1,0:T(8,128)(2,1)S(1)} %copy-done.2), channel_id=1, source_target_pairs={{0,448},{1,65},{32,480},{33,97},{64,0},{65,129},{96,32},{97,161},{... | collective-permute-start | bytes 995336 | tf_op jit(solution)/shard_map/ppermute | solution.py:191
  93.4 3.8 %collective-permute-done.4.arrived = bf16[288,576]{1,0:T(8,128)(2,1)S(1)} collective-permute-done((bf16[288,576]{1,0:T(8,128)(2,1)}, bf16[288,576]{1,0:T(8,128)(2,1)S(1)}, u32[]{:S(2)}, u32[]{:S(2)}) %collective-permute-start.4) | collective-permute-done | bytes 331808 | tf_op jit(solution)/shard_map/ppermute | solution.py:191
  97.2 2.6 %collective-permute-done.5.arrived = bf16[288,576]{1,0:T(8,128)(2,1)S(1)} collective-permute-done((bf16[288,576]{1,0:T(8,128)(2,1)S(1)}, bf16[288,576]{1,0:T(8,128)(2,1)S(1)}, u32[]{:S(2)}, u32[]{:S(2)}) %collective-permute-start.5) | collective-permute-done | bytes 331808 | tf_op jit(solution)/shard_map/ppermute | solution.py:191
  99.8 0.4 hop.7
  100.2 1.9 %collective-permute-start.9 = (bf16[288,576]{1,0:T(8,128)(2,1)S(1)}, bf16[288,576]{1,0:T(8,128)(2,1)S(1)}, u32[]{:S(2)}, u32[]{:S(2)}) collective-permute-start(bf16[288,576]{1,0:T(8,128)(2,1)S(1)} %hop.7), channel_id=1, source_target_pairs={{0,64},{1,449},{32,96},{33,481},{64,128},{65,1},{96,160},{97,33},{... | collective-permute-start | bytes 995336 | tf_op jit(solution)/shard_map/ppermute | solution.py:191
  102.1 0.7 hop.5
  102.8 5.6 %collective-permute-start.6 = (bf16[432,576]{1,0:T(8,128)(2,1)S(1)}, bf16[432,576]{1,0:T(8,128)(2,1)S(1)}, u32[]{:S(2)}, u32[]{:S(2)}) collective-permute-start(bf16[432,576]{1,0:T(8,128)(2,1)S(1)} %get-tuple-element.31), channel_id=1, source_target_pairs={{0,448},{1,65},{32,480},{33,97},{64,0},{65,129},{96,32},{97,161},{... | collective-permute-start | bytes 1493000 | tf_op jit(solution)/shard_map/ppermute | solution.py:191
  108.4 2.8 %collective-permute-done.9.arrived = bf16[288,576]{1,0:T(8,128)(2,1)S(1)} collective-permute-done((bf16[288,576]{1,0:T(8,128)(2,1)S(1)}, bf16[288,576]{1,0:T(8,128)(2,1)S(1)}, u32[]{:S(2)}, u32[]{:S(2)}) %collective-permute-start.9) | collective-permute-done | bytes 331808 | tf_op jit(solution)/shard_map/ppermute | solution.py:191
  111.3 0.4 hop.8
  111.7 1.9 %collective-permute-start.10 = (bf16[288,576]{1,0:T(8,128)(2,1)S(1)}, bf16[288,576]{1,0:T(8,128)(2,1)S(1)}, u32[]{:S(2)}, u32[]{:S(2)}) collective-permute-start(bf16[288,576]{1,0:T(8,128)(2,1)S(1)} %hop.8), channel_id=1, source_target_pairs={{0,64},{1,449},{32,96},{33,481},{64,128},{65,1},{96,160},{97,33},{... | collective-permute-start | bytes 995336 | tf_op jit(solution)/shard_map/ppermute | solution.py:191
  113.6 2.5 %collective-permute-done.6.arrived.refs_0_ = bf16[432,576]{1,0:T(8,128)(2,1)S(1)} collective-permute-done((bf16[432,576]{1,0:T(8,128)(2,1)S(1)}, bf16[432,576]{1,0:T(8,128)(2,1)S(1)}, u32[]{:S(2)}, u32[]{:S(2)}) %collective-permute-start.6) | collective-permute-done | bytes 497696 | tf_op jit(solution)/shard_map/ppermute | solution.py:191
  116.0 0.5 hop.6
  116.5 5.1 %collective-permute-start.7 = (bf16[144,576]{1,0:T(8,128)(2,1)S(1)}, bf16[144,576]{1,0:T(8,128)(2,1)S(1)}, u32[]{:S(2)}, u32[]{:S(2)}) collective-permute-start(bf16[144,576]{1,0:T(8,128)(2,1)S(1)} %get-tuple-element.32), channel_id=1, source_target_pairs={{0,448},{1,65},{32,480},{33,97},{64,0},{65,129},{96,32},{97,161},{... | collective-permute-start | bytes 497672 | tf_op jit(solution)/shard_map/ppermute | solution.py:191
  121.7 5.0 %collective-permute-start.8 = (bf16[144,576]{1,0:T(8,128)(2,1)S(1)}, bf16[144,576]{1,0:T(8,128)(2,1)}, u32[]{:S(2)}, u32[]{:S(2)}) collective-permute-start(bf16[144,576]{1,0:T(8,128)(2,1)S(1)} %get-tuple-element.33), channel_id=1, source_target_pairs={{0,480},{1,97},{32,448},{33,65},{64,32},{65,161},{96,0},{97,129},{... | collective-permute-start | bytes 497672 | tf_op jit(solution)/shard_map/ppermute | solution.py:191
  126.7 1.3 hop.9
  128.0 2.3 %collective-permute-start.11 = (bf16[144,576]{1,0:T(8,128)(2,1)}, bf16[144,576]{1,0:T(8,128)(2,1)S(1)}, u32[]{:S(2)}, u32[]{:S(2)}) collective-permute-start(bf16[144,576]{1,0:T(8,128)(2,1)} %get-tuple-element.37), channel_id=1, source_target_pairs={{0,64},{1,449},{32,96},{33,481},{64,128},{65,1},{96,160},{97,33},{... | collective-permute-start | bytes 497672 | tf_op jit(solution)/shard_map/ppermute | solution.py:191
  130.3 2.8 %collective-permute-start.12 = (bf16[144,576]{1,0:T(8,128)(2,1)}, bf16[144,576]{1,0:T(8,128)(2,1)S(1)}, u32[]{:S(2)}, u32[]{:S(2)}) collective-permute-start(bf16[144,576]{1,0:T(8,128)(2,1)} %get-tuple-element.39), channel_id=1, source_target_pairs={{0,96},{1,481},{32,64},{33,449},{64,160},{65,33},{96,128},{97,1},{... | collective-permute-start | bytes 497672 | tf_op jit(solution)/shard_map/ppermute | solution.py:191
  133.2 0.7 copy-done.11
  133.8 5.0 %all-to-all-start.1 = ((f32[4,8,2304]{2,1,0:T(8,128)}), f32[4,8,2304]{2,1,0:T(8,128)S(1)}, u32[]{:S(2)}, u32[]{:S(2)}) async-start(f32[4,8,2304]{2,1,0:T(8,128)} %bitcast.36), calls=%async_computation.2 | async-start | bytes 589824 | tf_op jit(solution)/shard_map/all_to_all | solution.py:277
  138.8 2.8 %collective-permute-done.12 = bf16[144,576]{1,0:T(8,128)(2,1)S(1)} collective-permute-done((bf16[144,576]{1,0:T(8,128)(2,1)}, bf16[144,576]{1,0:T(8,128)(2,1)S(1)}, u32[]{:S(2)}, u32[]{:S(2)}) %collective-permute-start.12) | collective-permute-done | bytes 165920 | tf_op jit(solution)/shard_map/ppermute | solution.py:191
  141.6 1.1 fusion.10
  143.1 0.6 copy-done.4
  143.9 1.2 fusion.6
  145.2 1.2 fusion.3
  146.4 0.6 reduce_sum.9
  (51 shorter events, 2.1 us)
Async XLA Ops:
  7.2 64.0 %all-gather.2.cloned.1.call-start = ((), (), s32[]{:S(2)}) async-start(), calls=%async_computation.3 | async-start | bytes 3317760 | tf_op jit(solution)/shard_map/all_gather | solution.py:203
  8.6 10.8 %copy-start.12 = (bf16[8,2304]{1,0:T(8,128)(2,1)S(1)}, bf16[8,2304]{1,0:T(8,128)(2,1)}, u32[]{:S(2)}) copy-start(bf16[8,2304]{1,0:T(8,128)(2,1)} %param.11) | copy-start | bytes 110596
  8.6 9.8 %collective-permute-start.2 = (bf16[144,576]{1,0:T(8,128)(2,1)S(1)}, bf16[144,576]{1,0:T(8,128)(2,1)S(1)}, u32[]{:S(2)}, u32[]{:S(2)}) collective-permute-start(bf16[144,576]{1,0:T(8,128)(2,1)S(1)} %broadcast_select_fusion.4), channel_id=1, source_target_pairs={{0,32},{32,0},{1,33},{33,1},{2,34},{34,2},{3,35},{35,3},{4,36},{36... | collective-permute-start | bytes 497672 | tf_op jit(solution)/shard_map/ppermute | solution.py:47
  20.5 11.1 %copy-start.10 = (bf16[256,576]{0,1:T(8,128)(2,1)S(1)}, bf16[256,576]{0,1:T(8,128)(2,1)}, u32[]{:S(2)}) copy-start(bf16[256,576]{0,1:T(8,128)(2,1)} %param.12) | copy-start | bytes 884740
  20.5 11.3 %copy-start.14 = (s32[256]{0:T(256)S(1)}, s32[256]{0:T(256)}, u32[]{:S(2)}) copy-start(s32[256]{0:T(256)} %param.13) | copy-start | bytes 3076
  20.5 11.3 %copy-start.13 = (s32[576]{0:T(1024)S(1)}, s32[576]{0:T(1024)}, u32[]{:S(2)}) copy-start(s32[576]{0:T(1024)} %param.14) | copy-start | bytes 6916
  20.5 40.4 %all-to-all-start = ((bf16[32,8,2304]{2,1,0:T(8,128)(2,1)}), bf16[32,8,2304]{2,1,0:T(8,128)(2,1)S(1)}, u32[]{:S(2)}, u32[]{:S(2)}) async-start(bf16[32,8,2304]{2,1,0:T(8,128)(2,1)} %broadcast_in_dim.4), calls=%async_computation | async-start | bytes 2359296 | tf_op jit(solution)/shard_map/all_to_all | solution.py:208
  30.9 103.0 %reduce-scatter.2.cloned.1.call-start = ((), (), s32[]{:S(2)}) async-start(), calls=%async_computation.4 | async-start | bytes 2654208 | tf_op jit(solution)/shard_map/reduce_scatter | solution.py:264
  32.3 12.2 %collective-permute-start = (bf16[256,288]{1,0:T(8,128)(2,1)S(1)}, bf16[256,288]{1,0:T(8,128)(2,1)S(1)}, u32[]{:S(2)}, u32[]{:S(2)}) collective-permute-start(bf16[256,288]{1,0:T(8,128)(2,1)S(1)} %broadcast_select_fusion), channel_id=1, source_target_pairs={{0,32},{32,0},{1,33},{33,1},{2,34},{34,2},{3,35},{35,3},{4,36},{36... | collective-permute-start | bytes 442376 | tf_op jit(solution)/shard_map/ppermute | solution.py:47
  60.9 4.9 %collective-permute-start.1 = (bf16[256,2304]{1,0:T(8,128)(2,1)S(1)}, bf16[256,2304]{1,0:T(8,128)(2,1)}, u32[]{:S(2)}, u32[]{:S(2)}) collective-permute-start(bf16[256,2304]{1,0:T(8,128)(2,1)S(1)} %bitcast.30), channel_id=1, source_target_pairs={{0,1},{1,0},{2,3},{3,2},{4,5},{5,4},{6,7},{7,6},{8,9},{9,8},{10,11... | collective-permute-start | bytes 3538952 | tf_op jit(solution)/shard_map/ppermute | solution.py:47
  71.2 1.8 %copy-start = (bf16[2304,576]{1,0:T(8,128)(2,1)S(1)}, bf16[2304,576]{1,0:T(8,128)(2,1)}, u32[]{:S(2)}) copy-start(bf16[2304,576]{1,0:T(8,128)(2,1)} %all-gather.2.cloned.1.call-done.weights) | copy-start | bytes 7962628
  75.8 0.7 copy-start.3
  76.6 1.1 copy-start.1
  77.7 4.7 %collective-permute-start.3 = (bf16[256,2304]{1,0:T(8,128)(2,1)S(1)}, bf16[256,2304]{1,0:T(8,128)(2,1)S(1)}, u32[]{:S(2)}, u32[]{:S(2)}) collective-permute-start(bf16[256,2304]{1,0:T(8,128)(2,1)S(1)} %inputs.3), channel_id=1, source_target_pairs={{0,1},{1,0},{2,3},{3,2},{4,5},{5,4},{6,7},{7,6},{8,9},{9,8},{10,11... | collective-permute-start | bytes 3538952 | tf_op jit(solution)/shard_map/ppermute | solution.py:47
  84.1 3.3 %copy-start.2 = (bf16[288,576]{1,0:T(8,128)(2,1)S(1)}, bf16[288,576]{1,0:T(8,128)(2,1)}, u32[]{:S(2)}) copy-start(bf16[288,576]{1,0:T(8,128)(2,1)} %copy-done.1) | copy-start | bytes 995332
  84.1 13.1 %collective-permute-start.4 = (bf16[288,576]{1,0:T(8,128)(2,1)}, bf16[288,576]{1,0:T(8,128)(2,1)S(1)}, u32[]{:S(2)}, u32[]{:S(2)}) collective-permute-start(bf16[288,576]{1,0:T(8,128)(2,1)} %copy-done.3), channel_id=1, source_target_pairs={{0,64},{1,449},{32,96},{33,481},{64,128},{65,1},{96,160},{97,33},{... | collective-permute-start | bytes 995336 | tf_op jit(solution)/shard_map/ppermute | solution.py:191
  87.4 12.4 %collective-permute-start.5 = (bf16[288,576]{1,0:T(8,128)(2,1)S(1)}, bf16[288,576]{1,0:T(8,128)(2,1)S(1)}, u32[]{:S(2)}, u32[]{:S(2)}) collective-permute-start(bf16[288,576]{1,0:T(8,128)(2,1)S(1)} %copy-done.2), channel_id=1, source_target_pairs={{0,448},{1,65},{32,480},{33,97},{64,0},{65,129},{96,32},{97,161},{... | collective-permute-start | bytes 995336 | tf_op jit(solution)/shard_map/ppermute | solution.py:191
  100.2 11.1 %collective-permute-start.9 = (bf16[288,576]{1,0:T(8,128)(2,1)S(1)}, bf16[288,576]{1,0:T(8,128)(2,1)S(1)}, u32[]{:S(2)}, u32[]{:S(2)}) collective-permute-start(bf16[288,576]{1,0:T(8,128)(2,1)S(1)} %hop.7), channel_id=1, source_target_pairs={{0,64},{1,449},{32,96},{33,481},{64,128},{65,1},{96,160},{97,33},{... | collective-permute-start | bytes 995336 | tf_op jit(solution)/shard_map/ppermute | solution.py:191
  102.8 13.2 %collective-permute-start.6 = (bf16[432,576]{1,0:T(8,128)(2,1)S(1)}, bf16[432,576]{1,0:T(8,128)(2,1)S(1)}, u32[]{:S(2)}, u32[]{:S(2)}) collective-permute-start(bf16[432,576]{1,0:T(8,128)(2,1)S(1)} %get-tuple-element.31), channel_id=1, source_target_pairs={{0,448},{1,65},{32,480},{33,97},{64,0},{65,129},{96,32},{97,161},{... | collective-permute-start | bytes 1493000 | tf_op jit(solution)/shard_map/ppermute | solution.py:191
  111.7 15.1 %collective-permute-start.10 = (bf16[288,576]{1,0:T(8,128)(2,1)S(1)}, bf16[288,576]{1,0:T(8,128)(2,1)S(1)}, u32[]{:S(2)}, u32[]{:S(2)}) collective-permute-start(bf16[288,576]{1,0:T(8,128)(2,1)S(1)} %hop.8), channel_id=1, source_target_pairs={{0,64},{1,449},{32,96},{33,481},{64,128},{65,1},{96,160},{97,33},{... | collective-permute-start | bytes 995336 | tf_op jit(solution)/shard_map/ppermute | solution.py:191
  116.5 16.6 %collective-permute-start.7 = (bf16[144,576]{1,0:T(8,128)(2,1)S(1)}, bf16[144,576]{1,0:T(8,128)(2,1)S(1)}, u32[]{:S(2)}, u32[]{:S(2)}) collective-permute-start(bf16[144,576]{1,0:T(8,128)(2,1)S(1)} %get-tuple-element.32), channel_id=1, source_target_pairs={{0,448},{1,65},{32,480},{33,97},{64,0},{65,129},{96,32},{97,161},{... | collective-permute-start | bytes 497672 | tf_op jit(solution)/shard_map/ppermute | solution.py:191
  121.7 12.1 %collective-permute-start.8 = (bf16[144,576]{1,0:T(8,128)(2,1)S(1)}, bf16[144,576]{1,0:T(8,128)(2,1)}, u32[]{:S(2)}, u32[]{:S(2)}) collective-permute-start(bf16[144,576]{1,0:T(8,128)(2,1)S(1)} %get-tuple-element.33), channel_id=1, source_target_pairs={{0,480},{1,97},{32,448},{33,65},{64,32},{65,161},{96,0},{97,129},{... | collective-permute-start | bytes 497672 | tf_op jit(solution)/shard_map/ppermute | solution.py:191
  128.0 10.9 %collective-permute-start.11 = (bf16[144,576]{1,0:T(8,128)(2,1)}, bf16[144,576]{1,0:T(8,128)(2,1)S(1)}, u32[]{:S(2)}, u32[]{:S(2)}) collective-permute-start(bf16[144,576]{1,0:T(8,128)(2,1)} %get-tuple-element.37), channel_id=1, source_target_pairs={{0,64},{1,449},{32,96},{33,481},{64,128},{65,1},{96,160},{97,33},{... | collective-permute-start | bytes 497672 | tf_op jit(solution)/shard_map/ppermute | solution.py:191
  130.3 11.3 %collective-permute-start.12 = (bf16[144,576]{1,0:T(8,128)(2,1)}, bf16[144,576]{1,0:T(8,128)(2,1)S(1)}, u32[]{:S(2)}, u32[]{:S(2)}) collective-permute-start(bf16[144,576]{1,0:T(8,128)(2,1)} %get-tuple-element.39), channel_id=1, source_target_pairs={{0,96},{1,481},{32,64},{33,449},{64,160},{65,33},{96,128},{97,1},{... | collective-permute-start | bytes 497672 | tf_op jit(solution)/shard_map/ppermute | solution.py:191
  133.1 0.7 copy-start.11
  133.8 12.5 %all-to-all-start.1 = ((f32[4,8,2304]{2,1,0:T(8,128)}), f32[4,8,2304]{2,1,0:T(8,128)S(1)}, u32[]{:S(2)}, u32[]{:S(2)}) async-start(f32[4,8,2304]{2,1,0:T(8,128)} %bitcast.36), calls=%async_computation.2 | async-start | bytes 589824 | tf_op jit(solution)/shard_map/all_to_all | solution.py:277
  142.7 0.9 copy-start.4
  142.8 1.1 copy-start.6
  142.8 1.2 copy-start.7
  143.0 2.1 %copy-start.5 = (bf16[144,576]{1,0:T(8,128)(2,1)S(1)}, bf16[144,576]{1,0:T(8,128)(2,1)}, u32[]{:S(2)}) copy-start(bf16[144,576]{1,0:T(8,128)(2,1)} %param.16) | copy-start | bytes 497668
  143.0 2.1 %copy-start.8 = (f32[144,576]{1,0:T(8,128)S(1)}, f32[144,576]{1,0:T(8,128)}, u32[]{:S(2)}) copy-start(f32[144,576]{1,0:T(8,128)} %param.18) | copy-start | bytes 995332
  143.1 2.1 %copy-start.9 = (f32[144,576]{1,0:T(8,128)S(1)}, f32[144,576]{1,0:T(8,128)}, u32[]{:S(2)}) copy-start(f32[144,576]{1,0:T(8,128)} %param.19) | copy-start | bytes 995332
Sparse Core Ops, SparseCore 0:
  19.5 51.6 all-gather.1
  84.2 43.5 reduce-scatter.1

commit v6 on v5

--- a/solution.py
+++ b/solution.py
@@ -82,9 +82,7 @@
     turned[...] = rows[...].T
 
 
-def forward_kernel(
-    depth, place_ref, turned, turned_other, weights, kept, dboth, forth, back
-):
+def forward_kernel(place_ref, turned, turned_other, weights, kept, dboth):
     half = kept.shape[1]
     tokens = turned.shape[1]
     both = [
@@ -104,10 +102,12 @@
         dropped = kept[span, :].astype(f32) * keep_scale
         dboth[span, :half] = (dropped * up * slope).astype(bf16)
         dboth[span, half:] = (dropped * act).astype(bf16)
+
+
+def begin_kernel(depth, place_ref, turned, turned_other, dboth, forth, back):
     far = depth // 2
     for out, step in ((forth, far), (back, 1 - far)):
-        term = block_product(place_ref, step, depth, turned, turned_other, dboth)
-        out[...] = term.astype(bf16)
+        out[...] = block_product(place_ref, step, depth, turned, turned_other, dboth).astype(bf16)
 
 
 def halves_of(place_ref, rows):
@@ -225,11 +225,12 @@
     turn = in_vmem(turn_kernel, [jax.ShapeDtypeStruct((model, tokens // 2), bf16)], "turn")
     turned = turn(place, core_rows)[0]
     turned_other = turn(place, swap(core_rows, "core"))[0]
-    dboth, forth, back = in_vmem(
-        functools.partial(forward_kernel, depth),
-        [jax.ShapeDtypeStruct(shape, bf16) for shape in ((tokens, own_units), block, block)],
-        "forward",
-    )(place, turned, turned_other, weights, kept)
+    dboth = in_vmem(
+        forward_kernel, [jax.ShapeDtypeStruct((tokens, own_units), bf16)], "forward"
+    )(place, turned, turned_other, weights, kept)[0]
+    forth, back = in_vmem(
+        functools.partial(begin_kernel, depth), [jax.ShapeDtypeStruct(block, bf16)] * 2, "begin"
+    )(place, turned, turned_other, dboth)
 
     rows_block, wide = (own_rows, own_units), pltpu.VMEM(block, f32)
 
@@ -260,7 +261,6 @@
     pair = back_product(0, f32) + other_part.astype(f32)
 
     forth, back = along(forth, 1), along(back, -1)
-    forth, back, dboth = lax.optimization_barrier((forth, back, dboth))
     columns = lax.psum_scatter(pair.reshape(across_y, -1, model), "y", scatter_dimension=0)
     forth = along(add_term(forth, far - 1), 1)
     message = (pair_rows + own_rows, own_units)

time: 155 us -> 154 us (level)
  the two profiles are of different devices: /device:TPU:2 before, /device:TPU:128 now
where the time goes in v6:
time: 154 us; the launch traced here: 153 us
  starting transfers between devices  63.3 us (41%)
  waiting for transfers between devices  50.2 us (33%)
  between operations  15.1 us (10%)
  Pallas kernels  10.3 us (7%)
  other arithmetic  7.75 us (5%)
  local copies, waits for them, and re-layouts  6.2 us (4%)
    ppermute x9, starting transfers between devices, ring(): return lax.ppermute(x, ('z', 'xh', 'core'), pairs)  35.8 us
    ppermute x4, waiting for transfers between devices, swap(): return lax.ppermute(x, axis, [(0, 1), (1, 0)])  16.3 us
    all_to_all x1, waiting for transfers between devices, on_device(): lax.all_to_all(spread, plane, split_axis=0, concat_axis=0)  15.6 us
    ppermute x9, waiting for transfers between devices, ring(): return lax.ppermute(x, ('z', 'xh', 'core'), pairs)  14.5 us
    ppermute x4, starting transfers between devices, swap(): return lax.ppermute(x, axis, [(0, 1), (1, 0)])  14 us
    pallas_call x11, Pallas kernels, call(): pl.pallas_call(kernel, out_shape=outs, in_specs=[pl.BlockSpec(memory_spac...  10.3 us
    all_to_all x1, starting transfers between devices, on_device(): lax.all_to_all(spread, plane, split_axis=0, concat_axis=0)  10.1 us
    unnamed x25, local copies, waits for them, and re-layouts  3.63 us
  transfers between devices with their start and end apart: 17, of which 10 were waited for; matrix products, arithmetic and copies ran while one was open for 4% of the time, Pallas kernels for 5%

profile of v6, /device:TPU:128, one launch (start us, length us, event | category | flops | bytes accessed | tf_op | source)
XLA Modules:
  0.0 152.9 jit_solution(1429000475408052086)
XLA Ops:
  7.2 1.2 fusion.17
  8.6 4.9 %collective-permute-start.2 = (bf16[144,576]{1,0:T(8,128)(2,1)S(1)}, bf16[144,576]{1,0:T(8,128)(2,1)S(1)}, u32[]{:S(2)}, u32[]{:S(2)}) collective-permute-start(bf16[144,576]{1,0:T(8,128)(2,1)S(1)} %broadcast_select_fusion.4), channel_id=1, source_target_pairs={{0,32},{32,0},{1,33},{33,1},{2,34},{34,2},{3,35},{35,3},{4,36},{36... | collective-permute-start | bytes 497672 | tf_op jit(solution)/shard_map/ppermute | solution.py:47
  13.5 4.8 %collective-permute-done.2 = bf16[144,576]{1,0:T(8,128)(2,1)S(1)} collective-permute-done((bf16[144,576]{1,0:T(8,128)(2,1)S(1)}, bf16[144,576]{1,0:T(8,128)(2,1)S(1)}, u32[]{:S(2)}, u32[]{:S(2)}) %collective-permute-start.2) | collective-permute-done | bytes 165920 | tf_op jit(solution)/shard_map/ppermute | solution.py:47
  18.5 0.8 pad_maximum_fusion.2
  19.3 1.1 broadcast_in_dim.4
  20.5 10.1 %all-to-all-start = ((bf16[32,8,2304]{2,1,0:T(8,128)(2,1)}), bf16[32,8,2304]{2,1,0:T(8,128)(2,1)S(1)}, u32[]{:S(2)}, u32[]{:S(2)}) async-start(bf16[32,8,2304]{2,1,0:T(8,128)(2,1)} %broadcast_in_dim.4), calls=%async_computation | async-start | bytes 2359296 | tf_op jit(solution)/shard_map/all_to_all | solution.py:208
  31.5 0.4 fusion
  32.0 5.2 %collective-permute-start = (bf16[256,288]{1,0:T(8,128)(2,1)S(1)}, bf16[256,288]{1,0:T(8,128)(2,1)S(1)}, u32[]{:S(2)}, u32[]{:S(2)}) collective-permute-start(bf16[256,288]{1,0:T(8,128)(2,1)S(1)} %broadcast_select_fusion), channel_id=1, source_target_pairs={{0,32},{32,0},{1,33},{33,1},{2,34},{34,2},{3,35},{35,3},{4,36},{36... | collective-permute-start | bytes 442376 | tf_op jit(solution)/shard_map/ppermute | solution.py:47
  37.2 7.2 %collective-permute-done = bf16[256,288]{1,0:T(8,128)(2,1)S(1)} collective-permute-done((bf16[256,288]{1,0:T(8,128)(2,1)S(1)}, bf16[256,288]{1,0:T(8,128)(2,1)S(1)}, u32[]{:S(2)}, u32[]{:S(2)}) %collective-permute-start) | collective-permute-done | bytes 147488 | tf_op jit(solution)/shard_map/ppermute | solution.py:47
  44.9 15.6 %all-to-all-done = bf16[32,8,2304]{2,1,0:T(8,128)(2,1)S(1)} async-done(((bf16[32,8,2304]{2,1,0:T(8,128)(2,1)}), bf16[32,8,2304]{2,1,0:T(8,128)(2,1)S(1)}, u32[]{:S(2)}, u32[]{:S(2)}) %all-to-all-start) | async-done | bytes 1179680 | tf_op jit(solution)/shard_map/all_to_all | solution.py:208
  60.5 1.9 %collective-permute-start.1 = (bf16[256,2304]{1,0:T(8,128)(2,1)S(1)}, bf16[256,2304]{1,0:T(8,128)(2,1)}, u32[]{:S(2)}, u32[]{:S(2)}) collective-permute-start(bf16[256,2304]{1,0:T(8,128)(2,1)S(1)} %bitcast.30), channel_id=1, source_target_pairs={{0,1},{1,0},{2,3},{3,2},{4,5},{5,4},{6,7},{7,6},{8,9},{9,8},{10,11... | collective-permute-start | bytes 3538952 | tf_op jit(solution)/shard_map/ppermute | solution.py:47
  62.4 0.4 turn.2.turned
  62.8 2.6 %collective-permute-done.1.rows = bf16[256,2304]{1,0:T(8,128)(2,1)} collective-permute-done((bf16[256,2304]{1,0:T(8,128)(2,1)S(1)}, bf16[256,2304]{1,0:T(8,128)(2,1)}, u32[]{:S(2)}, u32[]{:S(2)}) %collective-permute-start.1) | collective-permute-done | bytes 1179680 | tf_op jit(solution)/shard_map/ppermute | solution.py:47
  65.3 1.6 %turn.3.turned_other = bf16[2304,256]{1,0:T(8,128)(2,1)S(1)} custom-call(s32[1]{0:T(128)} %bitcast.place_ref, bf16[256,2304]{1,0:T(8,128)(2,1)} %collective-permute-done.1.rows), custom_call_target="tpu_custom_call" | custom-call | tf_op jit(solution)/shard_map/turn/pallas_call | solution.py:56
  67.0 1.7 %all-gather.2.cloned.1.call-done.weights = bf16[2304,576]{1,0:T(8,128)(2,1)} async-done(((bf16[288,576]{1,0:T(8,128)(2,1)}), bf16[2304,576]{1,0:T(8,128)(2,1)}) %all-gather.2.cloned.1.call-update) | async-done | bytes 2654224 | tf_op jit(solution)/shard_map/all_gather | solution.py:203
  68.7 1.8 %copy-done = bf16[2304,576]{1,0:T(8,128)(2,1)S(1)} copy-done((bf16[2304,576]{1,0:T(8,128)(2,1)S(1)}, bf16[2304,576]{1,0:T(8,128)(2,1)}, u32[]{:S(2)}) %copy-start) | copy-done | bytes 2654232
  70.6 2.2 %forward.1.dboth = bf16[512,576]{1,0:T(8,128)(2,1)S(1)} custom-call(s32[1]{0:T(128)} %bitcast.place_ref, bf16[2304,256]{1,0:T(8,128)(2,1)S(1)} %turn.2.turned, bf16[2304,256]{1,0:T(8,128)(2,1)S(1)} %turn.3.turned_other, bf16[2304,576]{1,0:T(8,128)(2,1)S(1)} %copy-done, bf16[512,288]{1,0:T(8,128)(2,1)S(1)} %bitcast.32), custom_call_target="tpu_custom_call" | custom-call | tf_op jit(solution)/shard_map/forward/pallas_call | solution.py:56
  72.8 1.1 inputs.3
  73.9 1.9 %collective-permute-start.3 = (bf16[256,2304]{1,0:T(8,128)(2,1)S(1)}, bf16[256,2304]{1,0:T(8,128)(2,1)S(1)}, u32[]{:S(2)}, u32[]{:S(2)}) collective-permute-start(bf16[256,2304]{1,0:T(8,128)(2,1)S(1)} %inputs.3), channel_id=1, source_target_pairs={{0,1},{1,0},{2,3},{3,2},{4,5},{5,4},{6,7},{7,6},{8,9},{9,8},{10,11... | collective-permute-start | bytes 3538952 | tf_op jit(solution)/shard_map/ppermute | solution.py:47
  75.8 1.1 inputs.2
  77.0 1.7 %collective-permute-done.3 = bf16[256,2304]{1,0:T(8,128)(2,1)S(1)} collective-permute-done((bf16[256,2304]{1,0:T(8,128)(2,1)S(1)}, bf16[256,2304]{1,0:T(8,128)(2,1)S(1)}, u32[]{:S(2)}, u32[]{:S(2)}) %collective-permute-start.3) | collective-permute-done | bytes 1179680 | tf_op jit(solution)/shard_map/ppermute | solution.py:47
  78.6 1.6 %convert_add_fusion = f32[256,2304]{1,0:T(8,128)} fusion(f32[256,2304]{1,0:T(8,128)S(1)} %inputs.2, bf16[256,2304]{1,0:T(8,128)(2,1)S(1)} %collective-permute-done.3), kind=kLoop, calls=%fused_computation | loop fusion | flops 1179648 | bytes 5898240 | tf_op jit(solution)/shard_map/add | solution.py:261
  80.3 0.6 begin.1
  80.9 3.3 %collective-permute-start.8 = (bf16[288,576]{1,0:T(8,128)(2,1)S(1)}, bf16[288,576]{1,0:T(8,128)(2,1)S(1)}, u32[]{:S(2)}, u32[]{:S(2)}) collective-permute-start(bf16[288,576]{1,0:T(8,128)(2,1)S(1)} %get-tuple-element.28), channel_id=1, source_target_pairs={{0,64},{1,449},{32,96},{33,481},{64,128},{65,1},{96,160},{97,33},{... | collective-permute-start | bytes 995336 | tf_op jit(solution)/shard_map/ppermute | solution.py:191
  84.2 2.5 %collective-permute-start.4 = (bf16[288,576]{1,0:T(8,128)(2,1)S(1)}, bf16[288,576]{1,0:T(8,128)(2,1)S(1)}, u32[]{:S(2)}, u32[]{:S(2)}) collective-permute-start(bf16[288,576]{1,0:T(8,128)(2,1)S(1)} %get-tuple-element.22), channel_id=1, source_target_pairs={{0,448},{1,65},{32,480},{33,97},{64,0},{65,129},{96,32},{97,161},{... | collective-permute-start | bytes 995336 | tf_op jit(solution)/shard_map/ppermute | solution.py:191
  86.8 5.7 %collective-permute-done.8.arrived = bf16[288,576]{1,0:T(8,128)(2,1)S(1)} collective-permute-done((bf16[288,576]{1,0:T(8,128)(2,1)S(1)}, bf16[288,576]{1,0:T(8,128)(2,1)S(1)}, u32[]{:S(2)}, u32[]{:S(2)}) %collective-permute-start.8) | collective-permute-done | bytes 331808 | tf_op jit(solution)/shard_map/ppermute | solution.py:191
  92.5 0.4 hop.7
  92.9 4.2 %collective-permute-start.9 = (bf16[288,576]{1,0:T(8,128)(2,1)S(1)}, bf16[288,576]{1,0:T(8,128)(2,1)S(1)}, u32[]{:S(2)}, u32[]{:S(2)}) collective-permute-start(bf16[288,576]{1,0:T(8,128)(2,1)S(1)} %hop.7), channel_id=1, source_target_pairs={{0,64},{1,449},{32,96},{33,481},{64,128},{65,1},{96,160},{97,33},{... | collective-permute-start | bytes 995336 | tf_op jit(solution)/shard_map/ppermute | solution.py:191
  97.1 0.7 hop.5
  97.9 1.9 %collective-permute-start.5 = (bf16[432,576]{1,0:T(8,128)(2,1)S(1)}, bf16[432,576]{1,0:T(8,128)(2,1)S(1)}, u32[]{:S(2)}, u32[]{:S(2)}) collective-permute-start(bf16[432,576]{1,0:T(8,128)(2,1)S(1)} %get-tuple-element.23), channel_id=1, source_target_pairs={{0,448},{1,65},{32,480},{33,97},{64,0},{65,129},{96,32},{97,161},{... | collective-permute-start | bytes 1493000 | tf_op jit(solution)/shard_map/ppermute | solution.py:191
  99.8 5.6 %collective-permute-done.9.arrived = bf16[288,576]{1,0:T(8,128)(2,1)S(1)} collective-permute-done((bf16[288,576]{1,0:T(8,128)(2,1)S(1)}, bf16[288,576]{1,0:T(8,128)(2,1)S(1)}, u32[]{:S(2)}, u32[]{:S(2)}) %collective-permute-start.9) | collective-permute-done | bytes 331808 | tf_op jit(solution)/shard_map/ppermute | solution.py:191
  105.4 0.4 hop.8
  105.8 5.9 %collective-permute-start.10 = (bf16[288,576]{1,0:T(8,128)(2,1)S(1)}, bf16[288,576]{1,0:T(8,128)(2,1)S(1)}, u32[]{:S(2)}, u32[]{:S(2)}) collective-permute-start(bf16[288,576]{1,0:T(8,128)(2,1)S(1)} %hop.8), channel_id=1, source_target_pairs={{0,64},{1,449},{32,96},{33,481},{64,128},{65,1},{96,160},{97,33},{... | collective-permute-start | bytes 995336 | tf_op jit(solution)/shard_map/ppermute | solution.py:191
  111.8 3.1 %collective-permute-done.5.arrived.refs_0_ = bf16[432,576]{1,0:T(8,128)(2,1)S(1)} collective-permute-done((bf16[432,576]{1,0:T(8,128)(2,1)S(1)}, bf16[432,576]{1,0:T(8,128)(2,1)S(1)}, u32[]{:S(2)}, u32[]{:S(2)}) %collective-permute-start.5) | collective-permute-done | bytes 497696 | tf_op jit(solution)/shard_map/ppermute | solution.py:191
  114.9 0.5 hop.6
  115.4 1.9 %collective-permute-start.6 = (bf16[144,576]{1,0:T(8,128)(2,1)S(1)}, bf16[144,576]{1,0:T(8,128)(2,1)S(1)}, u32[]{:S(2)}, u32[]{:S(2)}) collective-permute-start(bf16[144,576]{1,0:T(8,128)(2,1)S(1)} %get-tuple-element.24), channel_id=1, source_target_pairs={{0,448},{1,65},{32,480},{33,97},{64,0},{65,129},{96,32},{97,161},{... | collective-permute-start | bytes 497672 | tf_op jit(solution)/shard_map/ppermute | solution.py:191
  117.3 2.3 %collective-permute-start.7 = (bf16[144,576]{1,0:T(8,128)(2,1)S(1)}, bf16[144,576]{1,0:T(8,128)(2,1)}, u32[]{:S(2)}, u32[]{:S(2)}) collective-permute-start(bf16[144,576]{1,0:T(8,128)(2,1)S(1)} %get-tuple-element.25), channel_id=1, source_target_pairs={{0,480},{1,97},{32,448},{33,65},{64,32},{65,161},{96,0},{97,129},{... | collective-permute-start | bytes 497672 | tf_op jit(solution)/shard_map/ppermute | solution.py:191
  119.6 1.3 hop.9
  120.9 6.4 %collective-permute-start.11 = (bf16[144,576]{1,0:T(8,128)(2,1)}, bf16[144,576]{1,0:T(8,128)(2,1)S(1)}, u32[]{:S(2)}, u32[]{:S(2)}) collective-permute-start(bf16[144,576]{1,0:T(8,128)(2,1)} %get-tuple-element.29), channel_id=1, source_target_pairs={{0,64},{1,449},{32,96},{33,481},{64,128},{65,1},{96,160},{97,33},{... | collective-permute-start | bytes 497672 | tf_op jit(solution)/shard_map/ppermute | solution.py:191
  127.3 7.2 %collective-permute-start.12 = (bf16[144,576]{1,0:T(8,128)(2,1)}, bf16[144,576]{1,0:T(8,128)(2,1)S(1)}, u32[]{:S(2)}, u32[]{:S(2)}) collective-permute-start(bf16[144,576]{1,0:T(8,128)(2,1)} %get-tuple-element.31), channel_id=1, source_target_pairs={{0,96},{1,481},{32,64},{33,449},{64,160},{65,33},{96,128},{97,1},{... | collective-permute-start | bytes 497672 | tf_op jit(solution)/shard_map/ppermute | solution.py:191
  134.5 0.7 copy-done.8
  135.2 3.5 %all-to-all-start.1 = ((f32[4,8,2304]{2,1,0:T(8,128)}), f32[4,8,2304]{2,1,0:T(8,128)S(1)}, u32[]{:S(2)}, u32[]{:S(2)}) async-start(f32[4,8,2304]{2,1,0:T(8,128)} %bitcast.36), calls=%async_computation.2 | async-start | bytes 589824 | tf_op jit(solution)/shard_map/all_to_all | solution.py:277
  138.7 1.1 fusion.10
  140.1 0.6 copy-done.1
  141.0 1.2 fusion.6
  142.2 1.2 fusion.3
  143.4 2.0 %all-to-all-done.1 = f32[4,8,2304]{2,1,0:T(8,128)S(1)} async-done(((f32[4,8,2304]{2,1,0:T(8,128)}), f32[4,8,2304]{2,1,0:T(8,128)S(1)}, u32[]{:S(2)}, u32[]{:S(2)}) %all-to-all-start.1) | async-done | bytes 294944 | tf_op jit(solution)/shard_map/all_to_all | solution.py:277
  145.5 0.6 reduce_sum.9
  (46 shorter events, 1.7 us)
Async XLA Ops:
  7.2 61.6 %all-gather.2.cloned.1.call-start = ((), (), s32[]{:S(2)}) async-start(), calls=%async_computation.3 | async-start | bytes 3317760 | tf_op jit(solution)/shard_map/all_gather | solution.py:203
  8.6 10.8 %copy-start.9 = (bf16[8,2304]{1,0:T(8,128)(2,1)S(1)}, bf16[8,2304]{1,0:T(8,128)(2,1)}, u32[]{:S(2)}) copy-start(bf16[8,2304]{1,0:T(8,128)(2,1)} %param.11) | copy-start | bytes 110596
  8.6 9.8 %collective-permute-start.2 = (bf16[144,576]{1,0:T(8,128)(2,1)S(1)}, bf16[144,576]{1,0:T(8,128)(2,1)S(1)}, u32[]{:S(2)}, u32[]{:S(2)}) collective-permute-start(bf16[144,576]{1,0:T(8,128)(2,1)S(1)} %broadcast_select_fusion.4), channel_id=1, source_target_pairs={{0,32},{32,0},{1,33},{33,1},{2,34},{34,2},{3,35},{35,3},{4,36},{36... | collective-permute-start | bytes 497672 | tf_op jit(solution)/shard_map/ppermute | solution.py:47
  20.5 10.8 %copy-start.7 = (bf16[256,576]{0,1:T(8,128)(2,1)S(1)}, bf16[256,576]{0,1:T(8,128)(2,1)}, u32[]{:S(2)}) copy-start(bf16[256,576]{0,1:T(8,128)(2,1)} %param.12) | copy-start | bytes 884740
  20.5 11.0 %copy-start.11 = (s32[256]{0:T(256)S(1)}, s32[256]{0:T(256)}, u32[]{:S(2)}) copy-start(s32[256]{0:T(256)} %param.13) | copy-start | bytes 3076
  20.5 11.0 %copy-start.10 = (s32[576]{0:T(1024)S(1)}, s32[576]{0:T(1024)}, u32[]{:S(2)}) copy-start(s32[576]{0:T(1024)} %param.14) | copy-start | bytes 6916
  20.5 40.0 %all-to-all-start = ((bf16[32,8,2304]{2,1,0:T(8,128)(2,1)}), bf16[32,8,2304]{2,1,0:T(8,128)(2,1)S(1)}, u32[]{:S(2)}, u32[]{:S(2)}) async-start(bf16[32,8,2304]{2,1,0:T(8,128)(2,1)} %broadcast_in_dim.4), calls=%async_computation | async-start | bytes 2359296 | tf_op jit(solution)/shard_map/all_to_all | solution.py:208
  30.5 104.6 %reduce-scatter.2.cloned.1.call-start = ((), (), s32[]{:S(2)}) async-start(), calls=%async_computation.4 | async-start | bytes 2654208 | tf_op jit(solution)/shard_map/reduce_scatter | solution.py:264
  32.0 12.4 %collective-permute-start = (bf16[256,288]{1,0:T(8,128)(2,1)S(1)}, bf16[256,288]{1,0:T(8,128)(2,1)S(1)}, u32[]{:S(2)}, u32[]{:S(2)}) collective-permute-start(bf16[256,288]{1,0:T(8,128)(2,1)S(1)} %broadcast_select_fusion), channel_id=1, source_target_pairs={{0,32},{32,0},{1,33},{33,1},{2,34},{34,2},{3,35},{35,3},{4,36},{36... | collective-permute-start | bytes 442376 | tf_op jit(solution)/shard_map/ppermute | solution.py:47
  60.5 4.9 %collective-permute-start.1 = (bf16[256,2304]{1,0:T(8,128)(2,1)S(1)}, bf16[256,2304]{1,0:T(8,128)(2,1)}, u32[]{:S(2)}, u32[]{:S(2)}) collective-permute-start(bf16[256,2304]{1,0:T(8,128)(2,1)S(1)} %bitcast.30), channel_id=1, source_target_pairs={{0,1},{1,0},{2,3},{3,2},{4,5},{5,4},{6,7},{7,6},{8,9},{9,8},{10,11... | collective-permute-start | bytes 3538952 | tf_op jit(solution)/shard_map/ppermute | solution.py:47
  68.7 1.8 %copy-start = (bf16[2304,576]{1,0:T(8,128)(2,1)S(1)}, bf16[2304,576]{1,0:T(8,128)(2,1)}, u32[]{:S(2)}) copy-start(bf16[2304,576]{1,0:T(8,128)(2,1)} %all-gather.2.cloned.1.call-done.weights) | copy-start | bytes 7962628
  73.9 4.7 %collective-permute-start.3 = (bf16[256,2304]{1,0:T(8,128)(2,1)S(1)}, bf16[256,2304]{1,0:T(8,128)(2,1)S(1)}, u32[]{:S(2)}, u32[]{:S(2)}) collective-permute-start(bf16[256,2304]{1,0:T(8,128)(2,1)S(1)} %inputs.3), channel_id=1, source_target_pairs={{0,1},{1,0},{2,3},{3,2},{4,5},{5,4},{6,7},{7,6},{8,9},{9,8},{10,11... | collective-permute-start | bytes 3538952 | tf_op jit(solution)/shard_map/ppermute | solution.py:47
  80.9 11.6 %collective-permute-start.8 = (bf16[288,576]{1,0:T(8,128)(2,1)S(1)}, bf16[288,576]{1,0:T(8,128)(2,1)S(1)}, u32[]{:S(2)}, u32[]{:S(2)}) collective-permute-start(bf16[288,576]{1,0:T(8,128)(2,1)S(1)} %get-tuple-element.28), channel_id=1, source_target_pairs={{0,64},{1,449},{32,96},{33,481},{64,128},{65,1},{96,160},{97,33},{... | collective-permute-start | bytes 995336 | tf_op jit(solution)/shard_map/ppermute | solution.py:191
  84.2 12.9 %collective-permute-start.4 = (bf16[288,576]{1,0:T(8,128)(2,1)S(1)}, bf16[288,576]{1,0:T(8,128)(2,1)S(1)}, u32[]{:S(2)}, u32[]{:S(2)}) collective-permute-start(bf16[288,576]{1,0:T(8,128)(2,1)S(1)} %get-tuple-element.22), channel_id=1, source_target_pairs={{0,448},{1,65},{32,480},{33,97},{64,0},{65,129},{96,32},{97,161},{... | collective-permute-start | bytes 995336 | tf_op jit(solution)/shard_map/ppermute | solution.py:191
  92.9 12.5 %collective-permute-start.9 = (bf16[288,576]{1,0:T(8,128)(2,1)S(1)}, bf16[288,576]{1,0:T(8,128)(2,1)S(1)}, u32[]{:S(2)}, u32[]{:S(2)}) collective-permute-start(bf16[288,576]{1,0:T(8,128)(2,1)S(1)} %hop.7), channel_id=1, source_target_pairs={{0,64},{1,449},{32,96},{33,481},{64,128},{65,1},{96,160},{97,33},{... | collective-permute-start | bytes 995336 | tf_op jit(solution)/shard_map/ppermute | solution.py:191
  97.9 17.0 %collective-permute-start.5 = (bf16[432,576]{1,0:T(8,128)(2,1)S(1)}, bf16[432,576]{1,0:T(8,128)(2,1)S(1)}, u32[]{:S(2)}, u32[]{:S(2)}) collective-permute-start(bf16[432,576]{1,0:T(8,128)(2,1)S(1)} %get-tuple-element.23), channel_id=1, source_target_pairs={{0,448},{1,65},{32,480},{33,97},{64,0},{65,129},{96,32},{97,161},{... | collective-permute-start | bytes 1493000 | tf_op jit(solution)/shard_map/ppermute | solution.py:191
  105.8 13.8 %collective-permute-start.10 = (bf16[288,576]{1,0:T(8,128)(2,1)S(1)}, bf16[288,576]{1,0:T(8,128)(2,1)S(1)}, u32[]{:S(2)}, u32[]{:S(2)}) collective-permute-start(bf16[288,576]{1,0:T(8,128)(2,1)S(1)} %hop.8), channel_id=1, source_target_pairs={{0,64},{1,449},{32,96},{33,481},{64,128},{65,1},{96,160},{97,33},{... | collective-permute-start | bytes 995336 | tf_op jit(solution)/shard_map/ppermute | solution.py:191
  115.4 19.1 %collective-permute-start.6 = (bf16[144,576]{1,0:T(8,128)(2,1)S(1)}, bf16[144,576]{1,0:T(8,128)(2,1)S(1)}, u32[]{:S(2)}, u32[]{:S(2)}) collective-permute-start(bf16[144,576]{1,0:T(8,128)(2,1)S(1)} %get-tuple-element.24), channel_id=1, source_target_pairs={{0,448},{1,65},{32,480},{33,97},{64,0},{65,129},{96,32},{97,161},{... | collective-permute-start | bytes 497672 | tf_op jit(solution)/shard_map/ppermute | solution.py:191
  117.3 17.9 %collective-permute-start.7 = (bf16[144,576]{1,0:T(8,128)(2,1)S(1)}, bf16[144,576]{1,0:T(8,128)(2,1)}, u32[]{:S(2)}, u32[]{:S(2)}) collective-permute-start(bf16[144,576]{1,0:T(8,128)(2,1)S(1)} %get-tuple-element.25), channel_id=1, source_target_pairs={{0,480},{1,97},{32,448},{33,65},{64,32},{65,161},{96,0},{97,129},{... | collective-permute-start | bytes 497672 | tf_op jit(solution)/shard_map/ppermute | solution.py:191
  120.9 17.8 %collective-permute-start.11 = (bf16[144,576]{1,0:T(8,128)(2,1)}, bf16[144,576]{1,0:T(8,128)(2,1)S(1)}, u32[]{:S(2)}, u32[]{:S(2)}) collective-permute-start(bf16[144,576]{1,0:T(8,128)(2,1)} %get-tuple-element.29), channel_id=1, source_target_pairs={{0,64},{1,449},{32,96},{33,481},{64,128},{65,1},{96,160},{97,33},{... | collective-permute-start | bytes 497672 | tf_op jit(solution)/shard_map/ppermute | solution.py:191
  127.3 11.4 %collective-permute-start.12 = (bf16[144,576]{1,0:T(8,128)(2,1)}, bf16[144,576]{1,0:T(8,128)(2,1)S(1)}, u32[]{:S(2)}, u32[]{:S(2)}) collective-permute-start(bf16[144,576]{1,0:T(8,128)(2,1)} %get-tuple-element.31), channel_id=1, source_target_pairs={{0,96},{1,481},{32,64},{33,449},{64,160},{65,33},{96,128},{97,1},{... | collective-permute-start | bytes 497672 | tf_op jit(solution)/shard_map/ppermute | solution.py:191
  134.5 0.7 copy-start.8
  135.2 10.3 %all-to-all-start.1 = ((f32[4,8,2304]{2,1,0:T(8,128)}), f32[4,8,2304]{2,1,0:T(8,128)S(1)}, u32[]{:S(2)}, u32[]{:S(2)}) async-start(f32[4,8,2304]{2,1,0:T(8,128)} %bitcast.36), calls=%async_computation.2 | async-start | bytes 589824 | tf_op jit(solution)/shard_map/all_to_all | solution.py:277
  139.8 0.9 copy-start.1
  139.8 1.1 copy-start.3
  139.8 1.2 copy-start.4
  140.1 2.1 %copy-start.2 = (bf16[144,576]{1,0:T(8,128)(2,1)S(1)}, bf16[144,576]{1,0:T(8,128)(2,1)}, u32[]{:S(2)}) copy-start(bf16[144,576]{1,0:T(8,128)(2,1)} %param.16) | copy-start | bytes 497668
  140.1 2.1 %copy-start.5 = (f32[144,576]{1,0:T(8,128)S(1)}, f32[144,576]{1,0:T(8,128)}, u32[]{:S(2)}) copy-start(f32[144,576]{1,0:T(8,128)} %param.18) | copy-start | bytes 995332
  140.1 2.1 %copy-start.6 = (f32[144,576]{1,0:T(8,128)S(1)}, f32[144,576]{1,0:T(8,128)}, u32[]{:S(2)}) copy-start(f32[144,576]{1,0:T(8,128)} %param.19) | copy-start | bytes 995332
Sparse Core Ops, SparseCore 0:
  19.5 49.2 all-gather.1
  80.4 44.4 reduce-scatter.1
